TPU v7x, 256 devices: a whole 4x4x8 slice. The times are simulated.
256 devices in a mesh: lat: 16 (over z, x_hi), lon: 16 (over y, x_lo, core).
Axes of the slice: x: 4 (x_hi: 2, x_lo: 2; x = x_hi * 2 + x_lo), y: 4, z: 8, core: 2. Of those that a mesh axis runs over, the one named last changes fastest.
Arguments:
- fields: bfloat16 [4, 96, 192, 384], P(None, 'lat', 'lon'), may hold values from -6 to 6
- cotangent: bfloat16 [4, 96, 192, 384], P(None, 'lat', 'lon'), may hold values from -6 to 6
- window_mask: int32 [2, 16, 16], P(None, 'lat', 'lon'), may hold values 0 or 1
- mask_token: bfloat16 [384], replicated, may hold values from -4 to 4
- norm_gain: bfloat16 [384], replicated, may hold values from 0.5 to 1.5
- qkv_weight: bfloat16 [1152, 384], replicated, may hold values from -0.3125 to 0.3125
- out_weight: bfloat16 [384, 384], replicated, may hold values from -0.3125 to 0.3125
- bias_table: float32 [16, 12, 759], P('lat'), may hold values from -300 to 300
- bias_index: int32 [144, 144], replicated, may hold values from 0 to 758
Outputs:
- output: bfloat16 [4, 96, 192, 384], P(None, 'lat', 'lon')
- input_grad: bfloat16 [4, 96, 192, 384], P(None, 'lat', 'lon')
- weight_grads: float32 [1536, 384], P(('lat', 'lon'))
- table_grad: float32 [16, 12, 759], P('lat')
- vector_grads: float32 [2, 384], replicated
All inputs are finite; a program needn't handle non-finite values. No bound on the sum of `window_mask` on one device may be relied on, other than what follows from the above.
Results may differ from a plain program's by a relative error of at most 0.02.
Values may be sent and summed in bfloat16 or wider, within the bound.
No kernel may reach another device: no remote copies, remote signals or barrier semaphores. Data moves between devices by JAX's collectives and lax.ppermute only.
A program may use at most 64 MiB of HBM per device.

v0:
```python
import jax
import jax.numpy as jnp
from jax import lax
from jax.sharding import PartitionSpec as P

HEADS = 12
HEAD_DIM = 32
WIN_Z = 2
WIN_LAT = 6
WIN_LON = 12
WIN_TOK = 144
NBIAS = 759


EPS = 1e-05
BLOCKED = -10000.0
QUERY_BLOCK = 16


def passed_along(value, axis, steps):
    count = lax.axis_size(axis)
    pairs = [(source, (source + steps) % count) for source in range(count)]
    return lax.ppermute(value, axis, pairs)


def expand_mask(window_mask):
    spread = jnp.repeat(window_mask, WIN_Z, axis=0)
    spread = jnp.repeat(spread, WIN_LAT, axis=1)
    return jnp.repeat(spread, WIN_LON, axis=2)


def region_of(coords, extent, window):
    return (coords >= extent - window).astype(jnp.int32) + (coords >= extent - window // 2).astype(
        jnp.int32
    )


def to_windows(value):
    level_count, row_count, col_count, chan_count = value.shape
    value = value.reshape(
        level_count // WIN_Z,
        WIN_Z,
        row_count // WIN_LAT,
        WIN_LAT,
        col_count // WIN_LON,
        WIN_LON,
        chan_count,
    )
    value = value.transpose(2, 0, 4, 1, 3, 5, 6)
    return value.reshape(
        row_count // WIN_LAT, level_count // WIN_Z * (col_count // WIN_LON), WIN_TOK, chan_count
    )


def from_windows(value, level_count, col_count):
    row_groups = value.shape[0]
    chan_count = value.shape[3]
    value = value.reshape(
        row_groups, level_count // WIN_Z, col_count // WIN_LON, WIN_Z, WIN_LAT, WIN_LON, chan_count
    )
    value = value.transpose(1, 3, 0, 4, 2, 5, 6)
    return value.reshape(level_count, row_groups * WIN_LAT, col_count, chan_count)


def one_hot_block(ids):
    entries = jnp.arange(NBIAS, dtype=jnp.int32)
    return (ids[:, None] == entries[None, :]).astype(jnp.float32)


def index_blocks(bias_index):
    return bias_index.reshape(WIN_TOK // QUERY_BLOCK, QUERY_BLOCK * WIN_TOK)


def lookup_bias(bias_table, bias_index):
    row_groups = bias_table.shape[0]
    flat_table = bias_table.reshape(row_groups * HEADS, NBIAS)

    def pick(ids):
        return jnp.einsum(
            "rb,nb->rn", flat_table, one_hot_block(ids), precision=lax.Precision.HIGHEST
        )

    picked = lax.map(pick, index_blocks(bias_index))
    picked = picked.transpose(1, 0, 2)
    return picked.reshape(row_groups, HEADS, WIN_TOK, WIN_TOK)


def table_sums(bias_grad, bias_index):
    row_groups = bias_grad.shape[0]
    block_count = WIN_TOK // QUERY_BLOCK
    flat_grad = bias_grad.reshape(row_groups * HEADS, block_count, QUERY_BLOCK * WIN_TOK).transpose(
        1, 0, 2
    )

    def accumulate(total, items):
        grad_block, ids = items
        return (
            total
            + jnp.einsum(
                "rn,nb->rb", grad_block, one_hot_block(ids), precision=lax.Precision.HIGHEST
            ),
            None,
        )

    start = jnp.zeros((row_groups * HEADS, NBIAS), jnp.float32)
    total, _ = lax.scan(accumulate, start, (flat_grad, index_blocks(bias_index)))
    return total.reshape(row_groups, HEADS, NBIAS)


def roll_in(first, second):
    lat_shift = WIN_LAT // 2
    lon_shift = WIN_LON // 2
    first = jnp.roll(first, -(WIN_Z // 2), axis=0)
    second = jnp.roll(second, -(WIN_Z // 2), axis=0)
    strip = passed_along(jnp.stack((first[:, :lat_shift], second[:, :lat_shift])), "lat", -1)
    first = jnp.concatenate((first[:, lat_shift:], strip[0]), axis=1)
    second = jnp.concatenate((second[:, lat_shift:], strip[1]), axis=1)
    strip = passed_along(jnp.stack((first[:, :, :lon_shift], second[:, :, :lon_shift])), "lon", -1)
    first = jnp.concatenate((first[:, :, lon_shift:], strip[0]), axis=2)
    second = jnp.concatenate((second[:, :, lon_shift:], strip[1]), axis=2)
    return (first, second)


def roll_out_one(value):
    lat_shift = WIN_LAT // 2
    lon_shift = WIN_LON // 2
    strip = passed_along(value[:, -lat_shift:], "lat", 1)
    value = jnp.concatenate((strip, value[:, :-lat_shift]), axis=1)
    strip = passed_along(value[:, :, -lon_shift:], "lon", 1)
    value = jnp.concatenate((strip, value[:, :, :-lon_shift]), axis=2)
    return jnp.roll(value, WIN_Z // 2, axis=0)


def window_block(tokens_win, cot_win, bias, regions, qkv_weight, out_weight):
    wide = jnp.float32
    low = jnp.bfloat16
    groups = tokens_win.shape[0]
    members = tokens_win.shape[1]
    scale = HEAD_DIM ** (-0.5)
    projected = jnp.einsum(
        "rmtd,fd->rmtf", tokens_win, qkv_weight, preferred_element_type=wide
    ).astype(low)
    projected = projected.reshape(groups, members, WIN_TOK, 3, HEADS, HEAD_DIM)
    queries = projected[:, :, :, 0]
    key_rows = projected[:, :, :, 1]
    values = projected[:, :, :, 2]
    scores = (
        jnp.einsum("rmthe,rmshe->rmhts", queries, key_rows, preferred_element_type=wide) * scale
        + bias[:, None]
    )
    apart = regions[:, :, :, None] != regions[:, :, None, :]
    scores = jnp.where(apart[:, :, None], BLOCKED, scores)
    row_max = jnp.max(scores, axis=-1, keepdims=True)
    exponent = jnp.exp(scores - row_max)
    attn_prob = (exponent / jnp.sum(exponent, axis=-1, keepdims=True)).astype(low)
    mixed_heads = jnp.einsum(
        "rmhts,rmshe->rmthe", attn_prob, values, preferred_element_type=wide
    ).astype(low)
    mixed_heads = mixed_heads.reshape(groups, members, WIN_TOK, HEADS * HEAD_DIM)
    branch = jnp.einsum(
        "rmtd,fd->rmtf", mixed_heads, out_weight, preferred_element_type=wide
    ).astype(low)
    out_grad = jnp.einsum("rmtf,rmtd->fd", cot_win, mixed_heads, preferred_element_type=wide)
    grad_mixed = jnp.einsum(
        "rmtf,fd->rmtd", cot_win, out_weight, preferred_element_type=wide
    ).astype(low)
    grad_mixed = grad_mixed.reshape(groups, members, WIN_TOK, HEADS, HEAD_DIM)
    grad_attn = jnp.einsum("rmthe,rmshe->rmhts", grad_mixed, values, preferred_element_type=wide)
    grad_values = jnp.einsum(
        "rmhts,rmthe->rmshe", attn_prob, grad_mixed, preferred_element_type=wide
    ).astype(low)
    prob_float = attn_prob.astype(wide)
    grad_scores = prob_float * (grad_attn - jnp.sum(prob_float * grad_attn, axis=-1, keepdims=True))
    bias_grad = jnp.sum(grad_scores, axis=1)
    scores_low = grad_scores.astype(low)
    grad_queries = (
        jnp.einsum("rmhts,rmshe->rmthe", scores_low, key_rows, preferred_element_type=wide) * scale
    ).astype(low)
    grad_keys = (
        jnp.einsum("rmhts,rmthe->rmshe", scores_low, queries, preferred_element_type=wide) * scale
    ).astype(low)
    grad_qkv = jnp.stack((grad_queries, grad_keys, grad_values), axis=3).reshape(
        groups, members, WIN_TOK, 3 * HEADS * HEAD_DIM
    )
    qkv_grad = jnp.einsum("rmtf,rmtd->fd", grad_qkv, tokens_win, preferred_element_type=wide)
    grad_tokens = jnp.einsum(
        "rmtf,fd->rmtd", grad_qkv, qkv_weight, preferred_element_type=wide
    ).astype(low)
    return (branch, grad_tokens, qkv_grad, out_grad, bias_grad)


def local(
    fields,
    cotangent,
    window_mask,
    mask_token,
    norm_gain,
    qkv_weight,
    out_weight,
    bias_table,
    bias_index,
):
    wide = jnp.float32
    level_count, row_count, col_count, chan_count = fields.shape
    masked = expand_mask(window_mask) == 1
    filled = jnp.where(masked[..., None], mask_token, fields)
    filled_wide = filled.astype(wide)
    center = filled_wide - jnp.mean(filled_wide, axis=-1, keepdims=True)
    inv_std = lax.rsqrt(jnp.mean(center * center, axis=-1, keepdims=True) + EPS)
    standard = center * inv_std
    normed = (standard * norm_gain.astype(wide)).astype(jnp.bfloat16)
    shifted, shifted_cot = roll_in(normed, cotangent)
    lat_coords = lax.axis_index("lat") * row_count + jnp.arange(row_count, dtype=jnp.int32)
    level_ids = region_of(jnp.arange(level_count, dtype=jnp.int32), level_count, WIN_Z)
    lat_ids = region_of(lat_coords, row_count * lax.axis_size("lat"), WIN_LAT)
    regions = level_ids[:, None] * 3 + lat_ids[None, :]
    region_field = jnp.broadcast_to(
        regions[:, :, None, None], (level_count, row_count, col_count, 1)
    )
    region_win = to_windows(region_field)[..., 0]
    bias = lookup_bias(bias_table, bias_index)
    branch_win, grad_win, qkv_grad, out_grad, bias_grad = window_block(
        to_windows(shifted), to_windows(shifted_cot), bias, region_win, qkv_weight, out_weight
    )
    branch_local = from_windows(branch_win, level_count, col_count)
    grad_local = from_windows(grad_win, level_count, col_count)
    branch = roll_out_one(branch_local)
    grad_normed = roll_out_one(grad_local)
    output = (filled_wide + branch.astype(wide)).astype(jnp.bfloat16)
    scaled = grad_normed.astype(wide) * norm_gain.astype(wide)
    grad_filled = cotangent.astype(wide) + inv_std * (
        scaled
        - jnp.mean(scaled, axis=-1, keepdims=True)
        - standard * jnp.mean(scaled * standard, axis=-1, keepdims=True)
    )
    input_grad = jnp.where(masked[..., None], 0.0, grad_filled).astype(jnp.bfloat16)
    gain_grad = jnp.sum(grad_normed.astype(wide) * standard, axis=(0, 1, 2))
    token_grad = jnp.sum(jnp.where(masked[..., None], grad_filled, 0.0), axis=(0, 1, 2))
    vector_grads = lax.psum(jnp.stack((gain_grad, token_grad)), ("lat", "lon"))
    table_local = table_sums(bias_grad, bias_index)
    table_grad = lax.psum(table_local.astype(jnp.bfloat16), "lon").astype(jnp.float32)
    grad_terms = jnp.concatenate((qkv_grad, out_grad), axis=0)
    weight_grads = lax.psum_scatter(grad_terms, ("lat", "lon"), scatter_dimension=0, tiled=True)
    return (output, input_grad, weight_grads, table_grad, vector_grads)


def solution(mesh):
    placed = (
        P(None, "lat", "lon", None),
        P(None, "lat", "lon", None),
        P(None, "lat", "lon"),
        P(),
        P(),
        P(),
        P(),
        P("lat", None, None),
        P(),
    )
    return jax.shard_map(
        local,
        mesh=mesh,
        in_specs=placed,
        out_specs=(
            P(None, "lat", "lon", None),
            P(None, "lat", "lon", None),
            P(("lat", "lon"), None),
            P("lat", None, None),
            P(),
        ),
        check_vma=False,
    )
```

profile of v0, /device:TPU:2, one launch (start us, length us, event | category | flops | bytes accessed | tf_op | source)
XLA Modules:
  0.0 372.7 jit_solution(7033225869644779675)
XLA Ops:
  8.9 1.1 convert_reduce_fusion
  10.0 1.2 fusion.34
  11.3 1.1 fusion.30
  13.7 7.4 %collective-permute-start = (bf16[2,4,3,12,384]{4,3,2,1,0:T(8,128)(2,1)}, bf16[2,4,3,12,384]{4,3,2,1,0:T(8,128)(2,1)}, u32[]{:S(2)}, u32[]{:S(2)}) collective-permute-start(bf16[2,4,3,12,384]{4,3,2,1,0:T(8,128)(2,1)} %pad_maximum_fusion.11), channel_id=1, source_target_pairs={{0,240},{16,0},{32,16},{48,32},{64,48},{80,64},{96,80},{112,96},{1... | collective-permute-start | bytes 663560 | tf_op jit(solution)/shard_map/ppermute | solution.py:23
  21.3 38.2 %while.21 = (s32[]{:T(128)}, f32[9,12,2304]{2,1,0:T(8,128)}, s32[9,2304]{1,0:T(8,128)S(1)}, f32[12,759]{1,0:T(8,128)S(1)}, s32[]{:T(128)}) while((s32[]{:T(128)}, f32[9,12,2304]{2,1,0:T(8,128)}, s32[9,2304]{1,0:T(8,128)S(1)}, f32[12,759]{1,0:T(8,128)S(1)}, s32[]{:T(128)}) %tuple.71), condition=%wide.region_3.4_spmd, body=%wide.region_2.3_spmd.sunk | while | flops 253566720 | bytes 211613 | solution.py:83
  21.3 4.2 %fusion.84 = f32[9,12,2304]{2,1,0:T(8,128)} fusion(f32[9,12,2304]{2,1,0:T(8,128)} %get-tuple-element.186, s32[]{:T(128)S(6)} %copy.121, f32[12,759]{1,0:T(8,128)S(1)} %get-tuple-element.193, s32[2304]{0:T(1024)S(1)} %dynamic-slice_reduce_fusion.4), kind=kOutput, calls=%fused_computation.4.clone.1 | convolution fusion | flops 253566720 | bytes 193108 | tf_op jit(solution)/shard_map/while/body/eval_jaxpr/rb,nb->rn/dot_general | solution.py:79
  25.6 4.2 %fusion.84 = f32[9,12,2304]{2,1,0:T(8,128)} fusion(f32[9,12,2304]{2,1,0:T(8,128)} %get-tuple-element.186, s32[]{:T(128)S(6)} %copy.121, f32[12,759]{1,0:T(8,128)S(1)} %get-tuple-element.193, s32[2304]{0:T(1024)S(1)} %dynamic-slice_reduce_fusion.4), kind=kOutput, calls=%fused_computation.4.clone.1 | convolution fusion | flops 253566720 | bytes 193108 | tf_op jit(solution)/shard_map/while/body/eval_jaxpr/rb,nb->rn/dot_general | solution.py:79
  29.8 4.2 %fusion.84 = f32[9,12,2304]{2,1,0:T(8,128)} fusion(f32[9,12,2304]{2,1,0:T(8,128)} %get-tuple-element.186, s32[]{:T(128)S(6)} %copy.121, f32[12,759]{1,0:T(8,128)S(1)} %get-tuple-element.193, s32[2304]{0:T(1024)S(1)} %dynamic-slice_reduce_fusion.4), kind=kOutput, calls=%fused_computation.4.clone.1 | convolution fusion | flops 253566720 | bytes 193108 | tf_op jit(solution)/shard_map/while/body/eval_jaxpr/rb,nb->rn/dot_general | solution.py:79
  34.0 4.2 %fusion.84 = f32[9,12,2304]{2,1,0:T(8,128)} fusion(f32[9,12,2304]{2,1,0:T(8,128)} %get-tuple-element.186, s32[]{:T(128)S(6)} %copy.121, f32[12,759]{1,0:T(8,128)S(1)} %get-tuple-element.193, s32[2304]{0:T(1024)S(1)} %dynamic-slice_reduce_fusion.4), kind=kOutput, calls=%fused_computation.4.clone.1 | convolution fusion | flops 253566720 | bytes 193108 | tf_op jit(solution)/shard_map/while/body/eval_jaxpr/rb,nb->rn/dot_general | solution.py:79
  38.3 4.2 %fusion.84 = f32[9,12,2304]{2,1,0:T(8,128)} fusion(f32[9,12,2304]{2,1,0:T(8,128)} %get-tuple-element.186, s32[]{:T(128)S(6)} %copy.121, f32[12,759]{1,0:T(8,128)S(1)} %get-tuple-element.193, s32[2304]{0:T(1024)S(1)} %dynamic-slice_reduce_fusion.4), kind=kOutput, calls=%fused_computation.4.clone.1 | convolution fusion | flops 253566720 | bytes 193108 | tf_op jit(solution)/shard_map/while/body/eval_jaxpr/rb,nb->rn/dot_general | solution.py:79
  42.5 4.2 %fusion.84 = f32[9,12,2304]{2,1,0:T(8,128)} fusion(f32[9,12,2304]{2,1,0:T(8,128)} %get-tuple-element.186, s32[]{:T(128)S(6)} %copy.121, f32[12,759]{1,0:T(8,128)S(1)} %get-tuple-element.193, s32[2304]{0:T(1024)S(1)} %dynamic-slice_reduce_fusion.4), kind=kOutput, calls=%fused_computation.4.clone.1 | convolution fusion | flops 253566720 | bytes 193108 | tf_op jit(solution)/shard_map/while/body/eval_jaxpr/rb,nb->rn/dot_general | solution.py:79
  46.8 4.2 %fusion.84 = f32[9,12,2304]{2,1,0:T(8,128)} fusion(f32[9,12,2304]{2,1,0:T(8,128)} %get-tuple-element.186, s32[]{:T(128)S(6)} %copy.121, f32[12,759]{1,0:T(8,128)S(1)} %get-tuple-element.193, s32[2304]{0:T(1024)S(1)} %dynamic-slice_reduce_fusion.4), kind=kOutput, calls=%fused_computation.4.clone.1 | convolution fusion | flops 253566720 | bytes 193108 | tf_op jit(solution)/shard_map/while/body/eval_jaxpr/rb,nb->rn/dot_general | solution.py:79
  51.0 4.2 %fusion.84 = f32[9,12,2304]{2,1,0:T(8,128)} fusion(f32[9,12,2304]{2,1,0:T(8,128)} %get-tuple-element.186, s32[]{:T(128)S(6)} %copy.121, f32[12,759]{1,0:T(8,128)S(1)} %get-tuple-element.193, s32[2304]{0:T(1024)S(1)} %dynamic-slice_reduce_fusion.4), kind=kOutput, calls=%fused_computation.4.clone.1 | convolution fusion | flops 253566720 | bytes 193108 | tf_op jit(solution)/shard_map/while/body/eval_jaxpr/rb,nb->rn/dot_general | solution.py:79
  55.2 4.2 %fusion.84 = f32[9,12,2304]{2,1,0:T(8,128)} fusion(f32[9,12,2304]{2,1,0:T(8,128)} %get-tuple-element.186, s32[]{:T(128)S(6)} %copy.121, f32[12,759]{1,0:T(8,128)S(1)} %get-tuple-element.193, s32[2304]{0:T(1024)S(1)} %dynamic-slice_reduce_fusion.4), kind=kOutput, calls=%fused_computation.4.clone.1 | convolution fusion | flops 253566720 | bytes 193108 | tf_op jit(solution)/shard_map/while/body/eval_jaxpr/rb,nb->rn/dot_general | solution.py:79
  59.5 2.0 copy.61
  61.5 2.5 add.93
  64.0 3.0 copy.62
  67.2 1.0 slice_bitcast_fusion.19
  69.5 4.1 %collective-permute-done.1 = bf16[2,4,6,6,384]{4,3,2,1,0:T(8,128)(2,1)S(1)} collective-permute-done((bf16[2,4,6,6,384]{4,3,2,1,0:T(8,128)(2,1)S(1)}, bf16[2,4,6,6,384]{4,3,2,1,0:T(8,128)(2,1)S(1)}, u32[]{:S(2)}, u32[]{:S(2)}) %collective-permute-start.1) | collective-permute-done | bytes 221216 | tf_op jit(solution)/shard_map/ppermute | solution.py:23
  75.7 4.7 %fusion.64 = (f32[2,12,144]{2,1,0:T(8,128)S(1)}, f32[2,12,144,144]{2,3,1,0:T(8,128)}) fusion(f32[12,144,144]{1,2,0:T(8,128)} %copy.62, pred[2,144,144]{1,2,0:T(8,128)(4,1)S(1)} %broadcast_compare_fusion, bf16[1,2,144,3,12,32]{2,5,4,3,1,0:T(8,128)(2,1)S(1)} %bitcast.123), kind=kOutput, calls=%fused_computation.140 | convolution fusion | flops 34338960 | bytes 3859968 | tf_op jit(solution)/shard_map/sub | solution.py:154
  80.4 2.8 fusion.8
  83.9 2.1 fusion.10
  88.0 1.1 convolution_convert_fusion.5
  89.9 1.3 convolution_convert_fusion.3
  91.9 1.7 reshape_transpose_reshape.9
  93.6 1.7 fusion.61
  95.4 1.7 reshape_transpose_reshape.8
  97.1 1.7 fusion.62
  98.8 1.5 pad_maximum_fusion
  100.3 2.1 copy.74
  102.4 2.5 reshape.254
  104.9 41.0 %while.22 = (s32[]{:T(128)}, f32[12,759]{1,0:T(8,128)S(1)}, f32[9,12,2304]{2,0,1:T(8,128)}, s32[9,2304]{1,0:T(8,128)}, s32[]{:T(128)}, /*index=5*/s32[]{:T(128)}) while((s32[]{:T(128)}, f32[12,759]{1,0:T(8,128)S(1)}, f32[9,12,2304]{2,0,1:T(8,128)}, s32[9,2304]{1,0:T(8,128)}, s32[]{:T(128)}, /*index=5*/s32[]{:T(128)}) %tuple.70), condition=%wide.region_12.13_spmd.clone, body=%wide.region_11.12_spmd.clone.sunk | while | flops 253584928 | bytes 432383 | solution.py:106
  104.9 1.0 dynamic-slice_reduce_fusion.5
  105.9 1.3 constant_dynamic-slice_fusion.3
  107.2 2.3 fusion.85
  110.5 1.3 constant_dynamic-slice_fusion.3
  111.7 2.3 fusion.85
  114.1 0.9 dynamic-slice_reduce_fusion.5
  115.0 1.3 constant_dynamic-slice_fusion.3
  116.3 2.3 fusion.85
  118.6 0.9 dynamic-slice_reduce_fusion.5
  119.5 1.3 constant_dynamic-slice_fusion.3
  120.8 2.3 fusion.85
  123.2 0.9 dynamic-slice_reduce_fusion.5
  124.1 1.3 constant_dynamic-slice_fusion.3
  125.4 2.3 fusion.85
  128.6 1.3 constant_dynamic-slice_fusion.3
  129.9 2.3 fusion.85
  132.3 0.9 dynamic-slice_reduce_fusion.5
  133.2 1.3 constant_dynamic-slice_fusion.3
  134.4 2.3 fusion.85
  137.7 1.3 constant_dynamic-slice_fusion.3
  139.0 2.3 fusion.85
  142.3 1.3 constant_dynamic-slice_fusion.3
  143.5 2.3 fusion.85
  145.9 55.6 %psum.14 = bf16[1,12,759]{2,0,1:T(2,128)(2,1)S(1)} all-reduce(bf16[1,12,759]{2,0,1:T(2,128)(2,1)S(1)} %convert_element_type.161), channel_id=1, replica_groups=mesh['lat'=16,'lon'=16] {'lon'}, use_global_device_ids=true, to_apply=%region_13.14 | all-reduce | flops 9108 | bytes 36432 | tf_op jit(solution)/shard_map/psum | solution.py:241
  202.2 1.0 fusion.47
  203.3 1.0 fusion.48
  204.4 3.5 collective-permute-done.5
  207.9 1.4 fusion.25
  209.5 1.5 fusion.36
  212.5 82.3 %psum.15 = f32[2,384]{1,0:T(2,128)} all-reduce(f32[2,384]{1,0:T(2,128)S(1)} %pad_maximum_fusion.17), channel_id=1, replica_groups=mesh['lat'=16,'lon'=16] {'lat','lon'}, use_global_device_ids=true, to_apply=%region_16.17 | all-reduce | flops 768 | bytes 6144 | tf_op jit(solution)/shard_map/psum | solution.py:239
  294.9 69.7 %all-reduce.3.cloned.1.call-done = f32[1536,384]{1,0:T(8,128)} async-done(((f32[1536,384]{1,0:T(8,128)}), f32[1536,384]{1,0:T(8,128)}) %all-reduce.3.cloned.1.call-update) | async-done | bytes 2359312
  364.5 1.3 constant_dynamic-slice_fusion.1
  (107 shorter events, 17.4 us)
Async XLA Ops:
  7.2 67.4 %copy-start = (bf16[1152,384]{1,0:T(8,128)(2,1)S(1)}, bf16[1152,384]{1,0:T(8,128)(2,1)}, u32[]{:S(2)}) copy-start(bf16[1152,384]{1,0:T(8,128)(2,1)} %param.18) | copy-start | bytes 2654212
  7.2 5.3 %copy-start.4 = (bf16[4,6,12,384]{3,0,2,1:T(4,128)(2,1)S(1)}, bf16[4,6,12,384]{3,0,2,1:T(4,128)(2,1)}, u32[]{:S(2)}) copy-start(bf16[4,6,12,384]{3,0,2,1:T(4,128)(2,1)} %param.14) | copy-start | bytes 663556
  7.2 357.3 %all-reduce.3.cloned.1.call-start = ((), (), s32[]{:S(2)}) async-start(), calls=%async_computation | async-start | bytes 4718592
  12.4 8.7 %copy-start.11 = (s32[144,144]{1,0:T(8,128)S(1)}, s32[144,144]{1,0:T(8,128)}, u32[]{:S(2)}) copy-start(s32[144,144]{1,0:T(8,128)} %param.21) | copy-start | bytes 248836
  12.5 8.8 %copy-start.12 = (f32[1,12,759]{2,0,1:T(1,128)S(1)}, f32[1,12,759]{2,0,1:T(1,128)}, u32[]{:S(2)}) copy-start(f32[1,12,759]{2,0,1:T(1,128)} %param.20) | copy-start | bytes 109300
  13.7 53.5 %collective-permute-start = (bf16[2,4,3,12,384]{4,3,2,1,0:T(8,128)(2,1)}, bf16[2,4,3,12,384]{4,3,2,1,0:T(8,128)(2,1)}, u32[]{:S(2)}, u32[]{:S(2)}) collective-permute-start(bf16[2,4,3,12,384]{4,3,2,1,0:T(8,128)(2,1)} %pad_maximum_fusion.11), channel_id=1, source_target_pairs={{0,240},{16,0},{32,16},{48,32},{64,48},{80,64},{96,80},{112,96},{1... | collective-permute-start | bytes 663560 | tf_op jit(solution)/shard_map/ppermute | solution.py:23
  59.5 4.5 %copy-start.10 = (s32[9,2304]{1,0:T(8,128)}, s32[9,2304]{1,0:T(8,128)S(1)}, u32[]{:S(2)}) copy-start(s32[9,2304]{1,0:T(8,128)S(1)} %get-tuple-element.216) | copy-start | bytes 248836
  68.3 5.5 %copy-start.8 = (bf16[384,384]{1,0:T(8,128)(2,1)S(1)}, bf16[384,384]{1,0:T(8,128)(2,1)}, u32[]{:S(2)}) copy-start(bf16[384,384]{1,0:T(8,128)(2,1)} %param.19) | copy-start | bytes 884740
  68.5 5.1 %collective-permute-start.1 = (bf16[2,4,6,6,384]{4,3,2,1,0:T(8,128)(2,1)S(1)}, bf16[2,4,6,6,384]{4,3,2,1,0:T(8,128)(2,1)S(1)}, u32[]{:S(2)}, u32[]{:S(2)}) collective-permute-start(bf16[2,4,6,6,384]{4,3,2,1,0:T(8,128)(2,1)S(1)} %pad_maximum_fusion.12), channel_id=1, source_target_pairs={{0,15},{1,0},{2,1},{3,2},{4,3},{5,4},{6,5},{7,6},{8,7},{9,8},{10,9... | collective-permute-start | bytes 663560 | tf_op jit(solution)/shard_map/ppermute | solution.py:23
  73.8 0.7 copy-start.2
  87.0 1.0 copy-start.9
  87.0 2.0 copy-start.3
  95.4 106.9 %collective-permute-start.4 = (bf16[4,3,12,384]{3,2,1,0:T(8,128)(2,1)}, bf16[4,3,12,384]{3,2,1,0:T(8,128)(2,1)}, u32[]{:S(2)}, u32[]{:S(2)}) collective-permute-start(bf16[4,3,12,384]{3,2,1,0:T(8,128)(2,1)} %get-tuple-element.110), channel_id=1, source_target_pairs={{0,16},{16,32},{32,48},{48,64},{64,80},{80,96},{96,112},{112,128},... | collective-permute-start | bytes 331784 | tf_op jit(solution)/shard_map/ppermute | solution.py:23
  98.8 104.6 %collective-permute-start.2 = (bf16[4,3,12,384]{3,2,1,0:T(8,128)(2,1)}, bf16[4,3,12,384]{3,2,1,0:T(8,128)(2,1)}, u32[]{:S(2)}, u32[]{:S(2)}) collective-permute-start(bf16[4,3,12,384]{3,2,1,0:T(8,128)(2,1)} %get-tuple-element.113), channel_id=1, source_target_pairs={{0,16},{16,32},{32,48},{48,64},{64,80},{80,96},{96,112},{112,128},... | collective-permute-start | bytes 331784 | tf_op jit(solution)/shard_map/ppermute | solution.py:23
  104.9 97.3 %copy-start.7 = (bf16[4,3,12,384]{3,2,1,0:T(8,128)(2,1)S(1)}, bf16[4,3,12,384]{3,2,1,0:T(8,128)(2,1)}, u32[]{:S(2)}) copy-start(bf16[4,3,12,384]{3,2,1,0:T(8,128)(2,1)} %get-tuple-element.111) | copy-start | bytes 331780
  104.9 98.4 %copy-start.6 = (bf16[4,3,12,384]{3,2,1,0:T(8,128)(2,1)S(1)}, bf16[4,3,12,384]{3,2,1,0:T(8,128)(2,1)}, u32[]{:S(2)}) copy-start(bf16[4,3,12,384]{3,2,1,0:T(8,128)(2,1)} %get-tuple-element.112) | copy-start | bytes 331780
  104.9 103.0 %copy-start.1 = (bf16[4,6,12,384]{3,0,2,1:T(4,128)(2,1)S(1)}, bf16[4,6,12,384]{3,0,2,1:T(4,128)(2,1)}, u32[]{:S(2)}) copy-start(bf16[4,6,12,384]{3,0,2,1:T(4,128)(2,1)} %param.13) | copy-start | bytes 663556
  104.9 103.0 %copy-start.13 = (bf16[384]{0:T(512)(128)(2,1)S(1)}, bf16[384]{0:T(512)(128)(2,1)}, u32[]{:S(2)}) copy-start(bf16[384]{0:T(512)(128)(2,1)} %param.16) | copy-start | bytes 2308
  145.9 63.6 %copy-start.5 = (bf16[4,6,12,384]{3,0,2,1:T(4,128)(2,1)S(1)}, bf16[4,6,12,384]{3,0,2,1:T(4,128)(2,1)}, u32[]{:S(2)}) copy-start(bf16[4,6,12,384]{3,0,2,1:T(4,128)(2,1)} %param.14) | copy-start | bytes 663556
  203.2 4.6 %collective-permute-start.5 = (bf16[4,6,6,384]{3,2,1,0:T(8,128)(2,1)S(1)}, bf16[4,6,6,384]{3,2,1,0:T(8,128)(2,1)S(1)}, u32[]{:S(2)}, u32[]{:S(2)}) collective-permute-start(bf16[4,6,6,384]{3,2,1,0:T(8,128)(2,1)S(1)} %fusion.47), channel_id=1, source_target_pairs={{0,1},{1,2},{2,3},{3,4},{4,5},{5,6},{6,7},{7,8},{8,9},{9,10},{10,1... | collective-permute-start | bytes 331784 | tf_op jit(solution)/shard_map/ppermute | solution.py:23
  204.3 5.1 %collective-permute-start.3 = (bf16[4,6,6,384]{3,2,1,0:T(8,128)(2,1)S(1)}, bf16[4,6,6,384]{3,2,1,0:T(8,128)(2,1)S(1)}, u32[]{:S(2)}, u32[]{:S(2)}) collective-permute-start(bf16[4,6,6,384]{3,2,1,0:T(8,128)(2,1)S(1)} %fusion.48), channel_id=1, source_target_pairs={{0,1},{1,2},{2,3},{3,4},{4,5},{5,6},{6,7},{7,8},{8,9},{9,10},{10,1... | collective-permute-start | bytes 331784 | tf_op jit(solution)/shard_map/ppermute | solution.py:23
Sparse Core Ops, SparseCore 0:
  100.5 264.0 all-reduce.2
where the time goes:
time: 374 us; the launch traced here: 373 us
  blocking collectives  138 us (37%)
  waiting for transfers between devices  77.4 us (21%)
  matrix products  73 us (20%)
  local copies, waits for them, and re-layouts  45.2 us (12%)
  other arithmetic  15.9 us (4%)
  between operations  14.5 us (4%)
  starting transfers between devices  8.48 us (2%)
    psum x1, blocking collectives, local(): vector_grads = lax.psum(jnp.stack((gain_grad, token_grad)), ('lat', 'lon'))  82.3 us
    unnamed x2, waiting for transfers between devices  69.7 us
    psum x1, blocking collectives, local(): lax.psum(table_local.astype(jnp.bfloat16), 'lon').astype(jnp.float32)  55.6 us
    dot_general x9, matrix products, pick(): jnp.einsum('rb,nb->rn', flat_table, one_hot_block(ids), precision=lax.Pre...  37.9 us
    dot_general x9, matrix products, accumulate(): jnp.einsum('rn,nb->rb', grad_block, one_hot_block(ids), precision=lax.Pre...  21.1 us
    dynamic_slice x9, local copies, waits for them, and re-layouts, table_sums(): lax.scan(accumulate, start, (flat_grad, index_blocks(bias_index)))  11.3 us
    dynamic_slice x18, local copies, waits for them, and re-layouts, lookup_bias(): picked = lax.map(pick, index_blocks(bias_index))  8.69 us
    ppermute x6, starting transfers between devices, passed_along(): return lax.ppermute(value, axis, pairs)  8.44 us
  transfers between devices with their start and end apart: 7, of which 4 were waited for; matrix products, arithmetic and copies ran while one was open for 28% of the time, Pallas kernels for 0%

commit v1 on v0

v1 whole, which is shorter than its diff:
```python
import functools

import jax
import jax.numpy as jnp
from jax import lax
from jax.experimental import pallas as pl
from jax.experimental.pallas import tpu as pltpu
from jax.sharding import PartitionSpec as P

HEADS = 12
HEAD_DIM = 32
WIN_TOK = 144
NBIAS = 759
D = 384
TOK = 288
EPS = 1e-05
BLOCKED = -10000.0
MARK = 256.0
LANES = 128
QSLOTS = 8
CHUNK = 128

wide = jnp.float32
low = jnp.bfloat16

NN = (((1,), (0,)), ((), ()))
NT = (((1,), (1,)), ((), ()))
TN = (((0,), (0,)), ((), ()))


def mm(a, b, dims):
    return lax.dot_general(a, b, dims, preferred_element_type=wide)


def passed_along(value, axis, steps):
    count = lax.axis_size(axis)
    pairs = [(source, (source + steps) % count) for source in range(count)]
    return lax.ppermute(value, axis, pairs)


def bias_kernel(table_ref, ids_ref, bias_ref):
    def rows(step, _):
        at = pl.ds(pl.multiple_of(step * 8, 8), 8)
        for half in range(2):
            cols = slice(half * LANES, (half + 1) * LANES)
            ids = ids_ref[at, cols]
            place = ids & (LANES - 1)
            piece = ids >> 7
            picks = [piece == p for p in range(6)]
            for head in range(HEADS):
                got = jnp.zeros((8, LANES), wide)
                for p in range(6):
                    source = jnp.broadcast_to(
                        table_ref[head : head + 1, p * LANES : (p + 1) * LANES], (8, LANES)
                    )
                    found = jnp.take_along_axis(source, place, axis=1)
                    got = jnp.where(picks[p], found, got)
                bias_ref[head, at, cols] = got
        return 0

    lax.fori_loop(0, WIN_TOK // 8, rows, 0)


def main_kernel(
    scal_ref,
    fields_ref,
    cot_ref,
    lat_ref,
    lon_ref,
    token_ref,
    gain_ref,
    wqkv_ref,
    wout_ref,
    bias_ref,
    ids_ref,
    out_own_ref,
    out_lat_ref,
    send_ref,
    x_ref,
    c_ref,
    std_ref,
    qkv_ref,
    gm_ref,
    qt_ref,
    gmt_ref,
    mixed_ref,
    gq_ref,
    gkt_ref,
    gvt_ref,
    bg_ref,
    fin_ref,
):
    for which, own, dest in ((0, fields_ref, x_ref), (1, cot_ref, c_ref)):
        for zs in range(4):
            z = (zs + 1) % 4
            for a in range(6):
                base = zs * 72 + a * 12
                if a < 3:
                    piece = own[z, 3 + a].astype(wide)[6:12]
                    if which == 0:
                        piece = jnp.where(scal_ref[z // 2] == 1, MARK, piece)
                else:
                    piece = lat_ref[which, z, a - 3].astype(wide)[6:12]
                dest[base : base + 6, :] = piece
                dest[base + 6 : base + 12, :] = lon_ref[which, z, a].astype(wide)
    raw = x_ref[...]
    masked = raw > 0.5 * MARK
    filled = jnp.where(masked, token_ref[...], raw)
    x_ref[...] = filled
    gain = gain_ref[...]
    center = filled - jnp.mean(filled, axis=-1, keepdims=True)
    inv_std = lax.rsqrt(jnp.mean(center * center, axis=-1, keepdims=True) + EPS)
    standard = center * inv_std
    std_ref[...] = standard
    normed = (standard * gain).astype(low)
    cot = c_ref[...].astype(low)

    qkv_ref[...] = mm(normed, wqkv_ref[...], NT).astype(low)
    gm_ref[...] = mm(cot, wout_ref[...], NN).astype(low)
    qt_ref[...] = mm(wqkv_ref[0:D, :], normed, NT).astype(low)
    gmt_ref[...] = mm(wout_ref[...], cot, (((0,), (1,)), ((), ()))).astype(low)

    last = scal_ref[2] == 1
    ti = lax.broadcasted_iota(jnp.int32, (WIN_TOK, WIN_TOK), 0)
    tj = lax.broadcasted_iota(jnp.int32, (WIN_TOK, WIN_TOK), 1)
    zi = (ti >= 72).astype(jnp.int32)
    zj = (tj >= 72).astype(jnp.int32)
    ai = (ti - 72 * zi >= 36).astype(jnp.int32)
    aj = (tj - 72 * zj >= 36).astype(jnp.int32)
    lat_apart = jnp.where(last, (ai != aj).astype(wide), 0.0)
    lev_apart = (zi != zj).astype(wide)
    apart = (lat_apart > 0.0, lat_apart + lev_apart > 0.0)
    lane = lax.broadcasted_iota(jnp.int32, (1, LANES), 1) // HEAD_DIM
    scale = HEAD_DIM ** (-0.5)
    for group in range(3):
        cols = slice(group * LANES, (group + 1) * LANES)
        for sub in range(4):
            head = group * 4 + sub
            mask = (lane == sub).astype(low)
            feats = slice(head * HEAD_DIM, (head + 1) * HEAD_DIM)
            bias = bias_ref[head, :, 0:WIN_TOK]
            total = None
            for w in range(2):
                rows = slice(w * WIN_TOK, (w + 1) * WIN_TOK)
                q = qkv_ref[rows, group * LANES : (group + 1) * LANES] * mask
                k = qkv_ref[rows, D + group * LANES : D + (group + 1) * LANES] * mask
                v = qkv_ref[rows, 2 * D + group * LANES : 2 * D + (group + 1) * LANES] * mask
                g = gm_ref[rows, cols]
                scores = mm(q, k, NT) * scale + bias
                scores = jnp.where(apart[w], BLOCKED, scores)
                top = jnp.max(scores, axis=-1, keepdims=True)
                expo = jnp.exp(scores - top)
                prob = (expo * (1.0 / jnp.sum(expo, axis=-1, keepdims=True))).astype(low)
                mixed = mm(prob, v, NN)
                grad_attn = mm(g, v, NT)
                gvt_ref[feats, rows] = mm(gmt_ref[feats, rows], prob, NN).astype(low)
                pf = prob.astype(wide)
                grad = pf * (grad_attn - jnp.sum(pf * grad_attn, axis=-1, keepdims=True))
                total = grad if total is None else total + grad
                glow = grad.astype(low)
                gq = mm(glow, k, NN)
                gkt_ref[feats, rows] = (mm(qt_ref[feats, rows], glow, NN) * scale).astype(low)
                if sub == 0:
                    mixed_ref[rows, cols] = mixed
                    gq_ref[rows, cols] = gq
                else:
                    mixed_ref[rows, cols] += mixed
                    gq_ref[rows, cols] += gq
            bg_ref[head] = total

    mixed = mixed_ref[...].astype(low)
    branch = mm(mixed, wout_ref[...], NT).astype(low).astype(wide)
    fin_ref[0] = x_ref[...] + branch

    gq = (gq_ref[...] * scale).astype(low)
    gk = gkt_ref[...].T
    gv = gvt_ref[...].T
    grad_normed = (
        mm(gq, wqkv_ref[0:D, :], NN)
        + mm(gk, wqkv_ref[D : 2 * D, :], NN)
        + mm(gv, wqkv_ref[2 * D : 3 * D, :], NN)
    )
    grad_normed = grad_normed.astype(low).astype(wide)
    standard = std_ref[...]
    scaled = grad_normed * gain
    inner = (
        scaled
        - jnp.mean(scaled, axis=-1, keepdims=True)
        - standard * jnp.mean(scaled * standard, axis=-1, keepdims=True)
    )
    grad_filled = c_ref[...] + inv_std * inner
    fin_ref[1] = jnp.where(masked, 0.0, grad_filled)
    gain_grad = jnp.sum(grad_normed * standard, axis=0, keepdims=True)
    token_grad = jnp.sum(jnp.where(masked, grad_filled, 0.0), axis=0, keepdims=True)

    for which in range(2):
        for zs in range(4):
            z = (zs + 1) % 4
            for a in range(6):
                base = zs * 72 + a * 12
                piece = fin_ref[which, base : base + 12, :].astype(low)
                if a < 3:
                    out_own_ref[which, z, a] = piece
                else:
                    out_lat_ref[which, z, a - 3] = piece

    new = lax.broadcasted_iota(jnp.int32, (D, D), 0)
    old = lax.broadcasted_iota(jnp.int32, (D, D), 1)
    o_new = new // 24
    rest = new - o_new * 24
    a_new = rest // 6
    order = (old == a_new * 96 + o_new * 6 + (rest - a_new * 6)).astype(low)
    parts = []
    for value in (gq, gk, gv, cot):
        turned = mm(order, value, NT).astype(low)
        other = mixed if value is cot else normed
        parts.append(mm(turned, other, NN))
    for o in range(16):
        rows = slice(o * 24, (o + 1) * 24)
        chunk = jnp.concatenate([part[rows] for part in parts], axis=0)
        send_ref[o, 0:96, :] = chunk.astype(low)

    slot = lax.broadcasted_iota(jnp.int32, (QSLOTS, WIN_TOK), 0)
    spot = lax.broadcasted_iota(jnp.int32, (LANES, WIN_TOK), 0)

    def one_row(i, acc):
        ids = ids_ref[pl.ds(i, 1), 0:WIN_TOK]
        near = (ids & (LANES - 1)) == spot
        right = near.astype(wide).astype(low)
        here = (ids >> 7) == slot
        left = jnp.concatenate(
            [
                jnp.where(here, bg_ref[head, pl.ds(i, 1), :], 0.0)
                for head in range(HEADS)
            ],
            axis=0,
        ).astype(low)
        return acc + mm(left, right, NT)

    acc = lax.fori_loop(0, WIN_TOK, one_row, jnp.zeros((HEADS * QSLOTS, LANES), wide))
    row = lax.broadcasted_iota(jnp.int32, (HEADS * QSLOTS, 1), 0)
    for n, vec in enumerate((gain_grad, token_grad)):
        for p in range(3):
            at = row == QSLOTS * p + 6 + n
            acc = jnp.where(at, vec[:, p * LANES : (p + 1) * LANES], acc)
    extra = jnp.concatenate([acc[0:32], acc[32:64], acc[64:96]], axis=1).astype(low)
    for o in range(16):
        send_ref[o, 96:128, :] = extra


def local(
    fields,
    cotangent,
    window_mask,
    mask_token,
    norm_gain,
    qkv_weight,
    out_weight,
    bias_table,
    bias_index,
):
    own_mask = window_mask[:, 0, 0]
    last = (lax.axis_index("lat") == lax.axis_size("lat") - 1).astype(jnp.int32)
    scalars = jnp.concatenate([own_mask, last[None], last[None]])
    level_mask = jnp.repeat(own_mask, 2)[:, None, None, None] == 1
    marked = jnp.where(level_mask, jnp.bfloat16(MARK), fields)

    strip = jnp.stack((marked[:, :3], cotangent[:, :3]))
    lat_in = passed_along(strip, "lat", -1)

    table = jnp.pad(bias_table[0], ((0, 0), (0, 9)))
    ids = jnp.pad(bias_index, ((0, 0), (0, 256 - WIN_TOK)))
    vmem = pl.BlockSpec(memory_space=pltpu.VMEM)
    bias = pl.pallas_call(
        bias_kernel,
        out_shape=jax.ShapeDtypeStruct((HEADS, WIN_TOK, 256), wide),
        in_specs=[vmem, vmem],
        out_specs=vmem,
        compiler_params=pltpu.CompilerParams(vmem_limit_bytes=32 * 2**20),
        cost_estimate=pl.CostEstimate(flops=10**7, bytes_accessed=6 * 10**6, transcendentals=0),
    )(table, ids)

    own = jnp.stack((marked[:, 3:, :6], cotangent[:, 3:, :6]))
    lon_in = passed_along(jnp.concatenate((own, lat_in[:, :, :, :6]), axis=2), "lon", -1)

    out_own, out_lat, send = pl.pallas_call(
        main_kernel,
        out_shape=(
            jax.ShapeDtypeStruct((2, 4, 3, 12, D), low),
            jax.ShapeDtypeStruct((2, 4, 3, 12, D), low),
            jax.ShapeDtypeStruct((16, CHUNK, D), low),
        ),
        in_specs=[pl.BlockSpec(memory_space=pltpu.SMEM)] + [vmem] * 10,
        out_specs=(vmem, vmem, vmem),
        scratch_shapes=[
            pltpu.VMEM((TOK, D), wide),
            pltpu.VMEM((TOK, D), wide),
            pltpu.VMEM((TOK, D), wide),
            pltpu.VMEM((TOK, 3 * D), low),
            pltpu.VMEM((TOK, D), low),
            pltpu.VMEM((D, TOK), low),
            pltpu.VMEM((D, TOK), low),
            pltpu.VMEM((TOK, D), wide),
            pltpu.VMEM((TOK, D), wide),
            pltpu.VMEM((D, TOK), low),
            pltpu.VMEM((D, TOK), low),
            pltpu.VMEM((HEADS, WIN_TOK, WIN_TOK), wide),
            pltpu.VMEM((2, TOK, D), wide),
        ],
        compiler_params=pltpu.CompilerParams(vmem_limit_bytes=48 * 2**20),
        cost_estimate=pl.CostEstimate(
            flops=2 * 10**9, bytes_accessed=10**7, transcendentals=5 * 10**5
        ),
    )(
        scalars,
        fields,
        cotangent,
        lat_in,
        lon_in,
        mask_token.astype(wide)[None],
        norm_gain.astype(wide)[None],
        qkv_weight,
        out_weight,
        bias,
        ids,
    )

    lat_out = passed_along(out_lat, "lat", 1)
    full = jnp.concatenate((lat_out, out_own), axis=2)
    lon_out = passed_along(full[:, :, :, 6:], "lon", 1)

    got = lax.all_to_all(send, "lon", 0, 0, tiled=True)
    summed = jnp.sum(got.astype(wide), axis=0)
    extra = summed[96:].reshape(32, 3, LANES).transpose(1, 0, 2).reshape(HEADS, QSLOTS, LANES)
    table_grad = extra[:, :6].reshape(1, HEADS, 6 * LANES)[:, :, :NBIAS]
    vectors = extra[:3, 6:].transpose(1, 0, 2).reshape(2, D)
    second = jnp.concatenate(
        (summed[:96].reshape(16, 6, D), jnp.broadcast_to(vectors[None], (16, 2, D))), axis=1
    ).astype(low)
    final = jnp.sum(lax.all_to_all(second, "lat", 0, 0, tiled=True).astype(wide), axis=0)

    output = jnp.concatenate((lon_out[0], full[0, :, :, :6]), axis=2)
    input_grad = jnp.concatenate((lon_out[1], full[1, :, :, :6]), axis=2)
    return (output, input_grad, final[:6], table_grad, final[6:])


def solution(mesh):
    placed = (
        P(None, "lat", "lon", None),
        P(None, "lat", "lon", None),
        P(None, "lat", "lon"),
        P(),
        P(),
        P(),
        P(),
        P("lat", None, None),
        P(),
    )
    return jax.shard_map(
        local,
        mesh=mesh,
        in_specs=placed,
        out_specs=(
            P(None, "lat", "lon", None),
            P(None, "lat", "lon", None),
            P(("lat", "lon"), None),
            P("lat", None, None),
            P(),
        ),
        check_vma=False,
    )
```

time: 374 us -> 127 us (0.34)
  blocking collectives: 138 us -> 0 us
  matrix products: 73 us -> 0 us
  Pallas kernels: 0 us -> 47.7 us
  local copies, waits for them, and re-layouts: 45.2 us -> 5.71 us
  waiting for transfers between devices: 77.4 us -> 45.7 us
  starting transfers between devices: 8.48 us -> 23.2 us
  between operations: 14.5 us -> 0.97 us
  other arithmetic: 15.9 us -> 3.11 us
    psum x2 -> x0, blocking collectives: 138 us -> none  [the longest x1 82.3 us: local(): vector_grads = lax.psum(jnp.stack((gain_grad, token_grad)), ('lat', 'lon'))]
    unnamed x2 -> x0, waiting for transfers between devices: 69.7 us -> none
    dot_general x29 -> x0, matrix products: 68.3 us -> none  [the longest x9 37.9 us: pick(): jnp.einsum('rb,nb->rn', flat_table, one_hot_block(ids), precision=lax.Pre...]
    pallas_call x0 -> x2, Pallas kernels: none -> 47.7 us  [the longest x1 43.6 us: local(): pl.pallas_call(main_kernel, out_shape=(jax.ShapeDtypeStruct((2, 4, 3, 12,...]
    ppermute x6 -> x4, waiting for transfers between devices: 7.76 us -> 37.3 us  [passed_along(): return lax.ppermute(value, axis, pairs)]
    dynamic_slice x27 -> x0, local copies, waits for them, and re-layouts: 20 us -> none  [the longest x9 11.3 us: table_sums(): lax.scan(accumulate, start, (flat_grad, index_blocks(bias_index)))]
    all_to_all x0 -> x2, starting transfers between devices: none -> 15.6 us  [the longest x1 8.55 us: local(): lax.all_to_all(second, 'lat', 0, 0, tiled=True).astype(wide)]
    all_to_all x0 -> x2, waiting for transfers between devices: none -> 8.35 us  [the longest x1 8.35 us: local(): lax.all_to_all(second, 'lat', 0, 0, tiled=True).astype(wide)]
  transfers between devices with their start and end apart: 7 -> 6, of which waited for: 4 -> 4; matrix products, arithmetic and copies ran while one was open for 28% -> 2% of each run, Pallas kernels for 0% -> 3%
where the time goes in v1:
time: 127 us; the launch traced here: 126 us
  Pallas kernels  47.7 us (38%)
  waiting for transfers between devices  45.7 us (36%)
  starting transfers between devices  23.2 us (18%)
  local copies, waits for them, and re-layouts  5.71 us (4%)
  other arithmetic  3.11 us (2%)
    pallas_call x1, Pallas kernels, local(): pl.pallas_call(main_kernel, out_shape=(jax.ShapeDtypeStruct((2, 4, 3, 12,...  43.6 us
    ppermute x4, waiting for transfers between devices, passed_along(): return lax.ppermute(value, axis, pairs)  37.3 us
    all_to_all x1, starting transfers between devices, local(): lax.all_to_all(second, 'lat', 0, 0, tiled=True).astype(wide)  8.55 us
    all_to_all x1, waiting for transfers between devices, local(): lax.all_to_all(second, 'lat', 0, 0, tiled=True).astype(wide)  8.35 us
    ppermute x4, starting transfers between devices, passed_along(): return lax.ppermute(value, axis, pairs)  7.66 us
    all_to_all x1, starting transfers between devices, local(): got = lax.all_to_all(send, 'lon', 0, 0, tiled=True)  7.02 us
    unnamed x24, local copies, waits for them, and re-layouts  4.56 us
    pallas_call x1, Pallas kernels, local(): pl.pallas_call(bias_kernel, out_shape=jax.ShapeDtypeStruct((HEADS, WIN_TO...  4.1 us
  transfers between devices with their start and end apart: 6, of which 4 were waited for; matrix products, arithmetic and copies ran while one was open for 2% of the time, Pallas kernels for 3%

profile of v1, /device:TPU:2, one launch (start us, length us, event | category | flops | bytes accessed | tf_op | source)
XLA Modules:
  0.0 126.4 jit_solution(1439599089330274347)
XLA Ops:
  0.6 0.7 broadcast_compare_fusion
  1.3 0.1 broadcast_in_dim.41
  1.4 0.1 eq.17
  1.5 1.0 copy.41.cot_ref
  2.4 0.0 copy-start.6
  2.4 0.0 copy-start.7
  2.5 0.0 copy-start.4
  2.5 0.0 copy-start.3
  2.5 1.1 broadcast_select_fusion
  3.6 0.1 pad_maximum_fusion
  3.7 7.5 %collective-permute-start = (bf16[2,4,3,12,384]{4,3,2,1,0:T(8,128)(2,1)S(1)}, bf16[2,4,3,12,384]{4,3,2,1,0:T(8,128)(2,1)S(1)}, u32[]{:S(2)}, u32[]{:S(2)}) collective-permute-start(bf16[2,4,3,12,384]{4,3,2,1,0:T(8,128)(2,1)S(1)} %pad_maximum_fusion), channel_id=1, source_target_pairs={{0,240},{16,0},{32,16},{48,32},{64,48},{80,64},{96,80},{112,96},{1... | collective-permute-start | bytes 663560 | tf_op jit(solution)/shard_map/ppermute | solution.py:38
  11.2 6.2 %collective-permute-done.lat_ref = bf16[2,4,3,12,384]{4,3,2,1,0:T(8,128)(2,1)S(1)} collective-permute-done((bf16[2,4,3,12,384]{4,3,2,1,0:T(8,128)(2,1)S(1)}, bf16[2,4,3,12,384]{4,3,2,1,0:T(8,128)(2,1)S(1)}, u32[]{:S(2)}, u32[]{:S(2)}) %collective-permute-start) | collective-permute-done | bytes 221216 | tf_op jit(solution)/shard_map/ppermute | solution.py:38
  17.5 0.0 copy-start.8
  17.5 0.0 copy-start.1
  17.5 0.0 copy-start.2
  17.5 0.1 pad_maximum_fusion.1
  17.6 0.1 collective-permute-start.1
  17.7 0.0 copy-done.6
  17.7 0.0 copy-done.7
  17.7 0.0 copy-done.4
  17.8 0.0 copy-done.3
  17.8 4.1 %shard_map.128.bias_ref = f32[12,144,256]{2,1,0:T(8,128)S(1)} custom-call(f32[12,768]{1,0:T(8,128)S(1)} %pad.8.table_ref, s32[144,256]{1,0:T(8,128)S(1)} %pad.9.ids_ref), custom_call_target="tpu_custom_call" | custom-call | flops 10000000 | bytes 6000000 | tf_op jit(solution)/shard_map/pallas_call | solution.py:274
  21.9 0.0 copy-start
  21.9 1.2 copy-done
  23.1 0.0 copy-done.8
  23.1 0.1 pad_add_fusion.scal_ref
  23.2 0.0 collective-permute-done.1.lon_ref
  23.2 0.0 copy-done.1
  23.2 0.0 copy-done.2
  23.2 43.6 %shard_map.129 = (bf16[2,4,3,12,384]{4,3,2,1,0:T(8,128)(2,1)S(1)}, bf16[2,4,3,12,384]{4,3,2,1,0:T(8,128)(2,1)S(1)}, bf16[16,128,384]{2,1,0:T(8,128)(2,1)}) custom-call(s32[4]{0:T(128)S(1)} %pad_add_fusion.scal_ref, bf16[4,6,12,384]{3,2,1,0:T(8,128)(2,1)S(1)} %get-tuple-element.36.fields_ref, bf16[4,6,12,384]{3,2,1,0:T(8,128)(2,1)S(1)} %copy.41.cot_ref, ...), custom_call_target="tpu_custom_call" | custom-call | flops 2000000000 | bytes 10000000 | tf_op jit(solution)/shard_map/pallas_call | solution.py:286
  66.8 7.0 %all-to-all-start = ((bf16[16,128,384]{2,1,0:T(8,128)(2,1)}), bf16[16,128,384]{2,1,0:T(8,128)(2,1)S(1)}, u32[]{:S(2)}, u32[]{:S(2)}) async-start(bf16[16,128,384]{2,1,0:T(8,128)(2,1)} %get-tuple-element.10), calls=%async_computation | async-start | bytes 3145728 | tf_op jit(solution)/shard_map/all_to_all | solution.py:332
  73.9 0.0 collective-permute-start.2
  73.9 25.0 %collective-permute-done.2 = bf16[2,4,3,12,384]{4,3,2,1,0:T(8,128)(2,1)S(1)} collective-permute-done((bf16[2,4,3,12,384]{4,3,2,1,0:T(8,128)(2,1)S(1)}, bf16[2,4,3,12,384]{4,3,2,1,0:T(8,128)(2,1)S(1)}, u32[]{:S(2)}, u32[]{:S(2)}) %collective-permute-start.2) | collective-permute-done | bytes 221216 | tf_op jit(solution)/shard_map/ppermute | solution.py:38
  98.9 0.1 slice.74
  99.0 0.1 collective-permute-start.3
  99.1 6.1 %collective-permute-done.3 = bf16[2,4,6,6,384]{4,3,2,1,0:T(8,128)(2,1)S(1)} collective-permute-done((bf16[2,4,6,6,384]{4,3,2,1,0:T(8,128)(2,1)S(1)}, bf16[2,4,6,6,384]{4,3,2,1,0:T(8,128)(2,1)S(1)}, u32[]{:S(2)}, u32[]{:S(2)}) %collective-permute-start.3) | collective-permute-done | bytes 221216 | tf_op jit(solution)/shard_map/ppermute | solution.py:38
  105.3 0.0 all-to-all-done
  105.3 0.2 convert_reduce_fusion
  105.7 0.7 pad_maximum_fusion.4
  106.4 8.6 %all-to-all-start.1 = ((bf16[16,8,384]{2,1,0:T(8,128)(2,1)}), bf16[16,8,384]{2,1,0:T(8,128)(2,1)S(1)}, u32[]{:S(2)}, u32[]{:S(2)}) async-start(bf16[16,8,384]{2,1,0:T(8,128)(2,1)} %pad_maximum_fusion.4), calls=%async_computation.1 | async-start | bytes 196608 | tf_op jit(solution)/shard_map/all_to_all | solution.py:340
  114.9 0.1 pad_maximum_fusion.3
  115.0 0.8 copy.44
  115.8 0.1 pad_maximum_fusion.2
  115.9 0.8 copy.43
  116.7 0.7 copy.45
  117.4 8.4 %all-to-all-done.1 = bf16[16,8,384]{2,1,0:T(8,128)(2,1)S(1)} async-done(((bf16[16,8,384]{2,1,0:T(8,128)(2,1)}), bf16[16,8,384]{2,1,0:T(8,128)(2,1)S(1)}, u32[]{:S(2)}, u32[]{:S(2)}) %all-to-all-start.1) | async-done | bytes 98336 | tf_op jit(solution)/shard_map/all_to_all | solution.py:340
  125.8 0.0 copy-start.5
  125.8 0.6 slice.85
  126.4 0.0 copy-done.5
  (21 shorter events, 0.4 us)
Async XLA Ops:
  2.4 15.3 %copy-start.6 = (bf16[384]{0:T(512)(128)(2,1)S(1)}, bf16[384]{0:T(512)(128)(2,1)}, u32[]{:S(2)}) copy-start(bf16[384]{0:T(512)(128)(2,1)} %param.12) | copy-start | bytes 2308
  2.4 15.3 %copy-start.7 = (bf16[384]{0:T(512)(128)(2,1)S(1)}, bf16[384]{0:T(512)(128)(2,1)}, u32[]{:S(2)}) copy-start(bf16[384]{0:T(512)(128)(2,1)} %param.13) | copy-start | bytes 2308
  2.5 15.3 %copy-start.4 = (f32[1,12,759]{2,0,1:T(1,128)S(1)}, f32[1,12,759]{2,0,1:T(1,128)}, u32[]{:S(2)}) copy-start(f32[1,12,759]{2,0,1:T(1,128)} %param.16) | copy-start | bytes 109300
  2.5 15.3 %copy-start.3 = (s32[144,144]{1,0:T(8,128)S(1)}, s32[144,144]{1,0:T(8,128)}, u32[]{:S(2)}) copy-start(s32[144,144]{1,0:T(8,128)} %param.17) | copy-start | bytes 248836
  3.7 13.8 %collective-permute-start = (bf16[2,4,3,12,384]{4,3,2,1,0:T(8,128)(2,1)S(1)}, bf16[2,4,3,12,384]{4,3,2,1,0:T(8,128)(2,1)S(1)}, u32[]{:S(2)}, u32[]{:S(2)}) collective-permute-start(bf16[2,4,3,12,384]{4,3,2,1,0:T(8,128)(2,1)S(1)} %pad_maximum_fusion), channel_id=1, source_target_pairs={{0,240},{16,0},{32,16},{48,32},{64,48},{80,64},{96,80},{112,96},{1... | collective-permute-start | bytes 663560 | tf_op jit(solution)/shard_map/ppermute | solution.py:38
  17.5 5.7 %copy-start.8 = (s32[2,1,1]{0,2,1:T(1,128)S(1)}, s32[2,1,1]{0,2,1:T(1,128)}, u32[]{:S(2)}) copy-start(s32[2,1,1]{0,2,1:T(1,128)} %param.11) | copy-start | bytes 28
  17.5 5.8 %copy-start.1 = (bf16[1152,384]{1,0:T(8,128)(2,1)S(1)}, bf16[1152,384]{1,0:T(8,128)(2,1)}, u32[]{:S(2)}) copy-start(bf16[1152,384]{1,0:T(8,128)(2,1)} %wqkv_ref.1) | copy-start | bytes 2654212
  17.5 5.8 %copy-start.2 = (bf16[384,384]{1,0:T(8,128)(2,1)S(1)}, bf16[384,384]{1,0:T(8,128)(2,1)}, u32[]{:S(2)}) copy-start(bf16[384,384]{1,0:T(8,128)(2,1)} %wout_ref.1) | copy-start | bytes 884740
  17.6 5.6 %collective-permute-start.1 = (bf16[2,4,6,6,384]{4,3,2,1,0:T(8,128)(2,1)S(1)}, bf16[2,4,6,6,384]{4,3,2,1,0:T(8,128)(2,1)S(1)}, u32[]{:S(2)}, u32[]{:S(2)}) collective-permute-start(bf16[2,4,6,6,384]{4,3,2,1,0:T(8,128)(2,1)S(1)} %pad_maximum_fusion.1), channel_id=1, source_target_pairs={{0,15},{1,0},{2,1},{3,2},{4,3},{5,4},{6,5},{7,6},{8,7},{9,8},{10,9... | collective-permute-start | bytes 663560 | tf_op jit(solution)/shard_map/ppermute | solution.py:38
  21.9 1.2 copy-start
  66.8 38.4 %all-to-all-start = ((bf16[16,128,384]{2,1,0:T(8,128)(2,1)}), bf16[16,128,384]{2,1,0:T(8,128)(2,1)S(1)}, u32[]{:S(2)}, u32[]{:S(2)}) async-start(bf16[16,128,384]{2,1,0:T(8,128)(2,1)} %get-tuple-element.10), calls=%async_computation | async-start | bytes 3145728 | tf_op jit(solution)/shard_map/all_to_all | solution.py:332
  73.9 25.0 %collective-permute-start.2 = (bf16[2,4,3,12,384]{4,3,2,1,0:T(8,128)(2,1)S(1)}, bf16[2,4,3,12,384]{4,3,2,1,0:T(8,128)(2,1)S(1)}, u32[]{:S(2)}, u32[]{:S(2)}) collective-permute-start(bf16[2,4,3,12,384]{4,3,2,1,0:T(8,128)(2,1)S(1)} %get-tuple-element.8), channel_id=1, source_target_pairs={{0,16},{16,32},{32,48},{48,64},{64,80},{80,96},{96,112},{112,128},... | collective-permute-start | bytes 663560 | tf_op jit(solution)/shard_map/ppermute | solution.py:38
  99.0 6.2 %collective-permute-start.3 = (bf16[2,4,6,6,384]{4,3,2,1,0:T(8,128)(2,1)S(1)}, bf16[2,4,6,6,384]{4,3,2,1,0:T(8,128)(2,1)S(1)}, u32[]{:S(2)}, u32[]{:S(2)}) collective-permute-start(bf16[2,4,6,6,384]{4,3,2,1,0:T(8,128)(2,1)S(1)} %slice.74), channel_id=1, source_target_pairs={{0,1},{1,2},{2,3},{3,4},{4,5},{5,6},{6,7},{7,8},{8,9},{9,10},{10,1... | collective-permute-start | bytes 663560 | tf_op jit(solution)/shard_map/ppermute | solution.py:38
  106.4 19.4 %all-to-all-start.1 = ((bf16[16,8,384]{2,1,0:T(8,128)(2,1)}), bf16[16,8,384]{2,1,0:T(8,128)(2,1)S(1)}, u32[]{:S(2)}, u32[]{:S(2)}) async-start(bf16[16,8,384]{2,1,0:T(8,128)(2,1)} %pad_maximum_fusion.4), calls=%async_computation.1 | async-start | bytes 196608 | tf_op jit(solution)/shard_map/all_to_all | solution.py:340
  125.8 0.6 copy-start.5

commit v2 on v1

--- a/solution.py
+++ b/solution.py
@@ -73,9 +73,11 @@
     wout_ref,
     bias_ref,
     ids_ref,
+    rest_ref,
     out_own_ref,
     out_lat_ref,
-    send_ref,
+    keep_ref,
+    give_ref,
     x_ref,
     c_ref,
     std_ref,
@@ -88,21 +90,32 @@
     gkt_ref,
     gvt_ref,
     bg_ref,
-    fin_ref,
+    bt_ref,
+    rem_ref,
+    mix_ref,
 ):
+    level = lax.broadcasted_iota(jnp.int32, (4, 1), 0)
+    own_masked = jnp.where(level < 2, scal_ref[0], scal_ref[1]) == 1
     for which, own, dest in ((0, fields_ref, x_ref), (1, cot_ref, c_ref)):
+        for a in range(6):
+            for o in range(12):
+                if o >= 6:
+                    piece = lon_ref[which, a, o - 6]
+                elif a >= 3:
+                    piece = lat_ref[which, a - 3, 6 + o]
+                else:
+                    piece = own[3 + a, 6 + o]
+                piece = piece.astype(wide)
+                if which == 0 and o < 6 and a < 3:
+                    piece = jnp.where(own_masked, MARK, piece)
+                base = (a * 12 + o) * 4
+                for c in range(3):
+                    mix_ref[c, base : base + 4, :] = piece[:, c * LANES : (c + 1) * LANES]
         for zs in range(4):
-            z = (zs + 1) % 4
-            for a in range(6):
-                base = zs * 72 + a * 12
-                if a < 3:
-                    piece = own[z, 3 + a].astype(wide)[6:12]
-                    if which == 0:
-                        piece = jnp.where(scal_ref[z // 2] == 1, MARK, piece)
-                else:
-                    piece = lat_ref[which, z, a - 3].astype(wide)[6:12]
-                dest[base : base + 6, :] = piece
-                dest[base + 6 : base + 12, :] = lon_ref[which, z, a].astype(wide)
+            for c in range(3):
+                dest[zs * 72 : (zs + 1) * 72, c * LANES : (c + 1) * LANES] = mix_ref[
+                    c, pl.ds((zs + 1) % 4, 72, stride=4), :
+                ]
     raw = x_ref[...]
     masked = raw > 0.5 * MARK
     filled = jnp.where(masked, token_ref[...], raw)
@@ -117,8 +130,10 @@
 
     qkv_ref[...] = mm(normed, wqkv_ref[...], NT).astype(low)
     gm_ref[...] = mm(cot, wout_ref[...], NN).astype(low)
-    qt_ref[...] = mm(wqkv_ref[0:D, :], normed, NT).astype(low)
-    gmt_ref[...] = mm(wout_ref[...], cot, (((0,), (1,)), ((), ()))).astype(low)
+    for w in range(2):
+        rows = slice(w * WIN_TOK, (w + 1) * WIN_TOK)
+        qt_ref[w] = mm(wqkv_ref[0:D, :], normed[rows], NT).astype(low)
+        gmt_ref[w] = mm(wout_ref[...], cot[rows], (((0,), (1,)), ((), ()))).astype(low)
 
     last = scal_ref[2] == 1
     ti = lax.broadcasted_iota(jnp.int32, (WIN_TOK, WIN_TOK), 0)
@@ -134,6 +149,8 @@
     scale = HEAD_DIM ** (-0.5)
     for group in range(3):
         cols = slice(group * LANES, (group + 1) * LANES)
+        mixed_sum = [None, None]
+        gq_sum = [None, None]
         for sub in range(4):
             head = group * 4 + sub
             mask = (lane == sub).astype(low)
@@ -153,28 +170,44 @@
                 prob = (expo * (1.0 / jnp.sum(expo, axis=-1, keepdims=True))).astype(low)
                 mixed = mm(prob, v, NN)
                 grad_attn = mm(g, v, NT)
-                gvt_ref[feats, rows] = mm(gmt_ref[feats, rows], prob, NN).astype(low)
-                pf = prob.astype(wide)
-                grad = pf * (grad_attn - jnp.sum(pf * grad_attn, axis=-1, keepdims=True))
+                gvt_ref[w, feats, :] = mm(gmt_ref[w, feats, :], prob, NN).astype(low)
+                delta = jnp.sum(g.astype(wide) * mixed, axis=-1, keepdims=True)
+                grad = prob.astype(wide) * (grad_attn - delta)
                 total = grad if total is None else total + grad
                 glow = grad.astype(low)
                 gq = mm(glow, k, NN)
-                gkt_ref[feats, rows] = (mm(qt_ref[feats, rows], glow, NN) * scale).astype(low)
-                if sub == 0:
-                    mixed_ref[rows, cols] = mixed
-                    gq_ref[rows, cols] = gq
+                gkt_ref[w, feats, :] = (mm(qt_ref[w, feats, :], glow, NN) * scale).astype(low)
+                mixed_sum[w] = mixed if sub == 0 else mixed_sum[w] + mixed
+                gq_sum[w] = gq if sub == 0 else gq_sum[w] + gq
+            bg_ref[head] = total[:, 0:LANES]
+            bt_ref[head, :, 0:16] = total[:, LANES:WIN_TOK]
+        for w in range(2):
+            rows = slice(w * WIN_TOK, (w + 1) * WIN_TOK)
+            mixed_ref[rows, cols] = mixed_sum[w].astype(low)
+            gq_ref[rows, cols] = (gq_sum[w] * scale).astype(low)
+
+    def put_back(which, value):
+        for zs in range(4):
+            for c in range(3):
+                mix_ref[c, pl.ds((zs + 1) % 4, 72, stride=4), :] = value[
+                    zs * 72 : (zs + 1) * 72, c * LANES : (c + 1) * LANES
+                ]
+        for a in range(6):
+            for o in range(12):
+                base = (a * 12 + o) * 4
+                piece = jnp.concatenate([mix_ref[c, base : base + 4, :] for c in range(3)], axis=1)
+                if a < 3:
+                    out_own_ref[which, a, o] = piece.astype(low)
                 else:
-                    mixed_ref[rows, cols] += mixed
-                    gq_ref[rows, cols] += gq
-            bg_ref[head] = total
-
-    mixed = mixed_ref[...].astype(low)
+                    out_lat_ref[which, a - 3, o] = piece.astype(low)
+
+    mixed = mixed_ref[...]
     branch = mm(mixed, wout_ref[...], NT).astype(low).astype(wide)
-    fin_ref[0] = x_ref[...] + branch
-
-    gq = (gq_ref[...] * scale).astype(low)
-    gk = gkt_ref[...].T
-    gv = gvt_ref[...].T
+    put_back(0, x_ref[...] + branch)
+
+    gq = gq_ref[...]
+    gk = jnp.concatenate([gkt_ref[w].T for w in range(2)], axis=0)
+    gv = jnp.concatenate([gvt_ref[w].T for w in range(2)], axis=0)
     grad_normed = (
         mm(gq, wqkv_ref[0:D, :], NN)
         + mm(gk, wqkv_ref[D : 2 * D, :], NN)
@@ -189,25 +222,17 @@
         - standard * jnp.mean(scaled * standard, axis=-1, keepdims=True)
     )
     grad_filled = c_ref[...] + inv_std * inner
-    fin_ref[1] = jnp.where(masked, 0.0, grad_filled)
+    put_back(1, jnp.where(masked, 0.0, grad_filled))
     gain_grad = jnp.sum(grad_normed * standard, axis=0, keepdims=True)
     token_grad = jnp.sum(jnp.where(masked, grad_filled, 0.0), axis=0, keepdims=True)
 
-    for which in range(2):
-        for zs in range(4):
-            z = (zs + 1) % 4
-            for a in range(6):
-                base = zs * 72 + a * 12
-                piece = fin_ref[which, base : base + 12, :].astype(low)
-                if a < 3:
-                    out_own_ref[which, z, a] = piece
-                else:
-                    out_lat_ref[which, z, a - 3] = piece
-
     new = lax.broadcasted_iota(jnp.int32, (D, D), 0)
     old = lax.broadcasted_iota(jnp.int32, (D, D), 1)
-    o_new = new // 24
-    rest = new - o_new * 24
+    n_new = new // 24
+    rest = new - n_new * 24
+    half = n_new // 8
+    core = scal_ref[3]
+    o_new = 2 * (n_new - 8 * half) + (core + half - 2 * core * half)
     a_new = rest // 6
     order = (old == a_new * 96 + o_new * 6 + (rest - a_new * 6)).astype(low)
     parts = []
@@ -218,34 +243,45 @@
     for o in range(16):
         rows = slice(o * 24, (o + 1) * 24)
         chunk = jnp.concatenate([part[rows] for part in parts], axis=0)
-        send_ref[o, 0:96, :] = chunk.astype(low)
-
-    slot = lax.broadcasted_iota(jnp.int32, (QSLOTS, WIN_TOK), 0)
-    spot = lax.broadcasted_iota(jnp.int32, (LANES, WIN_TOK), 0)
-
-    def one_row(i, acc):
-        ids = ids_ref[pl.ds(i, 1), 0:WIN_TOK]
-        near = (ids & (LANES - 1)) == spot
-        right = near.astype(wide).astype(low)
-        here = (ids >> 7) == slot
-        left = jnp.concatenate(
-            [
-                jnp.where(here, bg_ref[head, pl.ds(i, 1), :], 0.0)
-                for head in range(HEADS)
-            ],
-            axis=0,
-        ).astype(low)
+        dest = keep_ref if o < 8 else give_ref
+        dest[o % 8, 0:96, :] = chunk.astype(low)
+
+    slot = lax.broadcasted_iota(jnp.int32, (QSLOTS, LANES), 0)
+    spot = lax.broadcasted_iota(jnp.int32, (LANES, LANES), 0)
+    for head in range(HEADS):
+        rem_ref[head] = jnp.concatenate(
+            [bt_ref[head, pl.ds(k, 18, stride=8), :][:, 0:16] for k in range(8)], axis=1
+        )
+
+    def one_step(step, acc):
+        lefts = []
+        rights = []
+        for s in range(9):
+            if s < 8:
+                ids = ids_ref[pl.ds(step * 8 + s, 1), :]
+                vals = [bg_ref[head, pl.ds(step * 8 + s, 1), :] for head in range(HEADS)]
+            else:
+                ids = rest_ref[pl.ds(step, 1), :]
+                vals = [rem_ref[head, pl.ds(step, 1), :] for head in range(HEADS)]
+            rights.append(((ids & (LANES - 1)) == spot).astype(wide).astype(low))
+            here = (ids >> 7) == slot
+            lefts.append(
+                jnp.concatenate([jnp.where(here, val, 0.0) for val in vals], axis=0).astype(low)
+            )
+        left = jnp.concatenate(lefts, axis=1)
+        right = jnp.concatenate(rights, axis=1)
         return acc + mm(left, right, NT)
 
-    acc = lax.fori_loop(0, WIN_TOK, one_row, jnp.zeros((HEADS * QSLOTS, LANES), wide))
+    acc = lax.fori_loop(0, 18, one_step, jnp.zeros((HEADS * QSLOTS, LANES), wide))
     row = lax.broadcasted_iota(jnp.int32, (HEADS * QSLOTS, 1), 0)
     for n, vec in enumerate((gain_grad, token_grad)):
         for p in range(3):
             at = row == QSLOTS * p + 6 + n
             acc = jnp.where(at, vec[:, p * LANES : (p + 1) * LANES], acc)
     extra = jnp.concatenate([acc[0:32], acc[32:64], acc[64:96]], axis=1).astype(low)
-    for o in range(16):
-        send_ref[o, 96:128, :] = extra
+    for n in range(8):
+        keep_ref[n, 96:128, :] = extra
+        give_ref[n, 96:128, :] = extra
 
 
 def local(
@@ -260,12 +296,13 @@
     bias_index,
 ):
     own_mask = window_mask[:, 0, 0]
-    last = (lax.axis_index("lat") == lax.axis_size("lat") - 1).astype(jnp.int32)
-    scalars = jnp.concatenate([own_mask, last[None], last[None]])
-    level_mask = jnp.repeat(own_mask, 2)[:, None, None, None] == 1
-    marked = jnp.where(level_mask, jnp.bfloat16(MARK), fields)
-
-    strip = jnp.stack((marked[:, :3], cotangent[:, :3]))
+    last = lax.axis_index("lat") == lax.axis_size("lat") - 1
+    core = lax.axis_index("lon") % 2
+    scalars = jnp.concatenate([own_mask, jnp.stack([last.astype(jnp.int32), core])])
+    fields = fields.transpose(1, 2, 0, 3)
+    cotangent = cotangent.transpose(1, 2, 0, 3)
+    hidden = jnp.repeat(own_mask, 2)[:, None] == 1
+    strip = jnp.stack((jnp.where(hidden, jnp.bfloat16(MARK), fields[:3]), cotangent[:3]))
     lat_in = passed_along(strip, "lat", -1)
 
     table = jnp.pad(bias_table[0], ((0, 0), (0, 9)))
@@ -276,38 +313,42 @@
         out_shape=jax.ShapeDtypeStruct((HEADS, WIN_TOK, 256), wide),
         in_specs=[vmem, vmem],
         out_specs=vmem,
-        compiler_params=pltpu.CompilerParams(vmem_limit_bytes=32 * 2**20),
+        compiler_params=pltpu.CompilerParams(vmem_limit_bytes=8 * 2**20),
         cost_estimate=pl.CostEstimate(flops=10**7, bytes_accessed=6 * 10**6, transcendentals=0),
     )(table, ids)
 
-    own = jnp.stack((marked[:, 3:, :6], cotangent[:, 3:, :6]))
-    lon_in = passed_along(jnp.concatenate((own, lat_in[:, :, :, :6]), axis=2), "lon", -1)
-
-    out_own, out_lat, send = pl.pallas_call(
+    lat_in, bias = lax.optimization_barrier((lat_in, bias))
+    own = jnp.stack((jnp.where(hidden, jnp.bfloat16(MARK), fields[3:, :6]), cotangent[3:, :6]))
+    lon_in = passed_along(jnp.concatenate((own, lat_in[:, :, :6]), axis=1), "lon", -1)
+
+    out_own, out_lat, keep, give = pl.pallas_call(
         main_kernel,
         out_shape=(
-            jax.ShapeDtypeStruct((2, 4, 3, 12, D), low),
-            jax.ShapeDtypeStruct((2, 4, 3, 12, D), low),
-            jax.ShapeDtypeStruct((16, CHUNK, D), low),
+            jax.ShapeDtypeStruct((2, 3, 12, 4, D), low),
+            jax.ShapeDtypeStruct((2, 3, 12, 4, D), low),
+            jax.ShapeDtypeStruct((8, CHUNK, D), low),
+            jax.ShapeDtypeStruct((8, CHUNK, D), low),
         ),
-        in_specs=[pl.BlockSpec(memory_space=pltpu.SMEM)] + [vmem] * 10,
-        out_specs=(vmem, vmem, vmem),
+        in_specs=[pl.BlockSpec(memory_space=pltpu.SMEM)] + [vmem] * 11,
+        out_specs=(vmem, vmem, vmem, vmem),
         scratch_shapes=[
             pltpu.VMEM((TOK, D), wide),
             pltpu.VMEM((TOK, D), wide),
             pltpu.VMEM((TOK, D), wide),
             pltpu.VMEM((TOK, 3 * D), low),
             pltpu.VMEM((TOK, D), low),
-            pltpu.VMEM((D, TOK), low),
-            pltpu.VMEM((D, TOK), low),
-            pltpu.VMEM((TOK, D), wide),
-            pltpu.VMEM((TOK, D), wide),
-            pltpu.VMEM((D, TOK), low),
-            pltpu.VMEM((D, TOK), low),
-            pltpu.VMEM((HEADS, WIN_TOK, WIN_TOK), wide),
-            pltpu.VMEM((2, TOK, D), wide),
+            pltpu.VMEM((2, D, WIN_TOK), low),
+            pltpu.VMEM((2, D, WIN_TOK), low),
+            pltpu.VMEM((TOK, D), low),
+            pltpu.VMEM((TOK, D), low),
+            pltpu.VMEM((2, D, WIN_TOK), low),
+            pltpu.VMEM((2, D, WIN_TOK), low),
+            pltpu.VMEM((HEADS, WIN_TOK, LANES), wide),
+            pltpu.VMEM((HEADS, WIN_TOK, LANES), wide),
+            pltpu.VMEM((HEADS, 18, LANES), wide),
+            pltpu.VMEM((3, TOK, LANES), wide),
         ],
-        compiler_params=pltpu.CompilerParams(vmem_limit_bytes=48 * 2**20),
+        compiler_params=pltpu.CompilerParams(vmem_limit_bytes=24 * 2**20),
         cost_estimate=pl.CostEstimate(
             flops=2 * 10**9, bytes_accessed=10**7, transcendentals=5 * 10**5
         ),
@@ -322,14 +363,16 @@
         qkv_weight,
         out_weight,
         bias,
-        ids,
+        bias_index[:, :LANES],
+        bias_index[:, LANES:].reshape(18, 8 * 16),
     )
 
+    size = lax.axis_size("lon")
+    taken = lax.ppermute(give, "lon", [(i, i ^ 1) for i in range(size)])
     lat_out = passed_along(out_lat, "lat", 1)
-    full = jnp.concatenate((lat_out, out_own), axis=2)
-    lon_out = passed_along(full[:, :, :, 6:], "lon", 1)
-
-    got = lax.all_to_all(send, "lon", 0, 0, tiled=True)
+    pair = (keep.astype(wide) + taken.astype(wide)).astype(low)
+    groups = [list(range(c, size, 2)) for c in range(2)]
+    got = lax.all_to_all(pair, "lon", 0, 0, axis_index_groups=groups, tiled=True)
     summed = jnp.sum(got.astype(wide), axis=0)
     extra = summed[96:].reshape(32, 3, LANES).transpose(1, 0, 2).reshape(HEADS, QSLOTS, LANES)
     table_grad = extra[:, :6].reshape(1, HEADS, 6 * LANES)[:, :, :NBIAS]
@@ -337,10 +380,12 @@
     second = jnp.concatenate(
         (summed[:96].reshape(16, 6, D), jnp.broadcast_to(vectors[None], (16, 2, D))), axis=1
     ).astype(low)
+    full = jnp.concatenate((lat_out, out_own), axis=1)
+    full, second = lax.optimization_barrier((full, second))
+    lon_out = passed_along(full[:, :, 6:], "lon", 1)
     final = jnp.sum(lax.all_to_all(second, "lat", 0, 0, tiled=True).astype(wide), axis=0)
-
-    output = jnp.concatenate((lon_out[0], full[0, :, :, :6]), axis=2)
-    input_grad = jnp.concatenate((lon_out[1], full[1, :, :, :6]), axis=2)
+    done = jnp.concatenate((lon_out, full[:, :, :6]), axis=2).transpose(0, 3, 1, 2, 4)
+    output, input_grad = done[0], done[1]
     return (output, input_grad, final[:6], table_grad, final[6:])
 
 

time: 127 us -> 92.2 us (0.73)
  the two profiles are of different devices: /device:TPU:2 before, /device:TPU:1 now
where the time goes in v2:
time: 92.2 us; the launch traced here: 91.8 us
  waiting for transfers between devices  28.3 us (31%)
  starting transfers between devices  27 us (29%)
  Pallas kernels  25.2 us (27%)
  local copies, waits for them, and re-layouts  5.63 us (6%)
  other arithmetic  4.76 us (5%)
  between operations  0.94 us (1%)
    pallas_call x1, Pallas kernels, local(): pl.pallas_call(main_kernel, out_shape=(jax.ShapeDtypeStruct((2, 3, 12, 4,...  21.1 us
    ppermute x4, waiting for transfers between devices, passed_along(): return lax.ppermute(value, axis, pairs)  17.5 us
    ppermute x4, starting transfers between devices, passed_along(): return lax.ppermute(value, axis, pairs)  10.2 us
    all_to_all x1, starting transfers between devices, local(): lax.all_to_all(second, 'lat', 0, 0, tiled=True).astype(wide)  10.1 us
    all_to_all x1, waiting for transfers between devices, local(): lax.all_to_all(second, 'lat', 0, 0, tiled=True).astype(wide)  8.86 us
    all_to_all x1, starting transfers between devices, local(): lax.all_to_all(pair, 'lon', 0, 0, axis_index_groups=groups, tiled=True)  5.27 us
    pallas_call x1, Pallas kernels, local(): pl.pallas_call(bias_kernel, out_shape=jax.ShapeDtypeStruct((HEADS, WIN_TO...  4.09 us
    unnamed x20, local copies, waits for them, and re-layouts  2.64 us
  transfers between devices with their start and end apart: 7, of which 4 were waited for; matrix products, arithmetic and copies ran while one was open for 4% of the time, Pallas kernels for 4%

profile of v2, /device:TPU:1, one launch (start us, length us, event | category | flops | bytes accessed | tf_op | source)
XLA Modules:
  0.0 91.8 jit_solution(163036608884801674)
XLA Ops:
  0.6 0.7 broadcast_compare_fusion
  1.3 0.1 broadcast_in_dim.44
  1.4 0.1 eq.18
  1.5 0.0 copy-start
  1.5 0.0 copy-start.1
  1.5 1.1 %slice_bitcast_fusion.2 = (bf16[1,3,12,4,384]{4,3,2,1,0:T(4,128)(2,1)S(1)}, bf16[1,3,12,4,384]{4,3,2,1,0:T(4,128)(2,1)S(1)}) fusion(bf16[6,12,4,384]{3,2,1,0:T(4,128)(2,1)} %bitcast.35, bf16[6,12,4,384]{3,2,1,0:T(4,128)(2,1)} %bitcast.32, pred[4]{0:T(512)(128)(4,1)S(1)} %eq.18), kind=kLoop, calls=%fused_computation.10 | loop fusion | flops 55296 | bytes 442372 | tf_op jit(solution)/shard_map/stack | solution.py:305
  2.6 0.2 pad_maximum_fusion.1
  2.7 8.9 %collective-permute-start = (bf16[2,3,12,4,384]{4,3,2,1,0:T(4,128)(2,1)S(1)}, bf16[2,3,12,4,384]{4,3,2,1,0:T(4,128)(2,1)S(1)}, u32[]{:S(2)}, u32[]{:S(2)}) collective-permute-start(bf16[2,3,12,4,384]{4,3,2,1,0:T(4,128)(2,1)S(1)} %pad_maximum_fusion.1), channel_id=1, source_target_pairs={{0,240},{16,0},{32,16},{48,32},{64,48},{80,64},{96,80},{112,96},{1... | collective-permute-start | bytes 663560 | tf_op jit(solution)/shard_map/ppermute | solution.py:38
  11.7 0.8 copy.20
  12.5 0.9 %pad.9.ids_ref = s32[144,256]{1,0:T(8,128)S(1)} pad(s32[144,144]{1,0:T(8,128)} %param.17, s32[]{:T(128)} %constant.24.clone.1), padding=0_0x0_112 | pad | bytes 230404 | tf_op jit(solution)/shard_map/jit(_pad)/pad | solution.py:309
  13.4 0.0 copy-start.4
  13.4 0.0 copy-start.6
  13.4 0.0 copy-start.7
  13.4 0.0 slice-start
  13.4 0.0 copy-start.8
  13.5 0.0 copy-start.3
  13.5 4.1 %shard_map.128.bias_ref = f32[12,144,256]{2,1,0:T(8,128)S(1)} custom-call(f32[12,768]{1,0:T(8,128)S(1)} %pad.8.table_ref, s32[144,256]{1,0:T(8,128)S(1)} %pad.9.ids_ref), custom_call_target="tpu_custom_call" | custom-call | flops 10000000 | bytes 6000000 | tf_op jit(solution)/shard_map/pallas_call | solution.py:311
  17.6 0.0 copy-done
  17.6 0.0 copy-done.1
  17.6 0.1 slice_bitcast_fusion.3
  17.7 0.0 collective-permute-done.lat_ref
  17.7 0.2 pad_maximum_fusion.2
  17.9 1.2 %collective-permute-start.1 = (bf16[2,6,6,4,384]{4,3,2,1,0:T(4,128)(2,1)S(1)}, bf16[2,6,6,4,384]{4,3,2,1,0:T(4,128)(2,1)S(1)}, u32[]{:S(2)}, u32[]{:S(2)}) collective-permute-start(bf16[2,6,6,4,384]{4,3,2,1,0:T(4,128)(2,1)S(1)} %pad_maximum_fusion.2), channel_id=1, source_target_pairs={{0,15},{1,0},{2,1},{3,2},{4,3},{5,4},{6,5},{7,6},{8,7},{9,8},{10,9... | collective-permute-start | bytes 663560 | tf_op jit(solution)/shard_map/ppermute | solution.py:38
  19.1 0.0 copy-done.4
  19.1 0.0 copy-done.6
  19.2 0.0 copy-done.7
  19.2 0.0 slice-done
  19.2 0.1 reshape.36.rest_ref
  19.3 0.0 copy-done.8
  19.3 0.1 pad_add_fusion.scal_ref
  19.4 4.1 %collective-permute-done.1.lon_ref = bf16[2,6,6,4,384]{4,3,2,1,0:T(4,128)(2,1)S(1)} collective-permute-done((bf16[2,6,6,4,384]{4,3,2,1,0:T(4,128)(2,1)S(1)}, bf16[2,6,6,4,384]{4,3,2,1,0:T(4,128)(2,1)S(1)}, u32[]{:S(2)}, u32[]{:S(2)}) %collective-permute-start.1) | collective-permute-done | bytes 221216 | tf_op jit(solution)/shard_map/ppermute | solution.py:38
  23.5 0.0 copy-done.3
  23.5 0.0 copy-start.2
  23.5 1.2 %copy-done.2 = bf16[1152,384]{1,0:T(8,128)(2,1)S(1)} copy-done((bf16[1152,384]{1,0:T(8,128)(2,1)S(1)}, bf16[1152,384]{1,0:T(8,128)(2,1)}, u32[]{:S(2)}) %copy-start.2) | copy-done | bytes 884760
  24.7 21.1 %shard_map.129 = (bf16[2,3,12,4,384]{4,3,2,1,0:T(4,128)(2,1)S(1)}, bf16[2,3,12,4,384]{4,3,2,1,0:T(4,128)(2,1)S(1)}, bf16[8,128,384]{2,1,0:T(8,128)(2,1)S(1)}, bf16[8,128,384]{2,1,0:T(8,128)(2,1)S(1)}) custom-call(s32[4]{0:T(128)S(1)} %pad_add_fusion.scal_ref, bf16[6,12,4,384]{3,2,1,0:T(4,128)(2,1)S(1)} %bitcast.34, bf16[6,12,4,384]{3,2,1,0:T(4,128)(2,1)S(1)} %bitcast.37, ...), custom_call_target="tpu_custom_call" | custom-call | flops 2000000000 | bytes 10000000 | tf_op jit(solution)/shard_map/pallas_call | solution.py:324
  45.8 1.4 %collective-permute-start.3 = (bf16[8,128,384]{2,1,0:T(8,128)(2,1)S(1)}, bf16[8,128,384]{2,1,0:T(8,128)(2,1)S(1)}, u32[]{:S(2)}, u32[]{:S(2)}) collective-permute-start(bf16[8,128,384]{2,1,0:T(8,128)(2,1)S(1)} %get-tuple-element.18), channel_id=1, source_target_pairs={{0,1},{1,0},{2,3},{3,2},{4,5},{5,4},{6,7},{7,6},{8,9},{9,8},{10,11... | collective-permute-start | bytes 2359304 | tf_op jit(solution)/shard_map/ppermute | solution.py:371
  47.2 1.9 %collective-permute-done.3 = bf16[8,128,384]{2,1,0:T(8,128)(2,1)S(1)} collective-permute-done((bf16[8,128,384]{2,1,0:T(8,128)(2,1)S(1)}, bf16[8,128,384]{2,1,0:T(8,128)(2,1)S(1)}, u32[]{:S(2)}, u32[]{:S(2)}) %collective-permute-start.3) | collective-permute-done | bytes 786464 | tf_op jit(solution)/shard_map/ppermute | solution.py:371
  49.1 1.1 %add_convert_fusion = bf16[8,128,384]{2,1,0:T(8,128)(2,1)} fusion(bf16[8,128,384]{2,1,0:T(8,128)(2,1)S(1)} %collective-permute-done.3, bf16[8,128,384]{2,1,0:T(8,128)(2,1)S(1)} %get-tuple-element.17), kind=kLoop, calls=%fused_computation.1 | loop fusion | flops 1572864 | bytes 2359296 | tf_op jit(solution)/shard_map/convert_element_type | solution.py:373
  50.1 5.3 %all-to-all-start = ((bf16[8,128,384]{2,1,0:T(8,128)(2,1)}), bf16[8,128,384]{2,1,0:T(8,128)(2,1)S(1)}, u32[]{:S(2)}, u32[]{:S(2)}) async-start(bf16[8,128,384]{2,1,0:T(8,128)(2,1)} %add_convert_fusion), calls=%async_computation | async-start | bytes 1572864 | tf_op jit(solution)/shard_map/all_to_all | solution.py:375
  55.4 0.0 collective-permute-start.2
  55.4 13.4 %collective-permute-done.2 = bf16[2,3,12,4,384]{4,3,2,1,0:T(4,128)(2,1)S(1)} collective-permute-done((bf16[2,3,12,4,384]{4,3,2,1,0:T(4,128)(2,1)S(1)}, bf16[2,3,12,4,384]{4,3,2,1,0:T(4,128)(2,1)S(1)}, u32[]{:S(2)}, u32[]{:S(2)}) %collective-permute-start.2) | collective-permute-done | bytes 221216 | tf_op jit(solution)/shard_map/ppermute | solution.py:38
  68.8 0.3 pad_maximum_fusion
  69.1 0.0 all-to-all-done
  69.1 0.1 convert_reduce_fusion
  69.3 0.7 pad_maximum_fusion.3
  70.0 10.1 %all-to-all-start.1 = ((bf16[16,8,384]{2,1,0:T(8,128)(2,1)}), bf16[16,8,384]{2,1,0:T(8,128)(2,1)S(1)}, u32[]{:S(2)}, u32[]{:S(2)}) async-start(bf16[16,8,384]{2,1,0:T(8,128)(2,1)} %pad_maximum_fusion.3), calls=%async_computation.1 | async-start | bytes 196608 | tf_op jit(solution)/shard_map/all_to_all | solution.py:386
  80.2 0.2 fusion.3
  80.3 0.1 collective-permute-start.4
  80.4 0.7 copy.17
  81.1 8.9 %all-to-all-done.1 = bf16[16,8,384]{2,1,0:T(8,128)(2,1)S(1)} async-done(((bf16[16,8,384]{2,1,0:T(8,128)(2,1)}), bf16[16,8,384]{2,1,0:T(8,128)(2,1)S(1)}, u32[]{:S(2)}, u32[]{:S(2)}) %all-to-all-start.1) | async-done | bytes 98336 | tf_op jit(solution)/shard_map/all_to_all | solution.py:386
  90.0 0.0 copy-start.5
  90.0 0.6 slice.85
  90.6 0.0 collective-permute-done.4
  90.6 0.3 maximum_bitcast_fusion
  90.9 0.9 slice_bitcast_fusion
  91.8 0.0 copy-done.5
  (14 shorter events, 0.2 us)
Async XLA Ops:
  1.5 16.1 %copy-start = (bf16[4,6,12,384]{3,0,2,1:T(4,128)(2,1)S(1)}, bf16[4,6,12,384]{3,0,2,1:T(4,128)(2,1)}, u32[]{:S(2)}) copy-start(bf16[4,6,12,384]{3,0,2,1:T(4,128)(2,1)} %param.9) | copy-start | bytes 663556
  1.5 16.1 %copy-start.1 = (bf16[4,6,12,384]{3,0,2,1:T(4,128)(2,1)S(1)}, bf16[4,6,12,384]{3,0,2,1:T(4,128)(2,1)}, u32[]{:S(2)}) copy-start(bf16[4,6,12,384]{3,0,2,1:T(4,128)(2,1)} %param.10) | copy-start | bytes 663556
  2.7 14.9 %collective-permute-start = (bf16[2,3,12,4,384]{4,3,2,1,0:T(4,128)(2,1)S(1)}, bf16[2,3,12,4,384]{4,3,2,1,0:T(4,128)(2,1)S(1)}, u32[]{:S(2)}, u32[]{:S(2)}) collective-permute-start(bf16[2,3,12,4,384]{4,3,2,1,0:T(4,128)(2,1)S(1)} %pad_maximum_fusion.1), channel_id=1, source_target_pairs={{0,240},{16,0},{32,16},{48,32},{64,48},{80,64},{96,80},{112,96},{1... | collective-permute-start | bytes 663560 | tf_op jit(solution)/shard_map/ppermute | solution.py:38
  13.4 5.7 %copy-start.4 = (s32[144,144]{1,0:T(8,128)S(1)}, s32[144,144]{1,0:T(8,128)}, u32[]{:S(2)}) copy-start(s32[144,144]{1,0:T(8,128)} %param.17) | copy-start | bytes 248836
  13.4 5.7 %copy-start.6 = (bf16[384]{0:T(512)(128)(2,1)S(1)}, bf16[384]{0:T(512)(128)(2,1)}, u32[]{:S(2)}) copy-start(bf16[384]{0:T(512)(128)(2,1)} %param.12) | copy-start | bytes 2308
  13.4 5.7 %copy-start.7 = (bf16[384]{0:T(512)(128)(2,1)S(1)}, bf16[384]{0:T(512)(128)(2,1)}, u32[]{:S(2)}) copy-start(bf16[384]{0:T(512)(128)(2,1)} %param.13) | copy-start | bytes 2308
  13.4 5.8 %slice-start = ((s32[144,144]{1,0:T(8,128)}), s32[144,16]{1,0:T(8,128)S(1)}, s32[]{:S(2)}) async-start(s32[144,144]{1,0:T(8,128)} %param.17), calls=%async_computation.2 | async-start | bytes 147456 | tf_op jit(solution)/shard_map/slice | solution.py:367
  13.4 5.8 %copy-start.8 = (s32[2,1,1]{0,2,1:T(1,128)S(1)}, s32[2,1,1]{0,2,1:T(1,128)}, u32[]{:S(2)}) copy-start(s32[2,1,1]{0,2,1:T(1,128)} %param.11) | copy-start | bytes 28
  13.5 10.1 %copy-start.3 = (bf16[384,384]{1,0:T(8,128)(2,1)S(1)}, bf16[384,384]{1,0:T(8,128)(2,1)}, u32[]{:S(2)}) copy-start(bf16[384,384]{1,0:T(8,128)(2,1)} %wout_ref.1) | copy-start | bytes 884740
  17.9 5.6 %collective-permute-start.1 = (bf16[2,6,6,4,384]{4,3,2,1,0:T(4,128)(2,1)S(1)}, bf16[2,6,6,4,384]{4,3,2,1,0:T(4,128)(2,1)S(1)}, u32[]{:S(2)}, u32[]{:S(2)}) collective-permute-start(bf16[2,6,6,4,384]{4,3,2,1,0:T(4,128)(2,1)S(1)} %pad_maximum_fusion.2), channel_id=1, source_target_pairs={{0,15},{1,0},{2,1},{3,2},{4,3},{5,4},{6,5},{7,6},{8,7},{9,8},{10,9... | collective-permute-start | bytes 663560 | tf_op jit(solution)/shard_map/ppermute | solution.py:38
  23.5 1.2 %copy-start.2 = (bf16[1152,384]{1,0:T(8,128)(2,1)S(1)}, bf16[1152,384]{1,0:T(8,128)(2,1)}, u32[]{:S(2)}) copy-start(bf16[1152,384]{1,0:T(8,128)(2,1)} %wqkv_ref.1) | copy-start | bytes 2654212
  45.8 3.3 %collective-permute-start.3 = (bf16[8,128,384]{2,1,0:T(8,128)(2,1)S(1)}, bf16[8,128,384]{2,1,0:T(8,128)(2,1)S(1)}, u32[]{:S(2)}, u32[]{:S(2)}) collective-permute-start(bf16[8,128,384]{2,1,0:T(8,128)(2,1)S(1)} %get-tuple-element.18), channel_id=1, source_target_pairs={{0,1},{1,0},{2,3},{3,2},{4,5},{5,4},{6,7},{7,6},{8,9},{9,8},{10,11... | collective-permute-start | bytes 2359304 | tf_op jit(solution)/shard_map/ppermute | solution.py:371
  50.1 18.9 %all-to-all-start = ((bf16[8,128,384]{2,1,0:T(8,128)(2,1)}), bf16[8,128,384]{2,1,0:T(8,128)(2,1)S(1)}, u32[]{:S(2)}, u32[]{:S(2)}) async-start(bf16[8,128,384]{2,1,0:T(8,128)(2,1)} %add_convert_fusion), calls=%async_computation | async-start | bytes 1572864 | tf_op jit(solution)/shard_map/all_to_all | solution.py:375
  55.4 13.4 %collective-permute-start.2 = (bf16[2,3,12,4,384]{4,3,2,1,0:T(4,128)(2,1)S(1)}, bf16[2,3,12,4,384]{4,3,2,1,0:T(4,128)(2,1)S(1)}, u32[]{:S(2)}, u32[]{:S(2)}) collective-permute-start(bf16[2,3,12,4,384]{4,3,2,1,0:T(4,128)(2,1)S(1)} %get-tuple-element.15), channel_id=1, source_target_pairs={{0,16},{16,32},{32,48},{48,64},{64,80},{80,96},{96,112},{112,128},... | collective-permute-start | bytes 663560 | tf_op jit(solution)/shard_map/ppermute | solution.py:38
  70.0 19.9 %all-to-all-start.1 = ((bf16[16,8,384]{2,1,0:T(8,128)(2,1)}), bf16[16,8,384]{2,1,0:T(8,128)(2,1)S(1)}, u32[]{:S(2)}, u32[]{:S(2)}) async-start(bf16[16,8,384]{2,1,0:T(8,128)(2,1)} %pad_maximum_fusion.3), calls=%async_computation.1 | async-start | bytes 196608 | tf_op jit(solution)/shard_map/all_to_all | solution.py:386
  80.3 10.2 %collective-permute-start.4 = (bf16[2,6,6,4,384]{4,3,2,1,0:T(4,128)(2,1)S(1)}, bf16[2,6,6,4,384]{4,3,2,1,0:T(4,128)(2,1)S(1)}, u32[]{:S(2)}, u32[]{:S(2)}) collective-permute-start(bf16[2,6,6,4,384]{4,3,2,1,0:T(4,128)(2,1)S(1)} %get-tuple-element.28), channel_id=1, source_target_pairs={{0,1},{1,2},{2,3},{3,4},{4,5},{5,6},{6,7},{7,8},{8,9},{9,10},{10,1... | collective-permute-start | bytes 663560 | tf_op jit(solution)/shard_map/ppermute | solution.py:38
  90.0 1.8 %copy-start.5 = (f32[8,384]{1,0:T(8,128)}, f32[8,384]{1,0:T(8,128)S(1)}, u32[]{:S(2)}) copy-start(f32[8,384]{1,0:T(8,128)S(1)} %convert_reduce_fusion.1) | copy-start | bytes 36868

commit v3 on v2

v3 whole, which is shorter than its diff:
```python
import functools

import jax
import jax.numpy as jnp
from jax import lax
from jax.experimental import pallas as pl
from jax.experimental.pallas import tpu as pltpu
from jax.sharding import PartitionSpec as P

HEADS = 12
HEAD_DIM = 32
WIN_TOK = 144
NBIAS = 759
D = 384
TOK = 288
EPS = 1e-05
BLOCKED = -10000.0
MARK = 256.0
LANES = 128
LOG2E = 1.4426950408889634
QSLOTS = 8
CHUNK = 56

wide = jnp.float32
low = jnp.bfloat16

NN = (((1,), (0,)), ((), ()))
NT = (((1,), (1,)), ((), ()))
TN = (((0,), (0,)), ((), ()))


def mm(a, b, dims):
    return lax.dot_general(a, b, dims, preferred_element_type=wide)


def passed_along(value, axis, steps):
    count = lax.axis_size(axis)
    pairs = [(source, (source + steps) % count) for source in range(count)]
    return lax.ppermute(value, axis, pairs)


def pre_kernel(scal_ref, table_ref, ids_ref, bias_ref, order_ref, tail_ref, far_ref):
    new = lax.broadcasted_iota(jnp.int32, (D, D), 0)
    old = lax.broadcasted_iota(jnp.int32, (D, D), 1)
    tens = new // 6
    r = new - 6 * tens
    zl = tens & 1
    xh = (tens >> 1) & 1
    j = (tens >> 2) & 7
    other = tens >> 5
    core = scal_ref[3]
    c = core + other - 2 * core * other
    order_ref[...] = (old == ((2 * zl + xh) * 16 + 2 * j + c) * 6 + r).astype(wide).astype(low)

    tail_ref[...] = jnp.zeros((WIN_TOK, LANES), jnp.int32)
    tail_ref[:, 0:16] = ids_ref[:, LANES:WIN_TOK]
    for head in range(HEADS):
        for p in range(6):
            stop = min((p + 1) * LANES, NBIAS)
            far_ref[head * 6 + p : head * 6 + p + 1, 0 : stop - p * LANES] = (
                table_ref[head, :, p * LANES : stop] * LOG2E
            )

    def rows(step, _):
        at = pl.ds(pl.multiple_of(step * 8, 8), 8)
        for half in range(2):
            ids = ids_ref[at, 0:LANES] if half == 0 else tail_ref[at, :]
            place = ids & (LANES - 1)
            piece = ids >> 7
            picks = [piece == p for p in range(6)]
            for head in range(HEADS):
                got = None
                for p in range(6):
                    source = jnp.broadcast_to(
                        far_ref[head * 6 + p : head * 6 + p + 1, :], (8, LANES)
                    )
                    found = jnp.take_along_axis(source, place, axis=1)
                    got = found if got is None else jnp.where(picks[p], found, got)
                bias_ref[head, at, half * LANES : (half + 1) * LANES] = got
        return 0

    lax.fori_loop(0, WIN_TOK // 8, rows, 0)


def main_kernel(
    scal_ref,
    fields_ref,
    cot_ref,
    lat_ref,
    lon_ref,
    token_ref,
    gain_ref,
    wqkv_ref,
    wout_ref,
    bias_in_ref,
    order_ref,
    out_own_ref,
    out_lat_ref,
    keep_ref,
    give_ref,
    bg_ref,
    bt_ref,
    x_ref,
    c_ref,
    std_ref,
    qkv_ref,
    gm_ref,
    qt_ref,
    gmt_ref,
    mixed_ref,
    gq_ref,
    gkt_ref,
    gvt_ref,
    bias_ref,
    bias_sem,
    mix_ref,
):
    bias_copy = pltpu.make_async_copy(bias_in_ref, bias_ref, bias_sem)
    bias_copy.start()
    level = lax.broadcasted_iota(jnp.int32, (4, 1), 0)
    own_masked = jnp.where(level < 2, scal_ref[0], scal_ref[1]) == 1
    for which, own, dest in ((0, fields_ref, x_ref), (1, cot_ref, c_ref)):
        for a in range(6):
            for o in range(12):
                if o >= 6:
                    piece = lon_ref[which, a, o - 6]
                elif a >= 3:
                    piece = lat_ref[which, a - 3, 6 + o]
                else:
                    piece = own[3 + a, 6 + o]
                piece = piece.astype(wide)
                if which == 0 and o < 6 and a < 3:
                    piece = jnp.where(own_masked, MARK, piece)
                base = (a * 12 + o) * 4
                for c in range(3):
                    mix_ref[c, base : base + 4, :] = piece[:, c * LANES : (c + 1) * LANES]
        for zs in range(4):
            for c in range(3):
                dest[zs * 72 : (zs + 1) * 72, c * LANES : (c + 1) * LANES] = mix_ref[
                    c, pl.ds((zs + 1) % 4, 72, stride=4), :
                ]
    raw = x_ref[...]
    masked = raw > 0.5 * MARK
    filled = jnp.where(masked, token_ref[...], raw)
    x_ref[...] = filled
    gain = gain_ref[...]
    center = filled - jnp.mean(filled, axis=-1, keepdims=True)
    inv_std = lax.rsqrt(jnp.mean(center * center, axis=-1, keepdims=True) + EPS)
    standard = center * inv_std
    std_ref[...] = standard
    normed = (standard * gain).astype(low)
    cot = c_ref[...].astype(low)

    qkv_ref[...] = mm(normed, wqkv_ref[...], NT).astype(low)
    gm_ref[...] = mm(cot, wout_ref[...], NN).astype(low)
    for w in range(2):
        rows = slice(w * WIN_TOK, (w + 1) * WIN_TOK)
        qt_ref[w] = mm(wqkv_ref[0:D, :], normed[rows], NT).astype(low)
        gmt_ref[w] = mm(wout_ref[...], cot[rows], (((0,), (1,)), ((), ()))).astype(low)

    last = scal_ref[2] == 1
    ti = lax.broadcasted_iota(jnp.int32, (WIN_TOK, WIN_TOK), 0)
    tj = lax.broadcasted_iota(jnp.int32, (WIN_TOK, WIN_TOK), 1)
    zi = (ti >= 72).astype(jnp.int32)
    zj = (tj >= 72).astype(jnp.int32)
    ai = (ti - 72 * zi >= 36).astype(jnp.int32)
    aj = (tj - 72 * zj >= 36).astype(jnp.int32)
    lat_apart = jnp.where(last, (ai != aj).astype(wide), 0.0)
    lev_apart = (zi != zj).astype(wide)
    apart = (lat_apart > 0.0, lat_apart + lev_apart > 0.0)
    lane = lax.broadcasted_iota(jnp.int32, (1, LANES), 1) // HEAD_DIM
    scale = HEAD_DIM ** (-0.5)
    masks = [(lane == sub).astype(low) for sub in range(4)]
    bias_copy.wait()
    for group in range(3):
        cols = slice(group * LANES, (group + 1) * LANES)
        kcols = slice(D + group * LANES, D + (group + 1) * LANES)
        vcols = slice(2 * D + group * LANES, 2 * D + (group + 1) * LANES)
        totals = [None] * 4
        for w in range(2):
            rows = slice(w * WIN_TOK, (w + 1) * WIN_TOK)
            q = qkv_ref[rows, cols]
            k = qkv_ref[rows, kcols]
            v = qkv_ref[rows, vcols]
            g = gm_ref[rows, cols]
            raw_scores = mm(jnp.concatenate([q * mask for mask in masks], axis=0), k, NT)
            raw_grads = mm(jnp.concatenate([g * mask for mask in masks], axis=0), v, NT)
            g_wide = g.astype(wide)
            mixed_sum = None
            gq_sum = None
            for sub in range(4):
                head = group * 4 + sub
                feats = slice(head * HEAD_DIM, (head + 1) * HEAD_DIM)
                part = slice(sub * WIN_TOK, (sub + 1) * WIN_TOK)
                scores = raw_scores[part] * (scale * LOG2E) + bias_ref[head, :, 0:WIN_TOK]
                scores = jnp.where(apart[w], BLOCKED * LOG2E, scores)
                top = jnp.max(scores, axis=-1, keepdims=True)
                expo = jnp.exp2(scores - top)
                prob = (expo * (1.0 / jnp.sum(expo, axis=-1, keepdims=True))).astype(low)
                mixed = mm(prob, v * masks[sub], NN)
                gvt_ref[w, feats, :] = mm(gmt_ref[w, feats, :], prob, NN).astype(low)
                delta = jnp.sum(g_wide * mixed, axis=-1, keepdims=True)
                grad = prob.astype(wide) * (raw_grads[part] - delta)
                glow = grad.astype(low)
                gq = mm(glow, k * masks[sub], NN)
                gkt_ref[w, feats, :] = (mm(qt_ref[w, feats, :], glow, NN) * scale).astype(low)
                mixed_sum = mixed if sub == 0 else mixed_sum + mixed
                gq_sum = gq if sub == 0 else gq_sum + gq
                if w == 0:
                    totals[sub] = grad
                else:
                    total = totals[sub] + grad
                    bg_ref[head] = total[:, 0:LANES]
                    bt_ref[head, :, 0:16] = total[:, LANES:WIN_TOK]
            mixed_ref[rows, cols] = mixed_sum.astype(low)
            gq_ref[rows, cols] = (gq_sum * scale).astype(low)

    def put_back(which, value):
        for zs in range(4):
            for c in range(3):
                mix_ref[c, pl.ds((zs + 1) % 4, 72, stride=4), :] = value[
                    zs * 72 : (zs + 1) * 72, c * LANES : (c + 1) * LANES
                ]
        for a in range(6):
            for o in range(12):
                base = (a * 12 + o) * 4
                piece = jnp.concatenate([mix_ref[c, base : base + 4, :] for c in range(3)], axis=1)
                if a < 3:
                    out_own_ref[which, a, o] = piece.astype(low)
                else:
                    out_lat_ref[which, a - 3, o] = piece.astype(low)

    mixed = mixed_ref[...]
    branch = mm(mixed, wout_ref[...], NT).astype(low).astype(wide)
    put_back(0, x_ref[...] + branch)

    gq = gq_ref[...]
    gk = jnp.concatenate([gkt_ref[w].T for w in range(2)], axis=0)
    gv = jnp.concatenate([gvt_ref[w].T for w in range(2)], axis=0)
    grad_normed = (
        mm(gq, wqkv_ref[0:D, :], NN)
        + mm(gk, wqkv_ref[D : 2 * D, :], NN)
        + mm(gv, wqkv_ref[2 * D : 3 * D, :], NN)
    )
    grad_normed = grad_normed.astype(low).astype(wide)
    standard = std_ref[...]
    scaled = grad_normed * gain
    inner = (
        scaled
        - jnp.mean(scaled, axis=-1, keepdims=True)
        - standard * jnp.mean(scaled * standard, axis=-1, keepdims=True)
    )
    grad_filled = c_ref[...] + inv_std * inner
    put_back(1, jnp.where(masked, 0.0, grad_filled))
    gain_grad = jnp.sum(grad_normed * standard, axis=0, keepdims=True)
    token_grad = jnp.sum(jnp.where(masked, grad_filled, 0.0), axis=0, keepdims=True)

    order = order_ref[...]
    parts = []
    for value in (gq, gk, gv, cot):
        turned = mm(order, value, NT).astype(low)
        other = mixed if value is cot else normed
        parts.append(mm(turned, other, NN))
    vectors = jnp.concatenate([gain_grad, token_grad, jnp.zeros((6, D), wide)], axis=0)
    for n in range(32):
        rows = slice(n * 12, (n + 1) * 12)
        chunk = jnp.concatenate([part[rows] for part in parts] + [vectors], axis=0)
        dest = keep_ref if n < 16 else give_ref
        dest[n % 16] = chunk.astype(low)


def table_kernel(bg_ref, bt_ref, ids_ref, sums_ref, rem_ref, near_ref, tail_ref, rest_ref):
    slot = lax.broadcasted_iota(jnp.int32, (QSLOTS, LANES), 0)
    spot = lax.broadcasted_iota(jnp.int32, (LANES, LANES), 0)
    near_ref[...] = ids_ref[:, 0:LANES]
    tail_ref[:, 0:16] = ids_ref[:, LANES:WIN_TOK]
    rest_ref[...] = jnp.concatenate(
        [tail_ref[pl.ds(k, 18, stride=8), :][:, 0:16] for k in range(8)], axis=1
    )
    for head in range(HEADS):
        rem_ref[head] = jnp.concatenate(
            [bt_ref[head, pl.ds(k, 18, stride=8), :][:, 0:16] for k in range(8)], axis=1
        )

    def one_step(step, acc):
        lefts = []
        rights = []
        for s in range(9):
            if s < 8:
                ids = near_ref[pl.ds(step * 8 + s, 1), :]
                vals = [bg_ref[head, pl.ds(step * 8 + s, 1), :] for head in range(HEADS)]
            else:
                ids = rest_ref[pl.ds(step, 1), :]
                vals = [rem_ref[head, pl.ds(step, 1), :] for head in range(HEADS)]
            rights.append(((ids & (LANES - 1)) == spot).astype(wide).astype(low))
            here = (ids >> 7) == slot
            lefts.append(
                jnp.concatenate([jnp.where(here, val, 0.0) for val in vals], axis=0).astype(low)
            )
        left = jnp.concatenate(lefts, axis=1)
        right = jnp.concatenate(rights, axis=1)
        return acc + mm(left, right, NT)

    start = jnp.zeros((HEADS * QSLOTS, LANES), wide)
    sums_ref[...] = lax.fori_loop(0, 18, one_step, start, unroll=6)


def pack_kernel(keep_ref, taken_ref, table_ref, send_ref):
    total = keep_ref[0].astype(wide) + taken_ref[0].astype(wide)
    table = table_ref[...]
    row = lax.broadcasted_iota(jnp.int32, (HEADS * QSLOTS, 1), 0)
    for n in range(2):
        for p in range(3):
            piece = total[48 + n : 49 + n, p * LANES : (p + 1) * LANES]
            table = jnp.where(row == QSLOTS * p + 6 + n, piece, table)
    extra = jnp.concatenate([table[0:32], table[32:64], table[64:96]], axis=1).astype(low)
    for m in range(16):
        total = keep_ref[m].astype(wide) + taken_ref[m].astype(wide)
        send_ref[m, 0:48, :] = total[0:48].astype(low)
        send_ref[m, 48:80, :] = extra


def sum_kernel(scal_ref, got_ref, second_ref, table_ref):
    weights = got_ref[0, 0:48, :].astype(wide)
    for m in range(1, 16):
        weights = weights + got_ref[m, 0:48, :].astype(wide)
    sides = []
    for xh in range(2):
        side = got_ref[xh, 48:80, :].astype(wide)
        for j in range(1, 8):
            side = side + got_ref[2 * j + xh, 48:80, :].astype(wide)
        sides.append(side)
    table_ref[...] = jnp.where(scal_ref[4] == 0, sides[0], sides[1])
    both = sides[0] + sides[1]
    vectors = jnp.concatenate(
        [both[QSLOTS * p + 6 : QSLOTS * p + 8, 0:LANES] for p in range(3)], axis=1
    )
    for z in range(8):
        chunk = jnp.concatenate([weights[6 * z : 6 * z + 6], vectors], axis=0)
        second_ref[z] = chunk.astype(low)


def local(
    fields,
    cotangent,
    window_mask,
    mask_token,
    norm_gain,
    qkv_weight,
    out_weight,
    bias_table,
    bias_index,
):
    own_mask = window_mask[:, 0, 0]
    last = lax.axis_index("lat") == lax.axis_size("lat") - 1
    core = lax.axis_index("lon") % 2
    side = lax.axis_index("lat") % 2
    scalars = jnp.concatenate([own_mask, jnp.stack([last.astype(jnp.int32), core, side])])
    fields = fields.transpose(1, 2, 0, 3)
    cotangent = cotangent.transpose(1, 2, 0, 3)
    hidden = jnp.repeat(own_mask, 2)[:, None] == 1
    strip = jnp.stack((jnp.where(hidden, jnp.bfloat16(MARK), fields[:3]), cotangent[:3]))
    lat_in = passed_along(strip, "lat", -1)

    smem = pl.BlockSpec(memory_space=pltpu.SMEM)
    vmem = pl.BlockSpec(memory_space=pltpu.VMEM)
    bias, order = pl.pallas_call(
        pre_kernel,
        out_shape=(
            jax.ShapeDtypeStruct((HEADS, WIN_TOK, 256), wide),
            jax.ShapeDtypeStruct((D, D), low),
        ),
        in_specs=[smem, vmem, vmem],
        out_specs=(vmem,) * 2,
        scratch_shapes=[
            pltpu.VMEM((WIN_TOK, LANES), jnp.int32),
            pltpu.VMEM((HEADS * 6, LANES), wide),
        ],
        compiler_params=pltpu.CompilerParams(vmem_limit_bytes=8 * 2**20),
        cost_estimate=pl.CostEstimate(flops=10**7, bytes_accessed=6 * 10**6, transcendentals=0),
    )(scalars, bias_table.transpose(1, 0, 2), bias_index)
    lat_in, bias, order = lax.optimization_barrier((lat_in, bias, order))
    own = jnp.stack((jnp.where(hidden, jnp.bfloat16(MARK), fields[3:, :6]), cotangent[3:, :6]))
    lon_in = passed_along(jnp.concatenate((own, lat_in[:, :, :6]), axis=1), "lon", -1)

    out_own, out_lat, keep, give, bias_grad, bias_tail = pl.pallas_call(
        main_kernel,
        out_shape=(
            jax.ShapeDtypeStruct((2, 3, 12, 4, D), low),
            jax.ShapeDtypeStruct((2, 3, 12, 4, D), low),
            jax.ShapeDtypeStruct((16, CHUNK, D), low),
            jax.ShapeDtypeStruct((16, CHUNK, D), low),
            jax.ShapeDtypeStruct((HEADS, WIN_TOK, LANES), wide),
            jax.ShapeDtypeStruct((HEADS, WIN_TOK, LANES), wide),
        ),
        in_specs=[smem] + [vmem] * 8 + [pl.BlockSpec(memory_space=pl.ANY), vmem],
        out_specs=(vmem,) * 6,
        scratch_shapes=[
            pltpu.VMEM((TOK, D), wide),
            pltpu.VMEM((TOK, D), wide),
            pltpu.VMEM((TOK, D), wide),
            pltpu.VMEM((TOK, 3 * D), low),
            pltpu.VMEM((TOK, D), low),
            pltpu.VMEM((2, D, WIN_TOK), low),
            pltpu.VMEM((2, D, WIN_TOK), low),
            pltpu.VMEM((TOK, D), low),
            pltpu.VMEM((TOK, D), low),
            pltpu.VMEM((2, D, WIN_TOK), low),
            pltpu.VMEM((2, D, WIN_TOK), low),
            pltpu.VMEM((HEADS, WIN_TOK, 256), wide),
            pltpu.SemaphoreType.DMA(()),
            pltpu.VMEM((3, TOK, LANES), wide),
        ],
        compiler_params=pltpu.CompilerParams(vmem_limit_bytes=24 * 2**20),
        cost_estimate=pl.CostEstimate(
            flops=2 * 10**9, bytes_accessed=10**7, transcendentals=5 * 10**5
        ),
    )(
        scalars,
        fields,
        cotangent,
        lat_in,
        lon_in,
        mask_token.astype(wide)[None],
        norm_gain.astype(wide)[None],
        qkv_weight,
        out_weight,
        bias,
        order,
    )

    size = lax.axis_size("lon")
    bands = lax.axis_size("lat")

    def swapped(value, bit):
        return lax.ppermute(value, "lon", [(i, i ^ bit) for i in range(size)])

    taken = swapped(give, 1)
    lat_out = passed_along(out_lat, "lat", 1)
    table = pl.pallas_call(
        table_kernel,
        out_shape=jax.ShapeDtypeStruct((HEADS * QSLOTS, LANES), wide),
        in_specs=[vmem] * 3,
        out_specs=vmem,
        scratch_shapes=[
            pltpu.VMEM((HEADS, 18, LANES), wide),
            pltpu.VMEM((WIN_TOK, LANES), jnp.int32),
            pltpu.VMEM((WIN_TOK, LANES), jnp.int32),
            pltpu.VMEM((18, LANES), jnp.int32),
        ],
        compiler_params=pltpu.CompilerParams(vmem_limit_bytes=8 * 2**20),
        cost_estimate=pl.CostEstimate(flops=10**9, bytes_accessed=10**6, transcendentals=0),
    )(bias_grad, bias_tail, bias_index)
    pair = pl.pallas_call(
        pack_kernel,
        out_shape=jax.ShapeDtypeStruct((16, 80, D), low),
        in_specs=[vmem] * 3,
        out_specs=vmem,
        compiler_params=pltpu.CompilerParams(vmem_limit_bytes=8 * 2**20),
        cost_estimate=pl.CostEstimate(flops=10**6, bytes_accessed=10**6, transcendentals=0),
    )(keep, taken, table)
    groups = [
        [(2 * z + xh) * size + 2 * j + c for j in range(size // 2) for xh in range(2)]
        for z in range(bands // 2)
        for c in range(2)
    ]
    got = lax.all_to_all(pair, ("lat", "lon"), 0, 0, axis_index_groups=groups, tiled=True)
    second, table = pl.pallas_call(
        sum_kernel,
        out_shape=(
            jax.ShapeDtypeStruct((8, 8, D), low),
            jax.ShapeDtypeStruct((32, D), wide),
        ),
        in_specs=[smem, vmem],
        out_specs=(vmem, vmem),
        compiler_params=pltpu.CompilerParams(vmem_limit_bytes=8 * 2**20),
        cost_estimate=pl.CostEstimate(flops=10**6, bytes_accessed=10**6, transcendentals=0),
    )(scalars, got)

    full = jnp.concatenate((lat_out, out_own), axis=1)
    full, second = lax.optimization_barrier((full, second))
    groups = [[(2 * z + xh) for z in range(bands // 2)] for xh in range(2)]
    final = lax.all_to_all(second, "lat", 0, 0, axis_index_groups=groups, tiled=True)
    lon_out = passed_along(full[:, :, 6:], "lon", 1)
    table = table + swapped(table, 1)
    done = jnp.concatenate((lon_out, full[:, :, :6]), axis=2).transpose(0, 3, 1, 2, 4)
    output, input_grad = done[0], done[1]
    table = table.reshape(32, 3, LANES).transpose(1, 0, 2).reshape(HEADS, QSLOTS, LANES)
    table_grad = table[:, :6].reshape(1, HEADS, 6 * LANES)
    table_grad = table_grad[:, :, :NBIAS]
    final, output, input_grad, table_grad = lax.optimization_barrier(
        (final, output, input_grad, table_grad)
    )
    weight_grads = jnp.sum(final[:, :6].astype(wide), axis=0)
    vector_grads = jnp.sum(final[:, 6:].astype(wide), axis=0)
    return (output, input_grad, weight_grads, table_grad, vector_grads)


def solution(mesh):
    placed = (
        P(None, "lat", "lon", None),
        P(None, "lat", "lon", None),
        P(None, "lat", "lon"),
        P(),
        P(),
        P(),
        P(),
        P("lat", None, None),
        P(),
    )
    return jax.shard_map(
        local,
        mesh=mesh,
        in_specs=placed,
        out_specs=(
            P(None, "lat", "lon", None),
            P(None, "lat", "lon", None),
            P(("lat", "lon"), None),
            P("lat", None, None),
            P(),
        ),
        check_vma=False,
    )
```

time: 92.2 us -> 85.4 us (0.926)
  the two profiles are of different devices: /device:TPU:1 before, /device:TPU:2 now
where the time goes in v3:
time: 85.4 us; the launch traced here: 84.5 us
  waiting for transfers between devices  26.4 us (31%)
  starting transfers between devices  24.6 us (29%)
  Pallas kernels  22.1 us (26%)
  other arithmetic  5.63 us (7%)
  local copies, waits for them, and re-layouts  4.84 us (6%)
    ppermute x4, waiting for transfers between devices, passed_along(): return lax.ppermute(value, axis, pairs)  16.7 us
    pallas_call x1, Pallas kernels, local(): pl.pallas_call(main_kernel, out_shape=(jax.ShapeDtypeStruct((2, 3, 12, 4,...  12.3 us
    ppermute x4, starting transfers between devices, passed_along(): return lax.ppermute(value, axis, pairs)  10.3 us
    all_to_all x1, waiting for transfers between devices, local(): lax.all_to_all(second, 'lat', 0, 0, axis_index_groups=groups, tiled=True)  6.9 us
    all_to_all x1, starting transfers between devices, local(): lax.all_to_all(pair, ('lat', 'lon'), 0, 0, axis_index_groups=groups, tile...  6.58 us
    pallas_call x1, Pallas kernels, local(): pl.pallas_call(pre_kernel, out_shape=(jax.ShapeDtypeStruct((HEADS, WIN_TO...  4.86 us
    ppermute x2, starting transfers between devices, swapped(): return lax.ppermute(value, 'lon', [(i, i ^ bit) for i in range(size)])  3.96 us
    all_to_all x1, starting transfers between devices, local(): lax.all_to_all(second, 'lat', 0, 0, axis_index_groups=groups, tiled=True)  3.74 us
  transfers between devices with their start and end apart: 8, of which 4 were waited for; matrix products, arithmetic and copies ran while one was open for 4% of the time, Pallas kernels for 9%

profile of v3, /device:TPU:2, one launch (start us, length us, event | category | flops | bytes accessed | tf_op | source)
XLA Modules:
  0.0 84.5 jit_solution(15960812680185048927)
XLA Ops:
  0.6 0.0 copy-start.3
  0.6 0.0 copy-start.2
  0.7 0.0 copy-start.7
  0.7 0.0 copy-start.8
  0.7 0.0 copy-start.6
  0.7 0.8 broadcast_compare_fusion
  1.5 0.1 broadcast_in_dim.37
  1.5 0.1 eq.19
  1.6 1.1 %slice_bitcast_fusion.2 = (bf16[1,3,12,4,384]{4,3,2,1,0:T(4,128)(2,1)S(1)}, bf16[1,3,12,4,384]{4,3,2,1,0:T(4,128)(2,1)S(1)}) fusion(bf16[6,12,4,384]{3,2,1,0:T(4,128)(2,1)} %bitcast.29, bf16[6,12,4,384]{3,2,1,0:T(4,128)(2,1)} %bitcast.26, pred[4]{0:T(512)(128)(4,1)S(1)} %eq.19), kind=kLoop, calls=%fused_computation.6 | loop fusion | flops 55296 | bytes 442372 | tf_op jit(solution)/shard_map/stack | solution.py:362
  2.7 0.2 pad_maximum_fusion.1
  2.8 7.5 %collective-permute-start = (bf16[2,3,12,4,384]{4,3,2,1,0:T(4,128)(2,1)S(1)}, bf16[2,3,12,4,384]{4,3,2,1,0:T(4,128)(2,1)S(1)}, u32[]{:S(2)}, u32[]{:S(2)}) collective-permute-start(bf16[2,3,12,4,384]{4,3,2,1,0:T(4,128)(2,1)S(1)} %pad_maximum_fusion.1), channel_id=1, source_target_pairs={{0,240},{16,0},{32,16},{48,32},{64,48},{80,64},{96,80},{112,96},{1... | collective-permute-start | bytes 663560 | tf_op jit(solution)/shard_map/ppermute | solution.py:39
  10.3 0.7 pad_add_fusion.scal_ref
  11.1 0.0 copy-start
  11.1 0.9 %copy-done = s32[144,144]{1,0:T(8,128)S(1)} copy-done((s32[144,144]{1,0:T(8,128)S(1)}, s32[144,144]{1,0:T(8,128)}, u32[]{:S(2)}) %copy-start) | copy-done | bytes 82968
  12.0 0.0 copy-start.4
  12.0 0.8 copy-done.4
  12.8 4.9 %shard_map.128 = (f32[12,144,256]{2,1,0:T(8,128)S(1)}, bf16[384,384]{1,0:T(8,128)(2,1)S(1)}) custom-call(s32[5]{0:T(128)S(1)} %pad_add_fusion.scal_ref, f32[12,1,759]{2,1,0:T(1,128)S(1)} %bitcast.32, s32[144,144]{1,0:T(8,128)S(1)} %copy-done), custom_call_target="tpu_custom_call" | custom-call | flops 10000000 | bytes 6000000 | tf_op jit(solution)/shard_map/pallas_call | solution.py:367
  17.6 0.9 %slice_bitcast_fusion.3 = (bf16[1,3,6,4,384]{4,3,2,1,0:T(4,128)(2,1)S(1)}, bf16[1,3,6,4,384]{4,3,2,1,0:T(4,128)(2,1)S(1)}) fusion(bf16[6,12,4,384]{3,2,1,0:T(4,128)(2,1)} %bitcast.30, bf16[6,12,4,384]{3,2,1,0:T(4,128)(2,1)} %bitcast.27, pred[4]{0:T(512)(128)(4,1)S(1)} %eq.19), kind=kLoop, calls=%fused_computation.10 | loop fusion | flops 27648 | bytes 221188 | tf_op jit(solution)/shard_map/stack | solution.py:383
  18.6 0.0 collective-permute-done.lat_ref
  18.6 0.2 pad_maximum_fusion.2
  18.8 0.7 collective-permute-start.1
  19.5 0.0 copy-done.7
  19.5 0.0 copy-done.8
  19.5 0.0 copy-start.1
  19.5 3.4 %collective-permute-done.1.lon_ref = bf16[2,6,6,4,384]{4,3,2,1,0:T(4,128)(2,1)S(1)} collective-permute-done((bf16[2,6,6,4,384]{4,3,2,1,0:T(4,128)(2,1)S(1)}, bf16[2,6,6,4,384]{4,3,2,1,0:T(4,128)(2,1)S(1)}, u32[]{:S(2)}, u32[]{:S(2)}) %collective-permute-start.1) | collective-permute-done | bytes 221216 | tf_op jit(solution)/shard_map/ppermute | solution.py:39
  22.9 0.0 copy-done.3
  22.9 0.0 copy-done.2
  22.9 0.0 copy-done.6
  22.9 0.0 copy-start.5
  22.9 1.2 %copy-done.5 = bf16[1152,384]{1,0:T(8,128)(2,1)S(1)} copy-done((bf16[1152,384]{1,0:T(8,128)(2,1)S(1)}, bf16[1152,384]{1,0:T(8,128)(2,1)}, u32[]{:S(2)}) %copy-start.5) | copy-done | bytes 884760
  24.1 12.3 %shard_map.129 = (bf16[2,3,12,4,384]{4,3,2,1,0:T(4,128)(2,1)S(1)}, bf16[2,3,12,4,384]{4,3,2,1,0:T(4,128)(2,1)S(1)}, bf16[16,56,384]{2,1,0:T(8,128)(2,1)S(1)}, bf...) custom-call(s32[5]{0:T(128)S(1)} %pad_add_fusion.scal_ref, ...), custom_call_target="tpu_custom_call" | custom-call | flops 2000000000 | bytes 10000000 | tf_op jit(solution)/shard_map/pallas_call | solution.py:386
  36.4 2.4 %collective-permute-start.3 = (bf16[16,56,384]{2,1,0:T(8,128)(2,1)S(1)}, bf16[16,56,384]{2,1,0:T(8,128)(2,1)S(1)}, u32[]{:S(2)}, u32[]{:S(2)}) collective-permute-start(bf16[16,56,384]{2,1,0:T(8,128)(2,1)S(1)} %get-tuple-element.32), channel_id=1, source_target_pairs={{0,1},{1,0},{2,3},{3,2},{4,5},{5,4},{6,7},{7,6},{8,9},{9,8},{10,11... | collective-permute-start | bytes 2064392 | tf_op jit(solution)/shard_map/ppermute | solution.py:436
  38.8 0.0 copy-done.1
  38.8 2.6 %shard_map.130.table_ref = f32[96,128]{1,0:T(8,128)S(1)} custom-call(f32[12,144,128]{2,1,0:T(8,128)S(1)} %get-tuple-element.33.bg_ref, f32[12,144,128]{2,1,0:T(8,128)S(1)} %get-tuple-element.34.bt_ref, s32[144,144]{1,0:T(8,128)S(1)} %copy-done.1), custom_call_target="tpu_custom_call" | custom-call | flops 1000000000 | bytes 1000000 | tf_op jit(solution)/shard_map/pallas_call | solution.py:440
  41.4 0.0 collective-permute-done.3.taken_ref
  41.4 1.1 %shard_map.131 = bf16[16,80,384]{2,1,0:T(8,128)(2,1)} custom-call(bf16[16,56,384]{2,1,0:T(8,128)(2,1)S(1)} %get-tuple-element.31.keep_ref, bf16[16,56,384]{2,1,0:T(8,128)(2,1)S(1)} %collective-permute-done.3.taken_ref, f32[96,128]{1,0:T(8,128)S(1)} %shard_map.130.table_ref), custom_call_target="tpu_custom_call" | custom-call | flops 1000000 | bytes 1000000 | tf_op jit(solution)/shard_map/pallas_call | solution.py:454
  42.6 6.6 %all-to-all-start = ((bf16[16,80,384]{2,1,0:T(8,128)(2,1)}), bf16[16,80,384]{2,1,0:T(8,128)(2,1)S(1)}, u32[]{:S(2)}, u32[]{:S(2)}) async-start(bf16[16,80,384]{2,1,0:T(8,128)(2,1)} %shard_map.131), calls=%async_computation | async-start | bytes 1966080 | tf_op jit(solution)/shard_map/all_to_all | solution.py:467
  49.1 2.1 %collective-permute-start.2 = (bf16[2,3,12,4,384]{4,3,2,1,0:T(4,128)(2,1)S(1)}, bf16[2,3,12,4,384]{4,3,2,1,0:T(4,128)(2,1)S(1)}, u32[]{:S(2)}, u32[]{:S(2)}) collective-permute-start(bf16[2,3,12,4,384]{4,3,2,1,0:T(4,128)(2,1)S(1)} %get-tuple-element.29), channel_id=1, source_target_pairs={{0,16},{16,32},{32,48},{48,64},{64,80},{80,96},{96,112},{112,128},... | collective-permute-start | bytes 663560 | tf_op jit(solution)/shard_map/ppermute | solution.py:39
  51.2 13.3 %collective-permute-done.2 = bf16[2,3,12,4,384]{4,3,2,1,0:T(4,128)(2,1)S(1)} collective-permute-done((bf16[2,3,12,4,384]{4,3,2,1,0:T(4,128)(2,1)S(1)}, bf16[2,3,12,4,384]{4,3,2,1,0:T(4,128)(2,1)S(1)}, u32[]{:S(2)}, u32[]{:S(2)}) %collective-permute-start.2) | collective-permute-done | bytes 221216 | tf_op jit(solution)/shard_map/ppermute | solution.py:39
  64.5 0.3 pad_maximum_fusion
  64.8 2.8 %all-to-all-done.got_ref = bf16[16,80,384]{2,1,0:T(8,128)(2,1)S(1)} async-done(((bf16[16,80,384]{2,1,0:T(8,128)(2,1)}), bf16[16,80,384]{2,1,0:T(8,128)(2,1)S(1)}, u32[]{:S(2)}, u32[]{:S(2)}) %all-to-all-start) | async-done | bytes 983072 | tf_op jit(solution)/shard_map/all_to_all | solution.py:467
  67.6 1.3 %shard_map.132 = (bf16[8,8,384]{2,1,0:T(8,128)(2,1)}, f32[32,384]{1,0:T(8,128)S(1)}) custom-call(s32[5]{0:T(128)S(1)} %pad_add_fusion.scal_ref, bf16[16,80,384]{2,1,0:T(8,128)(2,1)S(1)} %all-to-all-done.got_ref), custom_call_target="tpu_custom_call" | custom-call | flops 1000000 | bytes 1000000 | tf_op jit(solution)/shard_map/pallas_call | solution.py:468
  68.9 0.2 fusion.2
  69.0 0.1 collective-permute-start.4
  69.1 1.6 %collective-permute-start.5 = (f32[32,384]{1,0:T(8,128)S(1)}, f32[32,384]{1,0:T(8,128)S(1)}, u32[]{:S(2)}, u32[]{:S(2)}) collective-permute-start(f32[32,384]{1,0:T(8,128)S(1)} %get-tuple-element.38), channel_id=1, source_target_pairs={{0,1},{1,0},{2,3},{3,2},{4,5},{5,4},{6,7},{7,6},{8,9},{9,8},{10,11... | collective-permute-start | bytes 147464 | tf_op jit(solution)/shard_map/ppermute | solution.py:436
  70.7 3.7 %all-to-all-start.1 = ((bf16[8,8,384]{2,1,0:T(8,128)(2,1)}), bf16[8,8,384]{2,1,0:T(8,128)(2,1)S(1)}, u32[]{:S(2)}, u32[]{:S(2)}) async-start(bf16[8,8,384]{2,1,0:T(8,128)(2,1)} %get-tuple-element.36), calls=%async_computation.1 | async-start | bytes 98304 | tf_op jit(solution)/shard_map/all_to_all | solution.py:483
  74.4 0.0 collective-permute-done.5
  74.5 0.0 collective-permute-done.4
  74.5 0.3 maximum_bitcast_fusion
  74.8 0.9 %slice_bitcast_fusion = (bf16[4,6,12,384]{3,0,2,1:T(4,128)(2,1)}, bf16[4,6,12,384]{3,0,2,1:T(4,128)(2,1)}) fusion(bf16[2,4,6,12,384]{4,1,3,2,0:T(4,128)(2,1)S(1)} %maximum_bitcast_fusion), kind=kLoop, calls=%fused_computation.2 | loop fusion | bytes 884736 | tf_op jit(solution)/shard_map/squeeze | solution.py:487
  75.7 6.9 %all-to-all-done.1 = bf16[8,8,384]{2,1,0:T(8,128)(2,1)S(1)} async-done(((bf16[8,8,384]{2,1,0:T(8,128)(2,1)}), bf16[8,8,384]{2,1,0:T(8,128)(2,1)S(1)}, u32[]{:S(2)}, u32[]{:S(2)}) %all-to-all-start.1) | async-done | bytes 49184 | tf_op jit(solution)/shard_map/all_to_all | solution.py:483
  82.6 0.6 convert_reduce_fusion.1
  83.2 0.6 convert_reduce_fusion
  83.8 0.7 copy.17
  (7 shorter events, 0.1 us)
Async XLA Ops:
  0.6 22.3 %copy-start.3 = (bf16[4,6,12,384]{3,0,2,1:T(4,128)(2,1)S(1)}, bf16[4,6,12,384]{3,0,2,1:T(4,128)(2,1)}, u32[]{:S(2)}) copy-start(bf16[4,6,12,384]{3,0,2,1:T(4,128)(2,1)} %param.10) | copy-start | bytes 663556
  0.6 22.3 %copy-start.2 = (bf16[4,6,12,384]{3,0,2,1:T(4,128)(2,1)S(1)}, bf16[4,6,12,384]{3,0,2,1:T(4,128)(2,1)}, u32[]{:S(2)}) copy-start(bf16[4,6,12,384]{3,0,2,1:T(4,128)(2,1)} %param.9) | copy-start | bytes 663556
  0.7 18.8 %copy-start.7 = (bf16[384]{0:T(512)(128)(2,1)S(1)}, bf16[384]{0:T(512)(128)(2,1)}, u32[]{:S(2)}) copy-start(bf16[384]{0:T(512)(128)(2,1)} %param.12) | copy-start | bytes 2308
  0.7 18.8 %copy-start.8 = (bf16[384]{0:T(512)(128)(2,1)S(1)}, bf16[384]{0:T(512)(128)(2,1)}, u32[]{:S(2)}) copy-start(bf16[384]{0:T(512)(128)(2,1)} %param.13) | copy-start | bytes 2308
  0.7 22.2 %copy-start.6 = (bf16[384,384]{1,0:T(8,128)(2,1)S(1)}, bf16[384,384]{1,0:T(8,128)(2,1)}, u32[]{:S(2)}) copy-start(bf16[384,384]{1,0:T(8,128)(2,1)} %wout_ref.1) | copy-start | bytes 884740
  2.8 15.7 %collective-permute-start = (bf16[2,3,12,4,384]{4,3,2,1,0:T(4,128)(2,1)S(1)}, bf16[2,3,12,4,384]{4,3,2,1,0:T(4,128)(2,1)S(1)}, u32[]{:S(2)}, u32[]{:S(2)}) collective-permute-start(bf16[2,3,12,4,384]{4,3,2,1,0:T(4,128)(2,1)S(1)} %pad_maximum_fusion.1), channel_id=1, source_target_pairs={{0,240},{16,0},{32,16},{48,32},{64,48},{80,64},{96,80},{112,96},{1... | collective-permute-start | bytes 663560 | tf_op jit(solution)/shard_map/ppermute | solution.py:39
  11.1 0.9 %copy-start = (s32[144,144]{1,0:T(8,128)S(1)}, s32[144,144]{1,0:T(8,128)}, u32[]{:S(2)}) copy-start(s32[144,144]{1,0:T(8,128)} %ids_ref.3) | copy-start | bytes 248836
  12.0 0.8 copy-start.4
  18.8 4.1 %collective-permute-start.1 = (bf16[2,6,6,4,384]{4,3,2,1,0:T(4,128)(2,1)S(1)}, bf16[2,6,6,4,384]{4,3,2,1,0:T(4,128)(2,1)S(1)}, u32[]{:S(2)}, u32[]{:S(2)}) collective-permute-start(bf16[2,6,6,4,384]{4,3,2,1,0:T(4,128)(2,1)S(1)} %pad_maximum_fusion.2), channel_id=1, source_target_pairs={{0,15},{1,0},{2,1},{3,2},{4,3},{5,4},{6,5},{7,6},{8,7},{9,8},{10,9... | collective-permute-start | bytes 663560 | tf_op jit(solution)/shard_map/ppermute | solution.py:39
  19.5 19.3 %copy-start.1 = (s32[144,144]{1,0:T(8,128)S(1)}, s32[144,144]{1,0:T(8,128)}, u32[]{:S(2)}) copy-start(s32[144,144]{1,0:T(8,128)} %ids_ref.3) | copy-start | bytes 248836
  22.9 1.2 %copy-start.5 = (bf16[1152,384]{1,0:T(8,128)(2,1)S(1)}, bf16[1152,384]{1,0:T(8,128)(2,1)}, u32[]{:S(2)}) copy-start(bf16[1152,384]{1,0:T(8,128)(2,1)} %wqkv_ref.1) | copy-start | bytes 2654212
  36.4 5.0 %collective-permute-start.3 = (bf16[16,56,384]{2,1,0:T(8,128)(2,1)S(1)}, bf16[16,56,384]{2,1,0:T(8,128)(2,1)S(1)}, u32[]{:S(2)}, u32[]{:S(2)}) collective-permute-start(bf16[16,56,384]{2,1,0:T(8,128)(2,1)S(1)} %get-tuple-element.32), channel_id=1, source_target_pairs={{0,1},{1,0},{2,3},{3,2},{4,5},{5,4},{6,7},{7,6},{8,9},{9,8},{10,11... | collective-permute-start | bytes 2064392 | tf_op jit(solution)/shard_map/ppermute | solution.py:436
  42.6 25.1 %all-to-all-start = ((bf16[16,80,384]{2,1,0:T(8,128)(2,1)}), bf16[16,80,384]{2,1,0:T(8,128)(2,1)S(1)}, u32[]{:S(2)}, u32[]{:S(2)}) async-start(bf16[16,80,384]{2,1,0:T(8,128)(2,1)} %shard_map.131), calls=%async_computation | async-start | bytes 1966080 | tf_op jit(solution)/shard_map/all_to_all | solution.py:467
  49.1 15.4 %collective-permute-start.2 = (bf16[2,3,12,4,384]{4,3,2,1,0:T(4,128)(2,1)S(1)}, bf16[2,3,12,4,384]{4,3,2,1,0:T(4,128)(2,1)S(1)}, u32[]{:S(2)}, u32[]{:S(2)}) collective-permute-start(bf16[2,3,12,4,384]{4,3,2,1,0:T(4,128)(2,1)S(1)} %get-tuple-element.29), channel_id=1, source_target_pairs={{0,16},{16,32},{32,48},{48,64},{64,80},{80,96},{96,112},{112,128},... | collective-permute-start | bytes 663560 | tf_op jit(solution)/shard_map/ppermute | solution.py:39
  69.0 5.5 %collective-permute-start.4 = (bf16[2,6,6,4,384]{4,3,2,1,0:T(4,128)(2,1)S(1)}, bf16[2,6,6,4,384]{4,3,2,1,0:T(4,128)(2,1)S(1)}, u32[]{:S(2)}, u32[]{:S(2)}) collective-permute-start(bf16[2,6,6,4,384]{4,3,2,1,0:T(4,128)(2,1)S(1)} %get-tuple-element.50), channel_id=1, source_target_pairs={{0,1},{1,2},{2,3},{3,4},{4,5},{5,6},{6,7},{7,8},{8,9},{9,10},{10,1... | collective-permute-start | bytes 663560 | tf_op jit(solution)/shard_map/ppermute | solution.py:39
  69.1 5.3 %collective-permute-start.5 = (f32[32,384]{1,0:T(8,128)S(1)}, f32[32,384]{1,0:T(8,128)S(1)}, u32[]{:S(2)}, u32[]{:S(2)}) collective-permute-start(f32[32,384]{1,0:T(8,128)S(1)} %get-tuple-element.38), channel_id=1, source_target_pairs={{0,1},{1,0},{2,3},{3,2},{4,5},{5,4},{6,7},{7,6},{8,9},{9,8},{10,11... | collective-permute-start | bytes 147464 | tf_op jit(solution)/shard_map/ppermute | solution.py:436
  70.7 11.9 %all-to-all-start.1 = ((bf16[8,8,384]{2,1,0:T(8,128)(2,1)}), bf16[8,8,384]{2,1,0:T(8,128)(2,1)S(1)}, u32[]{:S(2)}, u32[]{:S(2)}) async-start(bf16[8,8,384]{2,1,0:T(8,128)(2,1)} %get-tuple-element.36), calls=%async_computation.1 | async-start | bytes 98304 | tf_op jit(solution)/shard_map/all_to_all | solution.py:483

commit v4 on v3

v4 whole, which is shorter than its diff:
```python
import functools

import jax
import jax.numpy as jnp
from jax import lax
from jax.experimental import pallas as pl
from jax.experimental.pallas import tpu as pltpu
from jax.sharding import PartitionSpec as P

HEADS = 12
HEAD_DIM = 32
WIN_TOK = 144
NBIAS = 759
D = 384
TOK = 288
EPS = 1e-05
BLOCKED = -10000.0
MARK = 256.0
LANES = 128
LOG2E = 1.4426950408889634
QSLOTS = 8
CHUNK = 104

wide = jnp.float32
low = jnp.bfloat16

NN = (((1,), (0,)), ((), ()))
NT = (((1,), (1,)), ((), ()))
TN = (((0,), (0,)), ((), ()))


def mm(a, b, dims):
    return lax.dot_general(a, b, dims, preferred_element_type=wide)


def passed_along(value, axis, steps):
    count = lax.axis_size(axis)
    pairs = [(source, (source + steps) % count) for source in range(count)]
    return lax.ppermute(value, axis, pairs)


def pre_kernel(
    place_ref, table_in, ids_in, bias_ref, order_ref, table_ref, ids_ref, tail_ref, far_ref, sems
):
    copies = [
        pltpu.make_async_copy(table_in, table_ref, sems.at[0]),
        pltpu.make_async_copy(ids_in, ids_ref, sems.at[1]),
    ]
    for copy in copies:
        copy.start()
    new = lax.broadcasted_iota(jnp.int32, (D, D), 0)
    old = lax.broadcasted_iota(jnp.int32, (D, D), 1)
    tens = new // 6
    r = new - 6 * tens
    a = tens & 3
    j = (tens >> 2) & 7
    other = tens >> 5
    core = place_ref[0]
    c = core + other - 2 * core * other
    order_ref[...] = (old == (a * 16 + 2 * j + c) * 6 + r).astype(wide).astype(low)

    for copy in copies:
        copy.wait()
    tail_ref[...] = jnp.zeros((WIN_TOK, LANES), jnp.int32)
    tail_ref[:, 0:16] = ids_ref[:, LANES:WIN_TOK]
    for head in range(HEADS):
        for p in range(6):
            stop = min((p + 1) * LANES, NBIAS)
            far_ref[head * 6 + p : head * 6 + p + 1, 0 : stop - p * LANES] = (
                table_ref[head, :, p * LANES : stop] * LOG2E
            )

    def rows(step, _):
        at = pl.ds(pl.multiple_of(step * 8, 8), 8)
        for half in range(2):
            ids = ids_ref[at, 0:LANES] if half == 0 else tail_ref[at, :]
            place = ids & (LANES - 1)
            piece = ids >> 7
            picks = [piece == p for p in range(6)]
            for head in range(HEADS):
                got = None
                for p in range(6):
                    source = jnp.broadcast_to(
                        far_ref[head * 6 + p : head * 6 + p + 1, :], (8, LANES)
                    )
                    found = jnp.take_along_axis(source, place, axis=1)
                    got = found if got is None else jnp.where(picks[p], found, got)
                bias_ref[head, at, half * LANES : (half + 1) * LANES] = got
        return 0

    lax.fori_loop(0, WIN_TOK // 8, rows, 0)


def main_kernel(
    place_ref,
    scal_ref,
    fields_ref,
    cot_ref,
    lat_ref,
    lon_ref,
    token_ref,
    gain_ref,
    wqkv_in_ref,
    wout_ref,
    bias_ref,
    order_ref,
    filled_ref,
    mixed_ref,
    igrad_ref,
    keep_ref,
    give_ref,
    bg_ref,
    bt_ref,
    x_ref,
    c_ref,
    std_ref,
    qkv_ref,
    gm_ref,
    qt_ref,
    gmt_ref,
    gq_ref,
    gkt_ref,
    gvt_ref,
    wqkv_ref,
    sem,
    mix_ref,
):
    wqkv_copy = pltpu.make_async_copy(wqkv_in_ref, wqkv_ref, sem)
    wqkv_copy.start()
    level = lax.broadcasted_iota(jnp.int32, (4, 1), 0)
    own_masked = jnp.where(level < 2, scal_ref[0], scal_ref[1]) == 1
    for which, own, dest in ((0, fields_ref, x_ref), (1, cot_ref, c_ref)):
        for a in range(6):
            for o in range(12):
                if o >= 6:
                    piece = lon_ref[which, a, o - 6]
                elif a >= 3:
                    piece = lat_ref[which, a - 3, 6 + o]
                else:
                    piece = own[3 + a, 6 + o]
                piece = piece.astype(wide)
                if which == 0 and o < 6 and a < 3:
                    piece = jnp.where(own_masked, MARK, piece)
                base = (a * 12 + o) * 4
                for c in range(3):
                    mix_ref[c, base : base + 4, :] = piece[:, c * LANES : (c + 1) * LANES]
        for zs in range(4):
            for c in range(3):
                dest[zs * 72 : (zs + 1) * 72, c * LANES : (c + 1) * LANES] = mix_ref[
                    c, pl.ds((zs + 1) % 4, 72, stride=4), :
                ]
    raw = x_ref[...]
    masked = raw > 0.5 * MARK
    filled = jnp.where(masked, token_ref[...], raw)
    filled_ref[...] = filled.astype(low)
    gain = gain_ref[...]
    center = filled - jnp.mean(filled, axis=-1, keepdims=True)
    inv_std = lax.rsqrt(jnp.mean(center * center, axis=-1, keepdims=True) + EPS)
    standard = center * inv_std
    std_ref[...] = standard
    normed = (standard * gain).astype(low)
    cot = c_ref[...].astype(low)

    wqkv_copy.wait()
    qkv_ref[...] = mm(normed, wqkv_ref[...], NT).astype(low)
    gm_ref[...] = mm(cot, wout_ref[...], NN).astype(low)
    for w in range(2):
        rows = slice(w * WIN_TOK, (w + 1) * WIN_TOK)
        qt_ref[w] = mm(wqkv_ref[0:D, :], normed[rows], NT).astype(low)
        gmt_ref[w] = mm(wout_ref[...], cot[rows], (((0,), (1,)), ((), ()))).astype(low)

    last = place_ref[1] == 1
    ti = lax.broadcasted_iota(jnp.int32, (WIN_TOK, WIN_TOK), 0)
    tj = lax.broadcasted_iota(jnp.int32, (WIN_TOK, WIN_TOK), 1)
    zi = (ti >= 72).astype(jnp.int32)
    zj = (tj >= 72).astype(jnp.int32)
    ai = (ti - 72 * zi >= 36).astype(jnp.int32)
    aj = (tj - 72 * zj >= 36).astype(jnp.int32)
    lat_apart = jnp.where(last, (ai != aj).astype(wide), 0.0)
    lev_apart = (zi != zj).astype(wide)
    apart = [
        jnp.concatenate([value] * 4, axis=0) > 0.0 for value in (lat_apart, lat_apart + lev_apart)
    ]
    lane = lax.broadcasted_iota(jnp.int32, (1, LANES), 1) // HEAD_DIM
    scale = HEAD_DIM ** (-0.5)
    masks = [(lane == sub).astype(low) for sub in range(4)]
    for group in range(3):
        cols = slice(group * LANES, (group + 1) * LANES)
        kcols = slice(D + group * LANES, D + (group + 1) * LANES)
        vcols = slice(2 * D + group * LANES, 2 * D + (group + 1) * LANES)
        totals = [None] * 4
        for w in range(2):
            rows = slice(w * WIN_TOK, (w + 1) * WIN_TOK)
            q = qkv_ref[rows, cols]
            k = qkv_ref[rows, kcols]
            v = qkv_ref[rows, vcols]
            g = gm_ref[rows, cols]
            q_four = jnp.concatenate([q * mask for mask in masks], axis=0)
            g_four = jnp.concatenate([g * mask for mask in masks], axis=0)
            biases = jnp.concatenate(
                [bias_ref[group * 4 + sub, :, 0:WIN_TOK] for sub in range(4)], axis=0
            )
            scores = mm(q_four, k, NT) * (scale * LOG2E) + biases
            scores = jnp.where(apart[w], BLOCKED * LOG2E, scores)
            top = jnp.max(scores, axis=-1, keepdims=True)
            expo = jnp.exp2(scores - top)
            prob = (expo * (1.0 / jnp.sum(expo, axis=-1, keepdims=True))).astype(low)
            mixed = mm(prob, v, NN)
            delta = jnp.sum(g_four.astype(wide) * mixed, axis=-1, keepdims=True)
            grad = prob.astype(wide) * (mm(g_four, v, NT) - delta)
            glow = grad.astype(low)
            gq = mm(glow, k, NN)
            mixed_sum = jnp.zeros((WIN_TOK, LANES), wide)
            gq_sum = jnp.zeros((WIN_TOK, LANES), wide)
            for sub in range(4):
                head = group * 4 + sub
                feats = slice(head * HEAD_DIM, (head + 1) * HEAD_DIM)
                part = slice(sub * WIN_TOK, (sub + 1) * WIN_TOK)
                mixed_sum = jnp.where(lane == sub, mixed[part], mixed_sum)
                gq_sum = jnp.where(lane == sub, gq[part], gq_sum)
                gvt_ref[w, feats, :] = mm(gmt_ref[w, feats, :], prob[part], NN).astype(low)
                gkt_ref[w, feats, :] = (mm(qt_ref[w, feats, :], glow[part], NN) * scale).astype(low)
                if w == 0:
                    totals[sub] = grad[part]
                else:
                    total = totals[sub] + grad[part]
                    bg_ref[head] = total[:, 0:LANES]
                    bt_ref[head, :, 0:16] = total[:, LANES:WIN_TOK]
            mixed_ref[rows, cols] = mixed_sum.astype(low)
            gq_ref[rows, cols] = (gq_sum * scale).astype(low)

    mixed = mixed_ref[...]
    gq = gq_ref[...]
    gk = jnp.concatenate([gkt_ref[w].T for w in range(2)], axis=0)
    gv = jnp.concatenate([gvt_ref[w].T for w in range(2)], axis=0)
    grad_normed = (
        mm(gq, wqkv_ref[0:D, :], NN)
        + mm(gk, wqkv_ref[D : 2 * D, :], NN)
        + mm(gv, wqkv_ref[2 * D : 3 * D, :], NN)
    )
    grad_normed = grad_normed.astype(low).astype(wide)
    standard = std_ref[...]
    scaled = grad_normed * gain
    inner = (
        scaled
        - jnp.mean(scaled, axis=-1, keepdims=True)
        - standard * jnp.mean(scaled * standard, axis=-1, keepdims=True)
    )
    grad_filled = c_ref[...] + inv_std * inner
    igrad_ref[...] = jnp.where(masked, 0.0, grad_filled).astype(low)
    gain_grad = jnp.sum(grad_normed * standard, axis=0, keepdims=True)
    token_grad = jnp.sum(jnp.where(masked, grad_filled, 0.0), axis=0, keepdims=True)

    order = order_ref[...]
    parts = []
    for value in (gq, gk, gv, cot):
        turned = mm(order, value, NT).astype(low)
        other = mixed if value is cot else normed
        parts.append(mm(turned, other, NN))
    vectors = jnp.concatenate([gain_grad, token_grad, jnp.zeros((6, D), wide)], axis=0)
    for n in range(16):
        rows = slice(n * 24, (n + 1) * 24)
        chunk = jnp.concatenate([part[rows] for part in parts] + [vectors], axis=0)
        dest = keep_ref if n < 8 else give_ref
        dest[n % 8] = chunk.astype(low)


def out_kernel(filled_ref, mixed_ref, igrad_ref, wout_ref, out_own_ref, out_lon_ref, mix_ref):
    def put_back(which, value):
        for zs in range(4):
            for c in range(3):
                mix_ref[c, pl.ds((zs + 1) % 4, 72, stride=4), :] = value[
                    zs * 72 : (zs + 1) * 72, c * LANES : (c + 1) * LANES
                ]
        for a in range(6):
            for o in range(12):
                base = (a * 12 + o) * 4
                piece = jnp.concatenate([mix_ref[c, base : base + 4, :] for c in range(3)], axis=1)
                if o < 6:
                    out_own_ref[which, a, o] = piece.astype(low)
                else:
                    out_lon_ref[which, a, o - 6] = piece.astype(low)

    branch = mm(mixed_ref[...], wout_ref[...], NT).astype(low).astype(wide)
    put_back(0, filled_ref[...].astype(wide) + branch)
    put_back(1, igrad_ref[...].astype(wide))


def table_kernel(bg_ref, bt_ref, ids_ref, sums_ref, rem_ref, near_ref, tail_ref, rest_ref):
    slot = lax.broadcasted_iota(jnp.int32, (QSLOTS, LANES), 0)
    spot = lax.broadcasted_iota(jnp.int32, (LANES, LANES), 0)
    near_ref[...] = ids_ref[:, 0:LANES]
    tail_ref[:, 0:16] = ids_ref[:, LANES:WIN_TOK]
    rest_ref[...] = jnp.concatenate(
        [tail_ref[pl.ds(k, 18, stride=8), :][:, 0:16] for k in range(8)], axis=1
    )
    for head in range(HEADS):
        rem_ref[head] = jnp.concatenate(
            [bt_ref[head, pl.ds(k, 18, stride=8), :][:, 0:16] for k in range(8)], axis=1
        )

    def one_step(step, acc):
        lefts = []
        rights = []
        for s in range(9):
            if s < 8:
                ids = near_ref[pl.ds(step * 8 + s, 1), :]
                vals = [bg_ref[head, pl.ds(step * 8 + s, 1), :] for head in range(HEADS)]
            else:
                ids = rest_ref[pl.ds(step, 1), :]
                vals = [rem_ref[head, pl.ds(step, 1), :] for head in range(HEADS)]
            rights.append(((ids & (LANES - 1)) == spot).astype(wide).astype(low))
            here = (ids >> 7) == slot
            lefts.append(
                jnp.concatenate([jnp.where(here, val, 0.0) for val in vals], axis=0).astype(low)
            )
        left = jnp.concatenate(lefts, axis=1)
        right = jnp.concatenate(rights, axis=1)
        return acc + mm(left, right, NT)

    start = jnp.zeros((HEADS * QSLOTS, LANES), wide)
    sums_ref[...] = lax.fori_loop(0, 18, one_step, start, unroll=6)


def pack_kernel(keep_ref, taken_ref, table_ref, send_ref):
    total = keep_ref[0].astype(wide) + taken_ref[0].astype(wide)
    table = table_ref[...]
    row = lax.broadcasted_iota(jnp.int32, (HEADS * QSLOTS, 1), 0)
    for n in range(2):
        for p in range(3):
            piece = total[96 + n : 97 + n, p * LANES : (p + 1) * LANES]
            table = jnp.where(row == QSLOTS * p + 6 + n, piece, table)
    extra = jnp.concatenate([table[0:32], table[32:64], table[64:96]], axis=1).astype(low)
    for m in range(8):
        total = keep_ref[m].astype(wide) + taken_ref[m].astype(wide)
        send_ref[m, 0:96, :] = total[0:96].astype(low)
        send_ref[m, 96:128, :] = extra


def sum_kernel(got_ref, second_ref, table_ref):
    total = got_ref[0].astype(wide)
    for m in range(1, 8):
        total = total + got_ref[m].astype(wide)
    table = total[96:128]
    table_ref[...] = table
    vectors = jnp.concatenate(
        [table[QSLOTS * p + 6 : QSLOTS * p + 8, 0:LANES] for p in range(3)], axis=1
    )
    for a in range(16):
        chunk = jnp.concatenate([total[6 * a : 6 * a + 6], vectors], axis=0)
        second_ref[a] = chunk.astype(low)


def spread_kernel(mine_ref, other_ref, table_ref):
    total = mine_ref[...] + other_ref[...]
    for head in range(HEADS):
        for q in range(6):
            spot = head * QSLOTS + q
            cols = slice(spot // 32 * LANES, (spot // 32 + 1) * LANES)
            width = min(LANES, NBIAS - q * LANES)
            piece = total[spot % 32 : spot % 32 + 1, cols]
            table_ref[head, :, q * LANES : q * LANES + width] = piece[:, 0:width]


def local(
    fields,
    cotangent,
    window_mask,
    mask_token,
    norm_gain,
    qkv_weight,
    out_weight,
    bias_table,
    bias_index,
):
    own_mask = window_mask[:, 0, 0]
    last = (lax.axis_index("lat") == lax.axis_size("lat") - 1).astype(jnp.int32)
    core = lax.axis_index("lon") % 2
    place = jnp.stack([core, last])
    fields = fields.transpose(1, 2, 0, 3)
    cotangent = cotangent.transpose(1, 2, 0, 3)
    smem = pl.BlockSpec(memory_space=pltpu.SMEM)
    vmem = pl.BlockSpec(memory_space=pltpu.VMEM)
    hbm = pl.BlockSpec(memory_space=pltpu.HBM)
    hidden = jnp.repeat(own_mask, 2)[:, None] == 1
    strip = jnp.stack((jnp.where(hidden, jnp.bfloat16(MARK), fields[:3]), cotangent[:3]))
    lat_in = passed_along(strip, "lat", -1)
    bias, order = pl.pallas_call(
        pre_kernel,
        out_shape=(
            jax.ShapeDtypeStruct((HEADS, WIN_TOK, 256), wide),
            jax.ShapeDtypeStruct((D, D), low),
        ),
        in_specs=[smem, hbm, hbm],
        out_specs=(vmem,) * 2,
        scratch_shapes=[
            pltpu.VMEM((HEADS, 1, NBIAS), wide),
            pltpu.VMEM((WIN_TOK, WIN_TOK), jnp.int32),
            pltpu.VMEM((WIN_TOK, LANES), jnp.int32),
            pltpu.VMEM((HEADS * 6, LANES), wide),
            pltpu.SemaphoreType.DMA((2,)),
        ],
        compiler_params=pltpu.CompilerParams(vmem_limit_bytes=8 * 2**20),
        cost_estimate=pl.CostEstimate(flops=5 * 10**9, bytes_accessed=0, transcendentals=0),
    )(place, bias_table.transpose(1, 0, 2), bias_index)
    lat_in, bias, order = lax.optimization_barrier((lat_in, bias, order))
    own = jnp.stack((jnp.where(hidden, jnp.bfloat16(MARK), fields[3:, :6]), cotangent[3:, :6]))
    lon_in = passed_along(jnp.concatenate((own, lat_in[:, :, :6]), axis=1), "lon", -1)

    filled, mixed, igrad, keep, give, bias_grad, bias_tail = pl.pallas_call(
        main_kernel,
        out_shape=(
            jax.ShapeDtypeStruct((TOK, D), low),
            jax.ShapeDtypeStruct((TOK, D), low),
            jax.ShapeDtypeStruct((TOK, D), low),
            jax.ShapeDtypeStruct((8, CHUNK, D), low),
            jax.ShapeDtypeStruct((8, CHUNK, D), low),
            jax.ShapeDtypeStruct((HEADS, WIN_TOK, LANES), wide),
            jax.ShapeDtypeStruct((HEADS, WIN_TOK, LANES), wide),
        ),
        in_specs=[smem, smem] + [vmem] * 6 + [hbm, vmem, vmem, vmem],
        out_specs=(vmem,) * 7,
        scratch_shapes=[
            pltpu.VMEM((TOK, D), wide),
            pltpu.VMEM((TOK, D), wide),
            pltpu.VMEM((TOK, D), wide),
            pltpu.VMEM((TOK, 3 * D), low),
            pltpu.VMEM((TOK, D), low),
            pltpu.VMEM((2, D, WIN_TOK), low),
            pltpu.VMEM((2, D, WIN_TOK), low),
            pltpu.VMEM((TOK, D), low),
            pltpu.VMEM((2, D, WIN_TOK), low),
            pltpu.VMEM((2, D, WIN_TOK), low),
            pltpu.VMEM((3 * D, D), low),
            pltpu.SemaphoreType.DMA(()),
            pltpu.VMEM((3, TOK, LANES), wide),
        ],
        compiler_params=pltpu.CompilerParams(vmem_limit_bytes=24 * 2**20),
        cost_estimate=pl.CostEstimate(
            flops=10**10, bytes_accessed=0, transcendentals=0
        ),
    )(
        place,
        own_mask,
        fields,
        cotangent,
        lat_in,
        lon_in,
        mask_token.astype(wide)[None],
        norm_gain.astype(wide)[None],
        qkv_weight,
        out_weight,
        bias,
        order,
    )

    size = lax.axis_size("lon")

    def swapped(value, bit):
        return lax.ppermute(value, "lon", [(i, i ^ bit) for i in range(size)])

    taken = swapped(give, 1)
    out_own, out_lon = pl.pallas_call(
        out_kernel,
        out_shape=(
            jax.ShapeDtypeStruct((2, 6, 6, 4, D), low),
            jax.ShapeDtypeStruct((2, 6, 6, 4, D), low),
        ),
        in_specs=[vmem] * 4,
        out_specs=(vmem, vmem),
        scratch_shapes=[pltpu.VMEM((3, TOK, LANES), wide)],
        compiler_params=pltpu.CompilerParams(vmem_limit_bytes=16 * 2**20),
        cost_estimate=pl.CostEstimate(flops=2 * 10**9, bytes_accessed=0, transcendentals=0),
    )(filled, mixed, igrad, out_weight)
    lon_out = passed_along(out_lon, "lon", 1)
    bias_grad, out_own = lax.optimization_barrier((bias_grad, out_own))
    table = pl.pallas_call(
        table_kernel,
        out_shape=jax.ShapeDtypeStruct((HEADS * QSLOTS, LANES), wide),
        in_specs=[vmem] * 3,
        out_specs=vmem,
        scratch_shapes=[
            pltpu.VMEM((HEADS, 18, LANES), wide),
            pltpu.VMEM((WIN_TOK, LANES), jnp.int32),
            pltpu.VMEM((WIN_TOK, LANES), jnp.int32),
            pltpu.VMEM((18, LANES), jnp.int32),
        ],
        compiler_params=pltpu.CompilerParams(vmem_limit_bytes=8 * 2**20),
        cost_estimate=pl.CostEstimate(flops=10**9, bytes_accessed=10**6, transcendentals=0),
    )(bias_grad, bias_tail, bias_index)
    pair = pl.pallas_call(
        pack_kernel,
        out_shape=jax.ShapeDtypeStruct((8, 128, D), low),
        in_specs=[vmem] * 3,
        out_specs=vmem,
        compiler_params=pltpu.CompilerParams(vmem_limit_bytes=8 * 2**20),
        cost_estimate=pl.CostEstimate(flops=10**6, bytes_accessed=10**6, transcendentals=0),
    )(keep, taken, table)
    pair, lon_out = lax.optimization_barrier((pair, lon_out))
    groups = [list(range(c, size, 2)) for c in range(2)]
    got = lax.all_to_all(pair, "lon", 0, 0, axis_index_groups=groups, tiled=True)
    second, table = pl.pallas_call(
        sum_kernel,
        out_shape=(
            jax.ShapeDtypeStruct((16, 8, D), low),
            jax.ShapeDtypeStruct((32, D), wide),
        ),
        in_specs=[vmem],
        out_specs=(vmem, vmem),
        compiler_params=pltpu.CompilerParams(vmem_limit_bytes=8 * 2**20),
        cost_estimate=pl.CostEstimate(flops=10**6, bytes_accessed=10**6, transcendentals=0),
    )(got)

    full = jnp.concatenate((lon_out, out_own), axis=2)
    full, second = lax.optimization_barrier((full, second))
    final = lax.all_to_all(second, "lat", 0, 0, tiled=True)
    lat_out = passed_along(full[:, 3:], "lat", 1)
    table_grad = pl.pallas_call(
        spread_kernel,
        out_shape=jax.ShapeDtypeStruct((HEADS, 1, NBIAS), wide),
        in_specs=[vmem, vmem],
        out_specs=vmem,
        cost_estimate=pl.CostEstimate(flops=10**5, bytes_accessed=10**5, transcendentals=0),
    )(table, swapped(table, 1)).transpose(1, 0, 2)
    done = jnp.concatenate((lat_out, full[:, :3]), axis=1).transpose(0, 3, 1, 2, 4)
    output, input_grad = done[0], done[1]
    final, output, input_grad, table_grad = lax.optimization_barrier(
        (final, output, input_grad, table_grad)
    )
    weight_grads = jnp.sum(final[:, :6].astype(wide), axis=0)
    vector_grads = jnp.sum(final[:, 6:].astype(wide), axis=0)
    return (output, input_grad, weight_grads, table_grad, vector_grads)


def solution(mesh):
    placed = (
        P(None, "lat", "lon", None),
        P(None, "lat", "lon", None),
        P(None, "lat", "lon"),
        P(),
        P(),
        P(),
        P(),
        P("lat", None, None),
        P(),
    )
    return jax.shard_map(
        local,
        mesh=mesh,
        in_specs=placed,
        out_specs=(
            P(None, "lat", "lon", None),
            P(None, "lat", "lon", None),
            P(("lat", "lon"), None),
            P("lat", None, None),
            P(),
        ),
        check_vma=False,
    )
```

time: 85.4 us -> 78.2 us (0.916)
  waiting for transfers between devices: 26.4 us -> 23.3 us
  other arithmetic: 5.63 us -> 4.04 us
  Pallas kernels: 22.1 us -> 20.6 us
  local copies, waits for them, and re-layouts: 4.84 us -> 3.74 us
    ppermute x4, waiting for transfers between devices: 16.7 us -> 5.25 us  [passed_along(): return lax.ppermute(value, axis, pairs)]
    all_to_all x2, waiting for transfers between devices: 9.71 us -> 18.1 us  [the longest x1 10.5 us: local(): lax.all_to_all(pair, 'lon', 0, 0, axis_index_groups=groups, tiled=True)]
    all_to_all x2, starting transfers between devices: 10.3 us -> 13.7 us  [the longest x1 7.03 us: local(): final = lax.all_to_all(second, 'lat', 0, 0, tiled=True)]
    pallas_call x3 -> x5, Pallas kernels: 14.7 us -> 12.9 us  [the longest x1 9.13 us: local(): pl.pallas_call(main_kernel, out_shape=(jax.ShapeDtypeStruct((TOK, D), low...]
    ppermute x4, starting transfers between devices: 10.3 us -> 8.53 us  [passed_along(): return lax.ppermute(value, axis, pairs)]
    ppermute x2, starting transfers between devices: 3.96 us -> 2.33 us  [swapped(): return lax.ppermute(value, 'lon', [(i, i ^ bit) for i in range(size)])]
    unnamed x19 -> x24, local copies, waits for them, and re-layouts: 3.53 us -> 2.46 us
  transfers between devices with their start and end apart: 8 -> 8, of which waited for: 4 -> 5; matrix products, arithmetic and copies ran while one was open for 4% -> 2% of each run, Pallas kernels for 9% -> 14%
where the time goes in v4:
time: 78.2 us; the launch traced here: 77.1 us
  starting transfers between devices  24.6 us (31%)
  waiting for transfers between devices  23.3 us (30%)
  Pallas kernels  20.6 us (26%)
  other arithmetic  4.04 us (5%)
  local copies, waits for them, and re-layouts  3.74 us (5%)
  between operations  0.83 us (1%)
    all_to_all x1, waiting for transfers between devices, local(): lax.all_to_all(pair, 'lon', 0, 0, axis_index_groups=groups, tiled=True)  10.5 us
    pallas_call x1, Pallas kernels, local(): pl.pallas_call(main_kernel, out_shape=(jax.ShapeDtypeStruct((TOK, D), low...  9.13 us
    ppermute x4, starting transfers between devices, passed_along(): return lax.ppermute(value, axis, pairs)  8.53 us
    all_to_all x1, waiting for transfers between devices, local(): final = lax.all_to_all(second, 'lat', 0, 0, tiled=True)  7.55 us
    all_to_all x1, starting transfers between devices, local(): final = lax.all_to_all(second, 'lat', 0, 0, tiled=True)  7.03 us
    all_to_all x1, starting transfers between devices, local(): lax.all_to_all(pair, 'lon', 0, 0, axis_index_groups=groups, tiled=True)  6.66 us
    ppermute x4, waiting for transfers between devices, passed_along(): return lax.ppermute(value, axis, pairs)  5.25 us
    pallas_call x1, Pallas kernels, local(): pl.pallas_call(pre_kernel, out_shape=(jax.ShapeDtypeStruct((HEADS, WIN_TO...  5.13 us
  transfers between devices with their start and end apart: 8, of which 5 were waited for; matrix products, arithmetic and copies ran while one was open for 2% of the time, Pallas kernels for 14%

profile of v4, /device:TPU:2, one launch (start us, length us, event | category | flops | bytes accessed | tf_op | source)
XLA Modules:
  0.0 77.1 jit_solution(9505620915538292823)
XLA Ops:
  0.6 0.7 broadcast_compare_fusion
  1.3 0.1 broadcast_in_dim.37
  1.4 0.1 eq.18
  1.5 1.1 %slice_bitcast_fusion.2 = (bf16[1,3,12,4,384]{4,3,2,1,0:T(4,128)(2,1)S(1)}, bf16[1,3,12,4,384]{4,3,2,1,0:T(4,128)(2,1)S(1)}) fusion(bf16[6,12,4,384]{3,2,1,0:T(4,128)(2,1)} %bitcast.25, bf16[6,12,4,384]{3,2,1,0:T(4,128)(2,1)} %bitcast.22, pred[4]{0:T(512)(128)(4,1)S(1)} %eq.18), kind=kLoop, calls=%fused_computation.7 | loop fusion | flops 55296 | bytes 442372 | tf_op jit(solution)/shard_map/stack | solution.py:386
  2.5 0.2 pad_maximum_fusion.1
  2.7 7.5 %collective-permute-start = (bf16[2,3,12,4,384]{4,3,2,1,0:T(4,128)(2,1)S(1)}, bf16[2,3,12,4,384]{4,3,2,1,0:T(4,128)(2,1)S(1)}, u32[]{:S(2)}, u32[]{:S(2)}) collective-permute-start(bf16[2,3,12,4,384]{4,3,2,1,0:T(4,128)(2,1)S(1)} %pad_maximum_fusion.1), channel_id=1, source_target_pairs={{0,240},{16,0},{32,16},{48,32},{64,48},{80,64},{96,80},{112,96},{1... | collective-permute-start | bytes 663560 | tf_op jit(solution)/shard_map/ppermute | solution.py:39
  10.2 0.1 pad_add_fusion.place_ref
  10.3 0.0 copy-start.5
  10.3 0.9 %copy-done.5 = s32[144,144]{1,0:T(8,128)S(1)} copy-done((s32[144,144]{1,0:T(8,128)S(1)}, s32[144,144]{1,0:T(8,128)}, u32[]{:S(2)}) %copy-start.5) | copy-done | bytes 82968
  11.2 0.0 copy-start.7
  11.2 0.8 copy-done.7
  11.9 0.0 copy-start
  11.9 0.0 copy-start.1
  11.9 0.0 copy-start.10
  11.9 0.0 copy-start.11
  11.9 0.0 copy-start.3
  12.0 0.0 copy-start.4
  12.0 0.0 copy-start.8
  12.0 5.1 %shard_map.128 = (f32[12,144,256]{2,1,0:T(8,128)S(1)}, bf16[384,384]{1,0:T(8,128)(2,1)S(1)}) custom-call(s32[2]{0:T(128)S(1)} %pad_add_fusion.place_ref, f32[12,1,759]{2,1,0:T(1,128)S(1)} %bitcast.28, s32[144,144]{1,0:T(8,128)S(1)} %copy-done.5), custom_call_target="tpu_custom_call" | custom-call | flops 5000000000 | tf_op jit(solution)/shard_map/pallas_call | solution.py:388
  17.1 0.0 copy-done
  17.1 0.0 copy-done.1
  17.1 0.1 slice_bitcast_fusion.3
  17.2 0.0 collective-permute-done.lat_ref
  17.3 0.2 pad_maximum_fusion.2
  17.5 0.7 collective-permute-start.1
  18.1 0.0 copy-done.10
  18.1 0.0 copy-done.11
  18.2 3.4 %collective-permute-done.1.lon_ref = bf16[2,6,6,4,384]{4,3,2,1,0:T(4,128)(2,1)S(1)} collective-permute-done((bf16[2,6,6,4,384]{4,3,2,1,0:T(4,128)(2,1)S(1)}, bf16[2,6,6,4,384]{4,3,2,1,0:T(4,128)(2,1)S(1)}, u32[]{:S(2)}, u32[]{:S(2)}) %collective-permute-start.1) | collective-permute-done | bytes 221216 | tf_op jit(solution)/shard_map/ppermute | solution.py:39
  21.6 0.0 copy-done.3
  21.6 0.0 copy-done.4
  21.6 0.0 copy-done.8
  21.6 9.1 %shard_map.129 = (bf16[288,384]{1,0:T(8,128)(2,1)S(1)}, bf16[288,384]{1,0:T(8,128)(2,1)S(1)}, bf16[288,384]{1,0:T(8,128)(2,1)S(1)}, bf16[8,104,384]{2,1,0:T(8,12...) custom-call(s32[2]{0:T(128)S(1)} %pad_add_fusion.place_ref, ...), custom_call_target="tpu_custom_call" | custom-call | flops 10000000000 | tf_op jit(solution)/shard_map/pallas_call | solution.py:410
  30.7 2.2 %collective-permute-start.2 = (bf16[8,104,384]{2,1,0:T(8,128)(2,1)S(1)}, bf16[8,104,384]{2,1,0:T(8,128)(2,1)S(1)}, u32[]{:S(2)}, u32[]{:S(2)}) collective-permute-start(bf16[8,104,384]{2,1,0:T(8,128)(2,1)S(1)} %get-tuple-element.37), channel_id=1, source_target_pairs={{0,1},{1,0},{2,3},{3,2},{4,5},{5,4},{6,7},{7,6},{8,9},{9,8},{10,11... | collective-permute-start | bytes 1916936 | tf_op jit(solution)/shard_map/ppermute | solution.py:460
  33.0 0.0 copy-start.6
  33.0 0.5 shard_map.130
  33.5 0.3 collective-permute-start.3
  33.8 0.1 copy-done.6
  33.9 2.6 %shard_map.131.table_ref = f32[96,128]{1,0:T(8,128)S(1)} custom-call(f32[12,144,128]{2,1,0:T(8,128)S(1)} %get-tuple-element.43.bg_ref, f32[12,144,128]{2,1,0:T(8,128)S(1)} %get-tuple-element.44.bt_ref, s32[144,144]{1,0:T(8,128)S(1)} %copy-done.6), custom_call_target="tpu_custom_call" | custom-call | flops 1000000000 | bytes 1000000 | tf_op jit(solution)/shard_map/pallas_call | solution.py:477
  36.5 0.0 collective-permute-done.2.taken_ref
  36.5 1.0 %shard_map.132 = bf16[8,128,384]{2,1,0:T(8,128)(2,1)} custom-call(bf16[8,104,384]{2,1,0:T(8,128)(2,1)S(1)} %get-tuple-element.36.keep_ref, bf16[8,104,384]{2,1,0:T(8,128)(2,1)S(1)} %collective-permute-done.2.taken_ref, f32[96,128]{1,0:T(8,128)S(1)} %shard_map.131.table_ref), custom_call_target="tpu_custom_call" | custom-call | flops 1000000 | bytes 1000000 | tf_op jit(solution)/shard_map/pallas_call | solution.py:491
  37.6 1.5 %collective-permute-done.3 = bf16[2,6,6,4,384]{4,3,2,1,0:T(4,128)(2,1)S(1)} collective-permute-done((bf16[2,6,6,4,384]{4,3,2,1,0:T(4,128)(2,1)S(1)}, bf16[2,6,6,4,384]{4,3,2,1,0:T(4,128)(2,1)S(1)}, u32[]{:S(2)}, u32[]{:S(2)}) %collective-permute-start.3) | collective-permute-done | bytes 221216 | tf_op jit(solution)/shard_map/ppermute | solution.py:39
  39.1 6.7 %all-to-all-start = ((bf16[8,128,384]{2,1,0:T(8,128)(2,1)}), bf16[8,128,384]{2,1,0:T(8,128)(2,1)S(1)}, u32[]{:S(2)}, u32[]{:S(2)}) async-start(bf16[8,128,384]{2,1,0:T(8,128)(2,1)} %shard_map.132), calls=%async_computation | async-start | bytes 1572864 | tf_op jit(solution)/shard_map/all_to_all | solution.py:501
  45.7 0.3 pad_maximum_fusion
  46.0 10.5 %all-to-all-done.got_ref = bf16[8,128,384]{2,1,0:T(8,128)(2,1)S(1)} async-done(((bf16[8,128,384]{2,1,0:T(8,128)(2,1)}), bf16[8,128,384]{2,1,0:T(8,128)(2,1)S(1)}, u32[]{:S(2)}, u32[]{:S(2)}) %all-to-all-start) | async-done | bytes 786464 | tf_op jit(solution)/shard_map/all_to_all | solution.py:501
  56.6 0.7 shard_map.133
  57.3 0.0 copy-start.2
  57.3 0.2 fusion.2
  57.5 0.1 collective-permute-start.4
  57.6 0.1 collective-permute-start.5
  57.7 7.0 %all-to-all-start.1 = ((bf16[16,8,384]{2,1,0:T(8,128)(2,1)}), bf16[16,8,384]{2,1,0:T(8,128)(2,1)S(1)}, u32[]{:S(2)}, u32[]{:S(2)}) async-start(bf16[16,8,384]{2,1,0:T(8,128)(2,1)} %get-tuple-element.50), calls=%async_computation.1 | async-start | bytes 196608 | tf_op jit(solution)/shard_map/all_to_all | solution.py:516
  64.7 0.0 collective-permute-done.5.other_ref
  64.7 0.0 copy-done.2
  64.7 0.0 copy-start.9
  64.7 0.6 copy-done.9
  65.4 1.5 %shard_map.134 = f32[12,1,759]{2,1,0:T(1,128)} custom-call(f32[32,384]{1,0:T(8,128)} %copy-done.2, f32[32,384]{1,0:T(8,128)} %copy-done.9), custom_call_target="tpu_custom_call" | custom-call | flops 100000 | bytes 100000 | tf_op jit(solution)/shard_map/pallas_call | solution.py:518
  66.8 0.3 collective-permute-done.4
  67.1 0.3 maximum_bitcast_fusion
  67.4 0.9 %slice_bitcast_fusion = (bf16[4,6,12,384]{3,0,2,1:T(4,128)(2,1)}, bf16[4,6,12,384]{3,0,2,1:T(4,128)(2,1)}) fusion(bf16[2,4,6,12,384]{4,1,3,2,0:T(4,128)(2,1)S(1)} %maximum_bitcast_fusion), kind=kLoop, calls=%fused_computation.2 | loop fusion | bytes 884736 | tf_op jit(solution)/shard_map/squeeze | solution.py:526
  68.3 7.5 %all-to-all-done.1 = bf16[16,8,384]{2,1,0:T(8,128)(2,1)S(1)} async-done(((bf16[16,8,384]{2,1,0:T(8,128)(2,1)}), bf16[16,8,384]{2,1,0:T(8,128)(2,1)S(1)}, u32[]{:S(2)}, u32[]{:S(2)}) %all-to-all-start.1) | async-done | bytes 98336 | tf_op jit(solution)/shard_map/all_to_all | solution.py:516
  75.9 0.6 convert_reduce_fusion.1
  76.5 0.6 convert_reduce_fusion
  (3 shorter events, 0.0 us)
Async XLA Ops:
  2.7 14.6 %collective-permute-start = (bf16[2,3,12,4,384]{4,3,2,1,0:T(4,128)(2,1)S(1)}, bf16[2,3,12,4,384]{4,3,2,1,0:T(4,128)(2,1)S(1)}, u32[]{:S(2)}, u32[]{:S(2)}) collective-permute-start(bf16[2,3,12,4,384]{4,3,2,1,0:T(4,128)(2,1)S(1)} %pad_maximum_fusion.1), channel_id=1, source_target_pairs={{0,240},{16,0},{32,16},{48,32},{64,48},{80,64},{96,80},{112,96},{1... | collective-permute-start | bytes 663560 | tf_op jit(solution)/shard_map/ppermute | solution.py:39
  10.3 0.9 %copy-start.5 = (s32[144,144]{1,0:T(8,128)S(1)}, s32[144,144]{1,0:T(8,128)}, u32[]{:S(2)}) copy-start(s32[144,144]{1,0:T(8,128)} %ids_ref.1) | copy-start | bytes 248836
  11.2 0.8 copy-start.7
  11.9 5.2 %copy-start = (bf16[4,6,12,384]{3,0,2,1:T(4,128)(2,1)S(1)}, bf16[4,6,12,384]{3,0,2,1:T(4,128)(2,1)}, u32[]{:S(2)}) copy-start(bf16[4,6,12,384]{3,0,2,1:T(4,128)(2,1)} %param.9) | copy-start | bytes 663556
  11.9 5.2 %copy-start.1 = (bf16[4,6,12,384]{3,0,2,1:T(4,128)(2,1)S(1)}, bf16[4,6,12,384]{3,0,2,1:T(4,128)(2,1)}, u32[]{:S(2)}) copy-start(bf16[4,6,12,384]{3,0,2,1:T(4,128)(2,1)} %param.10) | copy-start | bytes 663556
  11.9 6.2 %copy-start.10 = (bf16[384]{0:T(512)(128)(2,1)S(1)}, bf16[384]{0:T(512)(128)(2,1)}, u32[]{:S(2)}) copy-start(bf16[384]{0:T(512)(128)(2,1)} %param.12) | copy-start | bytes 2308
  11.9 6.2 %copy-start.11 = (bf16[384]{0:T(512)(128)(2,1)S(1)}, bf16[384]{0:T(512)(128)(2,1)}, u32[]{:S(2)}) copy-start(bf16[384]{0:T(512)(128)(2,1)} %param.13) | copy-start | bytes 2308
  11.9 9.6 %copy-start.3 = (bf16[1152,384]{1,0:T(8,128)(2,1)S(1)}, bf16[1152,384]{1,0:T(8,128)(2,1)}, u32[]{:S(2)}) copy-start(bf16[1152,384]{1,0:T(8,128)(2,1)} %wqkv_in_ref.1) | copy-start | bytes 2654212
  12.0 9.6 %copy-start.4 = (bf16[384,384]{1,0:T(8,128)(2,1)S(1)}, bf16[384,384]{1,0:T(8,128)(2,1)}, u32[]{:S(2)}) copy-start(bf16[384,384]{1,0:T(8,128)(2,1)} %wout_ref.3) | copy-start | bytes 884740
  12.0 9.6 %copy-start.8 = (s32[2,1,1]{0,2,1:T(1,128)S(1)}, s32[2,1,1]{0,2,1:T(1,128)}, u32[]{:S(2)}) copy-start(s32[2,1,1]{0,2,1:T(1,128)} %param.11) | copy-start | bytes 28
  17.5 4.1 %collective-permute-start.1 = (bf16[2,6,6,4,384]{4,3,2,1,0:T(4,128)(2,1)S(1)}, bf16[2,6,6,4,384]{4,3,2,1,0:T(4,128)(2,1)S(1)}, u32[]{:S(2)}, u32[]{:S(2)}) collective-permute-start(bf16[2,6,6,4,384]{4,3,2,1,0:T(4,128)(2,1)S(1)} %pad_maximum_fusion.2), channel_id=1, source_target_pairs={{0,15},{1,0},{2,1},{3,2},{4,3},{5,4},{6,5},{7,6},{8,7},{9,8},{10,9... | collective-permute-start | bytes 663560 | tf_op jit(solution)/shard_map/ppermute | solution.py:39
  30.7 5.8 %collective-permute-start.2 = (bf16[8,104,384]{2,1,0:T(8,128)(2,1)S(1)}, bf16[8,104,384]{2,1,0:T(8,128)(2,1)S(1)}, u32[]{:S(2)}, u32[]{:S(2)}) collective-permute-start(bf16[8,104,384]{2,1,0:T(8,128)(2,1)S(1)} %get-tuple-element.37), channel_id=1, source_target_pairs={{0,1},{1,0},{2,3},{3,2},{4,5},{5,4},{6,7},{7,6},{8,9},{9,8},{10,11... | collective-permute-start | bytes 1916936 | tf_op jit(solution)/shard_map/ppermute | solution.py:460
  33.0 0.9 %copy-start.6 = (s32[144,144]{1,0:T(8,128)S(1)}, s32[144,144]{1,0:T(8,128)}, u32[]{:S(2)}) copy-start(s32[144,144]{1,0:T(8,128)} %ids_ref.1) | copy-start | bytes 248836
  33.5 5.6 %collective-permute-start.3 = (bf16[2,6,6,4,384]{4,3,2,1,0:T(4,128)(2,1)S(1)}, bf16[2,6,6,4,384]{4,3,2,1,0:T(4,128)(2,1)S(1)}, u32[]{:S(2)}, u32[]{:S(2)}) collective-permute-start(bf16[2,6,6,4,384]{4,3,2,1,0:T(4,128)(2,1)S(1)} %get-tuple-element.45), channel_id=1, source_target_pairs={{0,1},{1,2},{2,3},{3,4},{4,5},{5,6},{6,7},{7,8},{8,9},{9,10},{10,1... | collective-permute-start | bytes 663560 | tf_op jit(solution)/shard_map/ppermute | solution.py:39
  39.1 17.5 %all-to-all-start = ((bf16[8,128,384]{2,1,0:T(8,128)(2,1)}), bf16[8,128,384]{2,1,0:T(8,128)(2,1)S(1)}, u32[]{:S(2)}, u32[]{:S(2)}) async-start(bf16[8,128,384]{2,1,0:T(8,128)(2,1)} %shard_map.132), calls=%async_computation | async-start | bytes 1572864 | tf_op jit(solution)/shard_map/all_to_all | solution.py:501
  57.3 7.4 %copy-start.2 = (f32[32,384]{1,0:T(8,128)}, f32[32,384]{1,0:T(8,128)S(1)}, u32[]{:S(2)}) copy-start(f32[32,384]{1,0:T(8,128)S(1)} %get-tuple-element.52.mine_ref) | copy-start | bytes 147460
  57.5 9.6 %collective-permute-start.4 = (bf16[2,3,12,4,384]{4,3,2,1,0:T(4,128)(2,1)S(1)}, bf16[2,3,12,4,384]{4,3,2,1,0:T(4,128)(2,1)S(1)}, u32[]{:S(2)}, u32[]{:S(2)}) collective-permute-start(bf16[2,3,12,4,384]{4,3,2,1,0:T(4,128)(2,1)S(1)} %get-tuple-element.59), channel_id=1, source_target_pairs={{0,16},{16,32},{32,48},{48,64},{64,80},{80,96},{96,112},{112,128},... | collective-permute-start | bytes 663560 | tf_op jit(solution)/shard_map/ppermute | solution.py:39
  57.6 7.1 %collective-permute-start.5 = (f32[32,384]{1,0:T(8,128)S(1)}, f32[32,384]{1,0:T(8,128)S(1)}, u32[]{:S(2)}, u32[]{:S(2)}) collective-permute-start(f32[32,384]{1,0:T(8,128)S(1)} %get-tuple-element.52.mine_ref), channel_id=1, source_target_pairs={{0,1},{1,0},{2,3},{3,2},{4,5},{5,4},{6,7},{7,6},{8,9},{9,8},{10,11... | collective-permute-start | bytes 147464 | tf_op jit(solution)/shard_map/ppermute | solution.py:460
  57.7 18.2 %all-to-all-start.1 = ((bf16[16,8,384]{2,1,0:T(8,128)(2,1)}), bf16[16,8,384]{2,1,0:T(8,128)(2,1)S(1)}, u32[]{:S(2)}, u32[]{:S(2)}) async-start(bf16[16,8,384]{2,1,0:T(8,128)(2,1)} %get-tuple-element.50), calls=%async_computation.1 | async-start | bytes 196608 | tf_op jit(solution)/shard_map/all_to_all | solution.py:516
  64.7 0.6 copy-start.9

commit v5 on v4

--- a/solution.py
+++ b/solution.py
@@ -109,8 +109,8 @@
     igrad_ref,
     keep_ref,
     give_ref,
-    bg_ref,
-    bt_ref,
+    bgk_ref,
+    bgg_ref,
     x_ref,
     c_ref,
     std_ref,
@@ -121,6 +121,8 @@
     gq_ref,
     gkt_ref,
     gvt_ref,
+    bg_ref,
+    bt_ref,
     wqkv_ref,
     sem,
     mix_ref,
@@ -230,6 +232,19 @@
             gq_ref[rows, cols] = (gq_sum * scale).astype(low)
 
     mixed = mixed_ref[...]
+
+    core = place_ref[0]
+    for i in range(6):
+        halves = []
+        for head in (i, i + 6):
+            tail = [bt_ref[head, pl.ds(k, 18, stride=8), :][:, 0:16] for k in range(8)]
+            blank = jnp.zeros((14, LANES), wide)
+            halves.append(
+                jnp.concatenate([bg_ref[head], jnp.concatenate(tail, axis=1), blank], axis=0)
+            )
+        bgk_ref[i] = jnp.where(core == 0, halves[0], halves[1])
+        bgg_ref[i] = jnp.where(core == 0, halves[1], halves[0]).astype(low)
+
     gq = gq_ref[...]
     gk = jnp.concatenate([gkt_ref[w].T for w in range(2)], axis=0)
     gv = jnp.concatenate([gvt_ref[w].T for w in range(2)], axis=0)
@@ -286,31 +301,30 @@
     put_back(1, igrad_ref[...].astype(wide))
 
 
-def table_kernel(bg_ref, bt_ref, ids_ref, sums_ref, rem_ref, near_ref, tail_ref, rest_ref):
-    slot = lax.broadcasted_iota(jnp.int32, (QSLOTS, LANES), 0)
-    spot = lax.broadcasted_iota(jnp.int32, (LANES, LANES), 0)
+def table_kernel(mine_ref, other_ref, ids_ref, sums_ref, total_ref, near_ref, tail_ref, rest_ref):
+    slot = lax.broadcasted_iota(jnp.int32, (2 * QSLOTS, LANES), 0)
+    slot = jnp.where(slot < QSLOTS, 2 * slot, 2 * (slot - QSLOTS) + 1)
+    spot = lax.broadcasted_iota(jnp.int32, (LANES // 2, LANES), 0)
     near_ref[...] = ids_ref[:, 0:LANES]
     tail_ref[:, 0:16] = ids_ref[:, LANES:WIN_TOK]
     rest_ref[...] = jnp.concatenate(
         [tail_ref[pl.ds(k, 18, stride=8), :][:, 0:16] for k in range(8)], axis=1
     )
-    for head in range(HEADS):
-        rem_ref[head] = jnp.concatenate(
-            [bt_ref[head, pl.ds(k, 18, stride=8), :][:, 0:16] for k in range(8)], axis=1
-        )
+    total_ref[...] = mine_ref[...] + other_ref[...].astype(wide)
 
     def one_step(step, acc):
         lefts = []
         rights = []
         for s in range(9):
             if s < 8:
-                ids = near_ref[pl.ds(step * 8 + s, 1), :]
-                vals = [bg_ref[head, pl.ds(step * 8 + s, 1), :] for head in range(HEADS)]
+                row = step * 8 + s
+                ids = near_ref[pl.ds(row, 1), :]
             else:
+                row = WIN_TOK + step
                 ids = rest_ref[pl.ds(step, 1), :]
-                vals = [rem_ref[head, pl.ds(step, 1), :] for head in range(HEADS)]
-            rights.append(((ids & (LANES - 1)) == spot).astype(wide).astype(low))
-            here = (ids >> 7) == slot
+            vals = [total_ref[head, pl.ds(row, 1), :] for head in range(HEADS // 2)]
+            rights.append(((ids & (LANES // 2 - 1)) == spot).astype(wide).astype(low))
+            here = (ids >> 6) == slot
             lefts.append(
                 jnp.concatenate([jnp.where(here, val, 0.0) for val in vals], axis=0).astype(low)
             )
@@ -318,47 +332,56 @@
         right = jnp.concatenate(rights, axis=1)
         return acc + mm(left, right, NT)
 
-    start = jnp.zeros((HEADS * QSLOTS, LANES), wide)
-    sums_ref[...] = lax.fori_loop(0, 18, one_step, start, unroll=6)
+    start = jnp.zeros((HEADS * QSLOTS, LANES // 2), wide)
+    acc = lax.fori_loop(0, 18, one_step, start, unroll=6)
+    for head in range(HEADS // 2):
+        even = acc[2 * QSLOTS * head : 2 * QSLOTS * head + QSLOTS]
+        odd = acc[2 * QSLOTS * head + QSLOTS : 2 * QSLOTS * (head + 1)]
+        sums_ref[QSLOTS * head : QSLOTS * (head + 1), :] = jnp.concatenate([even, odd], axis=1)
 
 
 def pack_kernel(keep_ref, taken_ref, table_ref, send_ref):
     total = keep_ref[0].astype(wide) + taken_ref[0].astype(wide)
     table = table_ref[...]
-    row = lax.broadcasted_iota(jnp.int32, (HEADS * QSLOTS, 1), 0)
+    row = lax.broadcasted_iota(jnp.int32, (HEADS // 2 * QSLOTS, 1), 0)
     for n in range(2):
         for p in range(3):
             piece = total[96 + n : 97 + n, p * LANES : (p + 1) * LANES]
             table = jnp.where(row == QSLOTS * p + 6 + n, piece, table)
-    extra = jnp.concatenate([table[0:32], table[32:64], table[64:96]], axis=1).astype(low)
+    extra = jnp.concatenate([table[0:16], table[16:32], table[32:48]], axis=1).astype(low)
     for m in range(8):
         total = keep_ref[m].astype(wide) + taken_ref[m].astype(wide)
         send_ref[m, 0:96, :] = total[0:96].astype(low)
-        send_ref[m, 96:128, :] = extra
+        send_ref[m, 96:112, :] = extra
 
 
 def sum_kernel(got_ref, second_ref, table_ref):
     total = got_ref[0].astype(wide)
     for m in range(1, 8):
         total = total + got_ref[m].astype(wide)
-    table = total[96:128]
+    extra = total[96:112]
+    table = jnp.concatenate([extra[:, p * LANES : (p + 1) * LANES] for p in range(3)], axis=0)
     table_ref[...] = table
     vectors = jnp.concatenate(
-        [table[QSLOTS * p + 6 : QSLOTS * p + 8, 0:LANES] for p in range(3)], axis=1
+        [table[QSLOTS * p + 6 : QSLOTS * p + 8] for p in range(3)], axis=1
     )
     for a in range(16):
         chunk = jnp.concatenate([total[6 * a : 6 * a + 6], vectors], axis=0)
         second_ref[a] = chunk.astype(low)
 
 
-def spread_kernel(mine_ref, other_ref, table_ref):
-    total = mine_ref[...] + other_ref[...]
+def spread_kernel(place_ref, mine_ref, other_ref, table_ref):
+    mine = mine_ref[...]
+    other = other_ref[...]
+    halves = (
+        jnp.where(place_ref[0] == 0, mine, other),
+        jnp.where(place_ref[0] == 0, other, mine),
+    )
     for head in range(HEADS):
         for q in range(6):
-            spot = head * QSLOTS + q
-            cols = slice(spot // 32 * LANES, (spot // 32 + 1) * LANES)
+            spot = head % 6 * QSLOTS + q
             width = min(LANES, NBIAS - q * LANES)
-            piece = total[spot % 32 : spot % 32 + 1, cols]
+            piece = halves[head // 6][spot : spot + 1, :]
             table_ref[head, :, q * LANES : q * LANES + width] = piece[:, 0:width]
 
 
@@ -407,7 +430,7 @@
     own = jnp.stack((jnp.where(hidden, jnp.bfloat16(MARK), fields[3:, :6]), cotangent[3:, :6]))
     lon_in = passed_along(jnp.concatenate((own, lat_in[:, :, :6]), axis=1), "lon", -1)
 
-    filled, mixed, igrad, keep, give, bias_grad, bias_tail = pl.pallas_call(
+    filled, mixed, igrad, keep, give, pairs, pairs_give = pl.pallas_call(
         main_kernel,
         out_shape=(
             jax.ShapeDtypeStruct((TOK, D), low),
@@ -415,8 +438,8 @@
             jax.ShapeDtypeStruct((TOK, D), low),
             jax.ShapeDtypeStruct((8, CHUNK, D), low),
             jax.ShapeDtypeStruct((8, CHUNK, D), low),
-            jax.ShapeDtypeStruct((HEADS, WIN_TOK, LANES), wide),
-            jax.ShapeDtypeStruct((HEADS, WIN_TOK, LANES), wide),
+            jax.ShapeDtypeStruct((HEADS // 2, 176, LANES), wide),
+            jax.ShapeDtypeStruct((HEADS // 2, 176, LANES), low),
         ),
         in_specs=[smem, smem] + [vmem] * 6 + [hbm, vmem, vmem, vmem],
         out_specs=(vmem,) * 7,
@@ -431,6 +454,8 @@
             pltpu.VMEM((TOK, D), low),
             pltpu.VMEM((2, D, WIN_TOK), low),
             pltpu.VMEM((2, D, WIN_TOK), low),
+            pltpu.VMEM((HEADS, WIN_TOK, LANES), wide),
+            pltpu.VMEM((HEADS, WIN_TOK, LANES), wide),
             pltpu.VMEM((3 * D, D), low),
             pltpu.SemaphoreType.DMA(()),
             pltpu.VMEM((3, TOK, LANES), wide),
@@ -459,7 +484,6 @@
     def swapped(value, bit):
         return lax.ppermute(value, "lon", [(i, i ^ bit) for i in range(size)])
 
-    taken = swapped(give, 1)
     out_own, out_lon = pl.pallas_call(
         out_kernel,
         out_shape=(
@@ -473,24 +497,26 @@
         cost_estimate=pl.CostEstimate(flops=2 * 10**9, bytes_accessed=0, transcendentals=0),
     )(filled, mixed, igrad, out_weight)
     lon_out = passed_along(out_lon, "lon", 1)
-    bias_grad, out_own = lax.optimization_barrier((bias_grad, out_own))
+    give, pairs_give, out_own = lax.optimization_barrier((give, pairs_give, out_own))
+    other_pairs = swapped(pairs_give, 1)
+    taken = swapped(give, 1)
     table = pl.pallas_call(
         table_kernel,
-        out_shape=jax.ShapeDtypeStruct((HEADS * QSLOTS, LANES), wide),
+        out_shape=jax.ShapeDtypeStruct((HEADS // 2 * QSLOTS, LANES), wide),
         in_specs=[vmem] * 3,
         out_specs=vmem,
         scratch_shapes=[
-            pltpu.VMEM((HEADS, 18, LANES), wide),
+            pltpu.VMEM((HEADS // 2, 176, LANES), wide),
             pltpu.VMEM((WIN_TOK, LANES), jnp.int32),
             pltpu.VMEM((WIN_TOK, LANES), jnp.int32),
             pltpu.VMEM((18, LANES), jnp.int32),
         ],
         compiler_params=pltpu.CompilerParams(vmem_limit_bytes=8 * 2**20),
         cost_estimate=pl.CostEstimate(flops=10**9, bytes_accessed=10**6, transcendentals=0),
-    )(bias_grad, bias_tail, bias_index)
+    )(pairs, other_pairs, bias_index)
     pair = pl.pallas_call(
         pack_kernel,
-        out_shape=jax.ShapeDtypeStruct((8, 128, D), low),
+        out_shape=jax.ShapeDtypeStruct((8, 112, D), low),
         in_specs=[vmem] * 3,
         out_specs=vmem,
         compiler_params=pltpu.CompilerParams(vmem_limit_bytes=8 * 2**20),
@@ -503,7 +529,7 @@
         sum_kernel,
         out_shape=(
             jax.ShapeDtypeStruct((16, 8, D), low),
-            jax.ShapeDtypeStruct((32, D), wide),
+            jax.ShapeDtypeStruct((HEADS // 2 * QSLOTS, LANES), wide),
         ),
         in_specs=[vmem],
         out_specs=(vmem, vmem),
@@ -515,13 +541,14 @@
     full, second = lax.optimization_barrier((full, second))
     final = lax.all_to_all(second, "lat", 0, 0, tiled=True)
     lat_out = passed_along(full[:, 3:], "lat", 1)
+    table, _ = lax.optimization_barrier((table, lat_out))
     table_grad = pl.pallas_call(
         spread_kernel,
         out_shape=jax.ShapeDtypeStruct((HEADS, 1, NBIAS), wide),
-        in_specs=[vmem, vmem],
+        in_specs=[smem, vmem, vmem],
         out_specs=vmem,
         cost_estimate=pl.CostEstimate(flops=10**5, bytes_accessed=10**5, transcendentals=0),
-    )(table, swapped(table, 1)).transpose(1, 0, 2)
+    )(place, table, swapped(table, 1)).transpose(1, 0, 2)
     done = jnp.concatenate((lat_out, full[:, :3]), axis=1).transpose(0, 3, 1, 2, 4)
     output, input_grad = done[0], done[1]
     final, output, input_grad, table_grad = lax.optimization_barrier(

time: 78.2 us -> 76.9 us (0.983)
  Pallas kernels: 20.6 us -> 19.7 us
    all_to_all x1, waiting for transfers between devices: 7.55 us -> 5.14 us  [local(): final = lax.all_to_all(second, 'lat', 0, 0, tiled=True)]
    ppermute x2 -> x3, waiting for transfers between devices: 0.01 us -> 1.58 us  [swapped(): return lax.ppermute(value, 'lon', [(i, i ^ bit) for i in range(size)])]
    ppermute x4, waiting for transfers between devices: 5.25 us -> 6.5 us  [passed_along(): return lax.ppermute(value, axis, pairs)]
    pallas_call x2, Pallas kernels: 3.65 us -> 2.75 us  [the longest x1 1.75 us: local(): pl.pallas_call(table_kernel, out_shape=jax.ShapeDtypeStruct((HEADS // 2 *...]
    unnamed x24 -> x26, local copies, waits for them, and re-layouts: 2.46 us -> 2.34 us
    ppermute x2 -> x3, starting transfers between devices: 2.33 us -> 2.33 us  [swapped(): return lax.ppermute(value, 'lon', [(i, i ^ bit) for i in range(size)])]
  transfers between devices with their start and end apart: 8 -> 9, of which waited for: 5 -> 6; matrix products, arithmetic and copies ran while one was open for 2% -> 2% of each run, Pallas kernels for 14% -> 12%
where the time goes in v5:
time: 76.9 us; the launch traced here: 76.5 us
  starting transfers between devices  25.2 us (33%)
  waiting for transfers between devices  23.1 us (30%)
  Pallas kernels  19.7 us (26%)
  other arithmetic  4.04 us (5%)
  local copies, waits for them, and re-layouts  3.62 us (5%)
  between operations  0.81 us (1%)
    all_to_all x1, waiting for transfers between devices, local(): lax.all_to_all(pair, 'lon', 0, 0, axis_index_groups=groups, tiled=True)  9.87 us
    pallas_call x1, Pallas kernels, local(): pl.pallas_call(main_kernel, out_shape=(jax.ShapeDtypeStruct((TOK, D), low...  9.24 us
    ppermute x4, starting transfers between devices, passed_along(): return lax.ppermute(value, axis, pairs)  8.66 us
    all_to_all x1, starting transfers between devices, local(): final = lax.all_to_all(second, 'lat', 0, 0, tiled=True)  7.14 us
    all_to_all x1, starting transfers between devices, local(): lax.all_to_all(pair, 'lon', 0, 0, axis_index_groups=groups, tiled=True)  7.03 us
    ppermute x4, waiting for transfers between devices, passed_along(): return lax.ppermute(value, axis, pairs)  6.5 us
    all_to_all x1, waiting for transfers between devices, local(): final = lax.all_to_all(second, 'lat', 0, 0, tiled=True)  5.14 us
    pallas_call x1, Pallas kernels, local(): pl.pallas_call(pre_kernel, out_shape=(jax.ShapeDtypeStruct((HEADS, WIN_TO...  5.13 us
  transfers between devices with their start and end apart: 9, of which 6 were waited for; matrix products, arithmetic and copies ran while one was open for 2% of the time, Pallas kernels for 12%

profile of v5, /device:TPU:2, one launch (start us, length us, event | category | flops | bytes accessed | tf_op | source)
XLA Modules:
  0.0 76.5 jit_solution(7619372437359828399)
XLA Ops:
  0.6 0.7 broadcast_compare_fusion
  1.3 0.1 broadcast_in_dim.37
  1.4 0.1 eq.18
  1.5 1.1 %slice_bitcast_fusion.2 = (bf16[1,3,12,4,384]{4,3,2,1,0:T(4,128)(2,1)S(1)}, bf16[1,3,12,4,384]{4,3,2,1,0:T(4,128)(2,1)S(1)}) fusion(bf16[6,12,4,384]{3,2,1,0:T(4,128)(2,1)} %bitcast.25, bf16[6,12,4,384]{3,2,1,0:T(4,128)(2,1)} %bitcast.22, pred[4]{0:T(512)(128)(4,1)S(1)} %eq.18), kind=kLoop, calls=%fused_computation.7 | loop fusion | flops 55296 | bytes 442372 | tf_op jit(solution)/shard_map/stack | solution.py:409
  2.5 0.2 pad_maximum_fusion.1
  2.7 7.5 %collective-permute-start = (bf16[2,3,12,4,384]{4,3,2,1,0:T(4,128)(2,1)S(1)}, bf16[2,3,12,4,384]{4,3,2,1,0:T(4,128)(2,1)S(1)}, u32[]{:S(2)}, u32[]{:S(2)}) collective-permute-start(bf16[2,3,12,4,384]{4,3,2,1,0:T(4,128)(2,1)S(1)} %pad_maximum_fusion.1), channel_id=1, source_target_pairs={{0,240},{16,0},{32,16},{48,32},{64,48},{80,64},{96,80},{112,96},{1... | collective-permute-start | bytes 663560 | tf_op jit(solution)/shard_map/ppermute | solution.py:39
  10.2 0.1 pad_add_fusion.place_ref
  10.3 0.0 copy-start.3
  10.3 0.0 copy-start.6
  10.3 0.9 %copy-done.6 = s32[144,144]{1,0:T(8,128)S(1)} copy-done((s32[144,144]{1,0:T(8,128)S(1)}, s32[144,144]{1,0:T(8,128)}, u32[]{:S(2)}) %copy-start.6) | copy-done | bytes 82968
  11.2 0.0 copy-start.8
  11.2 0.8 %copy-done.8 = f32[1,12,759]{2,0,1:T(1,128)S(1)} copy-done((f32[1,12,759]{2,0,1:T(1,128)S(1)}, f32[1,12,759]{2,0,1:T(1,128)}, u32[]{:S(2)}) %copy-start.8) | copy-done | bytes 36456
  11.9 0.0 copy-start
  11.9 0.0 copy-start.1
  11.9 0.0 copy-start.11
  11.9 0.0 copy-start.12
  11.9 0.0 copy-start.4
  12.0 0.0 copy-start.5
  12.0 0.0 copy-start.9
  12.0 5.1 %shard_map.128 = (f32[12,144,256]{2,1,0:T(8,128)S(1)}, bf16[384,384]{1,0:T(8,128)(2,1)S(1)}) custom-call(s32[2]{0:T(128)S(1)} %pad_add_fusion.place_ref, f32[12,1,759]{2,1,0:T(1,128)S(1)} %bitcast.28, s32[144,144]{1,0:T(8,128)S(1)} %copy-done.6), custom_call_target="tpu_custom_call" | custom-call | flops 5000000000 | tf_op jit(solution)/shard_map/pallas_call | solution.py:411
  17.1 0.0 copy-done
  17.1 0.0 copy-done.1
  17.1 0.1 slice_bitcast_fusion.3
  17.2 0.0 collective-permute-done.lat_ref
  17.3 0.2 pad_maximum_fusion.2
  17.5 0.7 collective-permute-start.1
  18.1 0.0 copy-done.11
  18.1 0.0 copy-done.12
  18.2 3.4 %collective-permute-done.1.lon_ref = bf16[2,6,6,4,384]{4,3,2,1,0:T(4,128)(2,1)S(1)} collective-permute-done((bf16[2,6,6,4,384]{4,3,2,1,0:T(4,128)(2,1)S(1)}, bf16[2,6,6,4,384]{4,3,2,1,0:T(4,128)(2,1)S(1)}, u32[]{:S(2)}, u32[]{:S(2)}) %collective-permute-start.1) | collective-permute-done | bytes 221216 | tf_op jit(solution)/shard_map/ppermute | solution.py:39
  21.6 0.0 copy-done.3
  21.6 0.0 copy-done.4
  21.6 0.0 copy-done.5
  21.6 0.0 copy-done.9
  21.6 9.2 %shard_map.129 = (bf16[288,384]{1,0:T(8,128)(2,1)S(1)}, bf16[288,384]{1,0:T(8,128)(2,1)S(1)}, bf16[288,384]{1,0:T(8,128)(2,1)S(1)}, bf16[8,104,384]{2,1,0:T(8,12...) custom-call(s32[2]{0:T(128)S(1)} %pad_add_fusion.place_ref, ...), custom_call_target="tpu_custom_call" | custom-call | flops 10000000000 | tf_op jit(solution)/shard_map/pallas_call | solution.py:433
  30.8 0.0 copy-start.7
  30.9 0.5 shard_map.130
  31.4 2.2 %collective-permute-start.2 = (bf16[8,104,384]{2,1,0:T(8,128)(2,1)S(1)}, bf16[8,104,384]{2,1,0:T(8,128)(2,1)S(1)}, u32[]{:S(2)}, u32[]{:S(2)}) collective-permute-start(bf16[8,104,384]{2,1,0:T(8,128)(2,1)S(1)} %get-tuple-element.45), channel_id=1, source_target_pairs={{0,1},{1,0},{2,3},{3,2},{4,5},{5,4},{6,7},{7,6},{8,9},{9,8},{10,11... | collective-permute-start | bytes 1916936 | tf_op jit(solution)/shard_map/ppermute | solution.py:485
  33.6 0.1 collective-permute-start.3
  33.7 0.4 collective-permute-start.4
  34.1 1.6 %collective-permute-done.3.other_ref = bf16[6,176,128]{2,1,0:T(8,128)(2,1)S(1)} collective-permute-done((bf16[6,176,128]{2,1,0:T(8,128)(2,1)S(1)}, bf16[6,176,128]{2,1,0:T(8,128)(2,1)S(1)}, u32[]{:S(2)}, u32[]{:S(2)}) %collective-permute-start.3) | collective-permute-done | bytes 270368 | tf_op jit(solution)/shard_map/ppermute | solution.py:485
  35.7 0.0 copy-done.7
  35.7 1.7 %shard_map.131.table_ref = f32[48,128]{1,0:T(8,128)S(1)} custom-call(f32[6,176,128]{2,1,0:T(8,128)S(1)} %get-tuple-element.46.mine_ref, bf16[6,176,128]{2,1,0:T(8,128)(2,1)S(1)} %collective-permute-done.3.other_ref, s32[144,144]{1,0:T(8,128)S(1)} %copy-done.7), custom_call_target="tpu_custom_call" | custom-call | flops 1000000000 | bytes 1000000 | tf_op jit(solution)/shard_map/pallas_call | solution.py:503
  37.4 0.0 collective-permute-done.2.taken_ref
  37.4 1.0 %shard_map.132 = bf16[8,112,384]{2,1,0:T(8,128)(2,1)} custom-call(bf16[8,104,384]{2,1,0:T(8,128)(2,1)S(1)} %get-tuple-element.38.keep_ref, bf16[8,104,384]{2,1,0:T(8,128)(2,1)S(1)} %collective-permute-done.2.taken_ref, f32[48,128]{1,0:T(8,128)S(1)} %shard_map.131.table_ref), custom_call_target="tpu_custom_call" | custom-call | flops 1000000 | bytes 1000000 | tf_op jit(solution)/shard_map/pallas_call | solution.py:517
  38.4 0.6 collective-permute-done.4
  39.0 7.0 %all-to-all-start = ((bf16[8,112,384]{2,1,0:T(8,128)(2,1)}), bf16[8,112,384]{2,1,0:T(8,128)(2,1)S(1)}, u32[]{:S(2)}, u32[]{:S(2)}) async-start(bf16[8,112,384]{2,1,0:T(8,128)(2,1)} %shard_map.132), calls=%async_computation | async-start | bytes 1376256 | tf_op jit(solution)/shard_map/all_to_all | solution.py:527
  46.1 0.3 pad_maximum_fusion
  46.4 9.9 %all-to-all-done.got_ref = bf16[8,112,384]{2,1,0:T(8,128)(2,1)S(1)} async-done(((bf16[8,112,384]{2,1,0:T(8,128)(2,1)}), bf16[8,112,384]{2,1,0:T(8,128)(2,1)S(1)}, u32[]{:S(2)}, u32[]{:S(2)}) %all-to-all-start) | async-done | bytes 688160 | tf_op jit(solution)/shard_map/all_to_all | solution.py:527
  56.2 0.7 shard_map.133
  57.0 0.0 copy-start.2
  57.0 0.2 fusion.2
  57.1 0.1 collective-permute-start.5
  57.2 7.1 %all-to-all-start.1 = ((bf16[16,8,384]{2,1,0:T(8,128)(2,1)}), bf16[16,8,384]{2,1,0:T(8,128)(2,1)S(1)}, u32[]{:S(2)}, u32[]{:S(2)}) async-start(bf16[16,8,384]{2,1,0:T(8,128)(2,1)} %get-tuple-element.53), calls=%async_computation.1 | async-start | bytes 196608 | tf_op jit(solution)/shard_map/all_to_all | solution.py:542
  64.4 2.5 %collective-permute-done.5 = bf16[2,3,12,4,384]{4,3,2,1,0:T(4,128)(2,1)S(1)} collective-permute-done((bf16[2,3,12,4,384]{4,3,2,1,0:T(4,128)(2,1)S(1)}, bf16[2,3,12,4,384]{4,3,2,1,0:T(4,128)(2,1)S(1)}, u32[]{:S(2)}, u32[]{:S(2)}) %collective-permute-start.5) | collective-permute-done | bytes 221216 | tf_op jit(solution)/shard_map/ppermute | solution.py:39
  66.8 0.0 collective-permute-start.6
  66.8 0.3 maximum_bitcast_fusion
  67.1 0.9 %slice_bitcast_fusion = (bf16[4,6,12,384]{3,0,2,1:T(4,128)(2,1)}, bf16[4,6,12,384]{3,0,2,1:T(4,128)(2,1)}) fusion(bf16[2,4,6,12,384]{4,1,3,2,0:T(4,128)(2,1)S(1)} %maximum_bitcast_fusion), kind=kLoop, calls=%fused_computation.2 | loop fusion | bytes 884736 | tf_op jit(solution)/shard_map/squeeze | solution.py:553
  68.0 0.0 collective-permute-done.6.other_ref
  68.0 0.0 copy-done.2
  68.0 0.6 copy-done.10
  68.7 1.4 %shard_map.134 = f32[12,1,759]{2,1,0:T(1,128)} custom-call(s32[2]{0:T(128)} %copy-done.3, f32[48,128]{1,0:T(8,128)} %copy-done.2, f32[48,128]{1,0:T(8,128)} %copy-done.10), custom_call_target="tpu_custom_call" | custom-call | flops 100000 | bytes 100000 | tf_op jit(solution)/shard_map/pallas_call | solution.py:545
  70.1 5.1 %all-to-all-done.1 = bf16[16,8,384]{2,1,0:T(8,128)(2,1)S(1)} async-done(((bf16[16,8,384]{2,1,0:T(8,128)(2,1)}), bf16[16,8,384]{2,1,0:T(8,128)(2,1)S(1)}, u32[]{:S(2)}, u32[]{:S(2)}) %all-to-all-start.1) | async-done | bytes 98336 | tf_op jit(solution)/shard_map/all_to_all | solution.py:542
  75.2 0.6 convert_reduce_fusion.1
  75.8 0.6 convert_reduce_fusion
  (4 shorter events, 0.0 us)
Async XLA Ops:
  2.7 14.6 %collective-permute-start = (bf16[2,3,12,4,384]{4,3,2,1,0:T(4,128)(2,1)S(1)}, bf16[2,3,12,4,384]{4,3,2,1,0:T(4,128)(2,1)S(1)}, u32[]{:S(2)}, u32[]{:S(2)}) collective-permute-start(bf16[2,3,12,4,384]{4,3,2,1,0:T(4,128)(2,1)S(1)} %pad_maximum_fusion.1), channel_id=1, source_target_pairs={{0,240},{16,0},{32,16},{48,32},{64,48},{80,64},{96,80},{112,96},{1... | collective-permute-start | bytes 663560 | tf_op jit(solution)/shard_map/ppermute | solution.py:39
  10.3 11.3 %copy-start.3 = (s32[2]{0:T(128)}, s32[2]{0:T(128)S(1)}, u32[]{:S(2)}) copy-start(s32[2]{0:T(128)S(1)} %pad_add_fusion.place_ref) | copy-start | bytes 28
  10.3 0.9 %copy-start.6 = (s32[144,144]{1,0:T(8,128)S(1)}, s32[144,144]{1,0:T(8,128)}, u32[]{:S(2)}) copy-start(s32[144,144]{1,0:T(8,128)} %ids_ref.1) | copy-start | bytes 248836
  11.2 0.8 %copy-start.8 = (f32[1,12,759]{2,0,1:T(1,128)S(1)}, f32[1,12,759]{2,0,1:T(1,128)}, u32[]{:S(2)}) copy-start(f32[1,12,759]{2,0,1:T(1,128)} %param.16) | copy-start | bytes 109300
  11.9 5.2 %copy-start = (bf16[4,6,12,384]{3,0,2,1:T(4,128)(2,1)S(1)}, bf16[4,6,12,384]{3,0,2,1:T(4,128)(2,1)}, u32[]{:S(2)}) copy-start(bf16[4,6,12,384]{3,0,2,1:T(4,128)(2,1)} %param.9) | copy-start | bytes 663556
  11.9 5.2 %copy-start.1 = (bf16[4,6,12,384]{3,0,2,1:T(4,128)(2,1)S(1)}, bf16[4,6,12,384]{3,0,2,1:T(4,128)(2,1)}, u32[]{:S(2)}) copy-start(bf16[4,6,12,384]{3,0,2,1:T(4,128)(2,1)} %param.10) | copy-start | bytes 663556
  11.9 6.2 %copy-start.11 = (bf16[384]{0:T(512)(128)(2,1)S(1)}, bf16[384]{0:T(512)(128)(2,1)}, u32[]{:S(2)}) copy-start(bf16[384]{0:T(512)(128)(2,1)} %param.12) | copy-start | bytes 2308
  11.9 6.2 %copy-start.12 = (bf16[384]{0:T(512)(128)(2,1)S(1)}, bf16[384]{0:T(512)(128)(2,1)}, u32[]{:S(2)}) copy-start(bf16[384]{0:T(512)(128)(2,1)} %param.13) | copy-start | bytes 2308
  11.9 9.6 %copy-start.4 = (bf16[1152,384]{1,0:T(8,128)(2,1)S(1)}, bf16[1152,384]{1,0:T(8,128)(2,1)}, u32[]{:S(2)}) copy-start(bf16[1152,384]{1,0:T(8,128)(2,1)} %wqkv_in_ref.1) | copy-start | bytes 2654212
  12.0 9.6 %copy-start.5 = (bf16[384,384]{1,0:T(8,128)(2,1)S(1)}, bf16[384,384]{1,0:T(8,128)(2,1)}, u32[]{:S(2)}) copy-start(bf16[384,384]{1,0:T(8,128)(2,1)} %wout_ref.3) | copy-start | bytes 884740
  12.0 9.6 %copy-start.9 = (s32[2,1,1]{0,2,1:T(1,128)S(1)}, s32[2,1,1]{0,2,1:T(1,128)}, u32[]{:S(2)}) copy-start(s32[2,1,1]{0,2,1:T(1,128)} %param.11) | copy-start | bytes 28
  17.5 4.1 %collective-permute-start.1 = (bf16[2,6,6,4,384]{4,3,2,1,0:T(4,128)(2,1)S(1)}, bf16[2,6,6,4,384]{4,3,2,1,0:T(4,128)(2,1)S(1)}, u32[]{:S(2)}, u32[]{:S(2)}) collective-permute-start(bf16[2,6,6,4,384]{4,3,2,1,0:T(4,128)(2,1)S(1)} %pad_maximum_fusion.2), channel_id=1, source_target_pairs={{0,15},{1,0},{2,1},{3,2},{4,3},{5,4},{6,5},{7,6},{8,7},{9,8},{10,9... | collective-permute-start | bytes 663560 | tf_op jit(solution)/shard_map/ppermute | solution.py:39
  30.8 4.8 %copy-start.7 = (s32[144,144]{1,0:T(8,128)S(1)}, s32[144,144]{1,0:T(8,128)}, u32[]{:S(2)}) copy-start(s32[144,144]{1,0:T(8,128)} %ids_ref.1) | copy-start | bytes 248836
  31.4 6.1 %collective-permute-start.2 = (bf16[8,104,384]{2,1,0:T(8,128)(2,1)S(1)}, bf16[8,104,384]{2,1,0:T(8,128)(2,1)S(1)}, u32[]{:S(2)}, u32[]{:S(2)}) collective-permute-start(bf16[8,104,384]{2,1,0:T(8,128)(2,1)S(1)} %get-tuple-element.45), channel_id=1, source_target_pairs={{0,1},{1,0},{2,3},{3,2},{4,5},{5,4},{6,7},{7,6},{8,9},{9,8},{10,11... | collective-permute-start | bytes 1916936 | tf_op jit(solution)/shard_map/ppermute | solution.py:485
  33.6 2.1 %collective-permute-start.3 = (bf16[6,176,128]{2,1,0:T(8,128)(2,1)S(1)}, bf16[6,176,128]{2,1,0:T(8,128)(2,1)S(1)}, u32[]{:S(2)}, u32[]{:S(2)}) collective-permute-start(bf16[6,176,128]{2,1,0:T(8,128)(2,1)S(1)} %get-tuple-element.47), channel_id=1, source_target_pairs={{0,1},{1,0},{2,3},{3,2},{4,5},{5,4},{6,7},{7,6},{8,9},{9,8},{10,11... | collective-permute-start | bytes 811016 | tf_op jit(solution)/shard_map/ppermute | solution.py:485
  33.7 5.4 %collective-permute-start.4 = (bf16[2,6,6,4,384]{4,3,2,1,0:T(4,128)(2,1)S(1)}, bf16[2,6,6,4,384]{4,3,2,1,0:T(4,128)(2,1)S(1)}, u32[]{:S(2)}, u32[]{:S(2)}) collective-permute-start(bf16[2,6,6,4,384]{4,3,2,1,0:T(4,128)(2,1)S(1)} %get-tuple-element.48), channel_id=1, source_target_pairs={{0,1},{1,2},{2,3},{3,4},{4,5},{5,6},{6,7},{7,8},{8,9},{9,10},{10,1... | collective-permute-start | bytes 663560 | tf_op jit(solution)/shard_map/ppermute | solution.py:39
  39.0 17.2 %all-to-all-start = ((bf16[8,112,384]{2,1,0:T(8,128)(2,1)}), bf16[8,112,384]{2,1,0:T(8,128)(2,1)S(1)}, u32[]{:S(2)}, u32[]{:S(2)}) async-start(bf16[8,112,384]{2,1,0:T(8,128)(2,1)} %shard_map.132), calls=%async_computation | async-start | bytes 1376256 | tf_op jit(solution)/shard_map/all_to_all | solution.py:527
  57.0 11.1 %copy-start.2 = (f32[48,128]{1,0:T(8,128)}, f32[48,128]{1,0:T(8,128)S(1)}, u32[]{:S(2)}) copy-start(f32[48,128]{1,0:T(8,128)S(1)} %get-tuple-element.56.mine_ref) | copy-start | bytes 73732
  57.1 9.7 %collective-permute-start.5 = (bf16[2,3,12,4,384]{4,3,2,1,0:T(4,128)(2,1)S(1)}, bf16[2,3,12,4,384]{4,3,2,1,0:T(4,128)(2,1)S(1)}, u32[]{:S(2)}, u32[]{:S(2)}) collective-permute-start(bf16[2,3,12,4,384]{4,3,2,1,0:T(4,128)(2,1)S(1)} %get-tuple-element.63), channel_id=1, source_target_pairs={{0,16},{16,32},{32,48},{48,64},{64,80},{80,96},{96,112},{112,128},... | collective-permute-start | bytes 663560 | tf_op jit(solution)/shard_map/ppermute | solution.py:39
  57.2 18.0 %all-to-all-start.1 = ((bf16[16,8,384]{2,1,0:T(8,128)(2,1)}), bf16[16,8,384]{2,1,0:T(8,128)(2,1)S(1)}, u32[]{:S(2)}, u32[]{:S(2)}) async-start(bf16[16,8,384]{2,1,0:T(8,128)(2,1)} %get-tuple-element.53), calls=%async_computation.1 | async-start | bytes 196608 | tf_op jit(solution)/shard_map/all_to_all | solution.py:542
  66.8 1.2 %collective-permute-start.6 = (f32[48,128]{1,0:T(8,128)S(1)}, f32[48,128]{1,0:T(8,128)S(1)}, u32[]{:S(2)}, u32[]{:S(2)}) collective-permute-start(f32[48,128]{1,0:T(8,128)S(1)} %get-tuple-element.56.mine_ref), channel_id=1, source_target_pairs={{0,1},{1,0},{2,3},{3,2},{4,5},{5,4},{6,7},{7,6},{8,9},{9,8},{10,11... | collective-permute-start | bytes 73736 | tf_op jit(solution)/shard_map/ppermute | solution.py:485
  68.0 0.6 copy-start.10

commit v6 on v5

--- a/solution.py
+++ b/solution.py
@@ -186,50 +186,71 @@
     lane = lax.broadcasted_iota(jnp.int32, (1, LANES), 1) // HEAD_DIM
     scale = HEAD_DIM ** (-0.5)
     masks = [(lane == sub).astype(low) for sub in range(4)]
-    for group in range(3):
+    totals = [None] * HEADS
+
+    def first_products(group, w):
+        rows = slice(w * WIN_TOK, (w + 1) * WIN_TOK)
+        q = qkv_ref[rows, group * LANES : (group + 1) * LANES]
+        k = qkv_ref[rows, D + group * LANES : D + (group + 1) * LANES]
+        v = qkv_ref[rows, 2 * D + group * LANES : 2 * D + (group + 1) * LANES]
+        g = gm_ref[rows, group * LANES : (group + 1) * LANES]
+        g_four = jnp.concatenate([g * mask for mask in masks], axis=0)
+        scores = mm(jnp.concatenate([q * mask for mask in masks], axis=0), k, NT)
+        return k, v, g_four, scores, mm(g_four, v, NT)
+
+    def weights_of(group, w, k, v, g_four, scores, grad_attn):
+        biases = jnp.concatenate(
+            [bias_ref[group * 4 + sub, :, 0:WIN_TOK] for sub in range(4)], axis=0
+        )
+        scores = scores * (scale * LOG2E) + biases
+        scores = jnp.where(apart[w], BLOCKED * LOG2E, scores)
+        top = jnp.max(scores, axis=-1, keepdims=True)
+        expo = jnp.exp2(scores - top)
+        prob = (expo * (1.0 / jnp.sum(expo, axis=-1, keepdims=True))).astype(low)
+        return k, g_four, grad_attn, prob, mm(prob, v, NN)
+
+    def score_grads(group, w, k, g_four, grad_attn, prob, mixed):
+        delta = jnp.sum(g_four.astype(wide) * mixed, axis=-1, keepdims=True)
+        grad = prob.astype(wide) * (grad_attn - delta)
+        for sub in range(4):
+            head = group * 4 + sub
+            part = slice(sub * WIN_TOK, (sub + 1) * WIN_TOK)
+            if w == 0:
+                totals[head] = grad[part]
+            else:
+                total = totals[head] + grad[part]
+                bg_ref[head] = total[:, 0:LANES]
+                bt_ref[head, :, 0:16] = total[:, LANES:WIN_TOK]
+        return k, prob, mixed, grad.astype(low)
+
+    def last_products(group, w, k, prob, mixed, glow):
         cols = slice(group * LANES, (group + 1) * LANES)
-        kcols = slice(D + group * LANES, D + (group + 1) * LANES)
-        vcols = slice(2 * D + group * LANES, 2 * D + (group + 1) * LANES)
-        totals = [None] * 4
-        for w in range(2):
-            rows = slice(w * WIN_TOK, (w + 1) * WIN_TOK)
-            q = qkv_ref[rows, cols]
-            k = qkv_ref[rows, kcols]
-            v = qkv_ref[rows, vcols]
-            g = gm_ref[rows, cols]
-            q_four = jnp.concatenate([q * mask for mask in masks], axis=0)
-            g_four = jnp.concatenate([g * mask for mask in masks], axis=0)
-            biases = jnp.concatenate(
-                [bias_ref[group * 4 + sub, :, 0:WIN_TOK] for sub in range(4)], axis=0
-            )
-            scores = mm(q_four, k, NT) * (scale * LOG2E) + biases
-            scores = jnp.where(apart[w], BLOCKED * LOG2E, scores)
-            top = jnp.max(scores, axis=-1, keepdims=True)
-            expo = jnp.exp2(scores - top)
-            prob = (expo * (1.0 / jnp.sum(expo, axis=-1, keepdims=True))).astype(low)
-            mixed = mm(prob, v, NN)
-            delta = jnp.sum(g_four.astype(wide) * mixed, axis=-1, keepdims=True)
-            grad = prob.astype(wide) * (mm(g_four, v, NT) - delta)
-            glow = grad.astype(low)
-            gq = mm(glow, k, NN)
-            mixed_sum = jnp.zeros((WIN_TOK, LANES), wide)
-            gq_sum = jnp.zeros((WIN_TOK, LANES), wide)
-            for sub in range(4):
-                head = group * 4 + sub
-                feats = slice(head * HEAD_DIM, (head + 1) * HEAD_DIM)
-                part = slice(sub * WIN_TOK, (sub + 1) * WIN_TOK)
-                mixed_sum = jnp.where(lane == sub, mixed[part], mixed_sum)
-                gq_sum = jnp.where(lane == sub, gq[part], gq_sum)
-                gvt_ref[w, feats, :] = mm(gmt_ref[w, feats, :], prob[part], NN).astype(low)
-                gkt_ref[w, feats, :] = (mm(qt_ref[w, feats, :], glow[part], NN) * scale).astype(low)
-                if w == 0:
-                    totals[sub] = grad[part]
-                else:
-                    total = totals[sub] + grad[part]
-                    bg_ref[head] = total[:, 0:LANES]
-                    bt_ref[head, :, 0:16] = total[:, LANES:WIN_TOK]
-            mixed_ref[rows, cols] = mixed_sum.astype(low)
-            gq_ref[rows, cols] = (gq_sum * scale).astype(low)
+        rows = slice(w * WIN_TOK, (w + 1) * WIN_TOK)
+        gq = mm(glow, k, NN)
+        mixed_sum = jnp.zeros((WIN_TOK, LANES), wide)
+        gq_sum = jnp.zeros((WIN_TOK, LANES), wide)
+        for sub in range(4):
+            head = group * 4 + sub
+            feats = slice(head * HEAD_DIM, (head + 1) * HEAD_DIM)
+            part = slice(sub * WIN_TOK, (sub + 1) * WIN_TOK)
+            mixed_sum = jnp.where(lane == sub, mixed[part], mixed_sum)
+            gq_sum = jnp.where(lane == sub, gq[part], gq_sum)
+            gvt_ref[w, feats, :] = mm(gmt_ref[w, feats, :], prob[part], NN).astype(low)
+            gkt_ref[w, feats, :] = (mm(qt_ref[w, feats, :], glow[part], NN) * scale).astype(low)
+        mixed_ref[rows, cols] = mixed_sum.astype(low)
+        gq_ref[rows, cols] = (gq_sum * scale).astype(low)
+
+    work = [(group, w) for group in range(3) for w in range(2)]
+    states = [None] * 6
+    for n in range(-3, 9):
+        if 0 <= n + 1 < 6:
+            states[n + 1] = first_products(*work[n + 1])
+        if 0 <= n < 6:
+            states[n] = weights_of(*work[n], *states[n])
+        if 0 <= n - 1 < 6:
+            last_products(*work[n - 1], *states[n - 1])
+        if 0 <= n < 6:
+            states[n] = score_grads(*work[n], *states[n])
 
     mixed = mixed_ref[...]
 
@@ -267,11 +288,8 @@
     token_grad = jnp.sum(jnp.where(masked, grad_filled, 0.0), axis=0, keepdims=True)
 
     order = order_ref[...]
-    parts = []
-    for value in (gq, gk, gv, cot):
-        turned = mm(order, value, NT).astype(low)
-        other = mixed if value is cot else normed
-        parts.append(mm(turned, other, NN))
+    turned = [mm(order, value, NT).astype(low) for value in (gq, gk, gv, cot)]
+    parts = [mm(value, normed, NN) for value in turned[:3]] + [mm(turned[3], mixed, NN)]
     vectors = jnp.concatenate([gain_grad, token_grad, jnp.zeros((6, D), wide)], axis=0)
     for n in range(16):
         rows = slice(n * 24, (n + 1) * 24)
@@ -554,8 +572,8 @@
     final, output, input_grad, table_grad = lax.optimization_barrier(
         (final, output, input_grad, table_grad)
     )
-    weight_grads = jnp.sum(final[:, :6].astype(wide), axis=0)
-    vector_grads = jnp.sum(final[:, 6:].astype(wide), axis=0)
+    final = jnp.sum(final.astype(wide), axis=0)
+    weight_grads, vector_grads = final[:6], final[6:]
     return (output, input_grad, weight_grads, table_grad, vector_grads)
 
 

time: 76.9 us -> 74.4 us (0.967)
  Pallas kernels: 19.7 us -> 17.9 us
  other arithmetic: 4.04 us -> 2.81 us
    pallas_call x1, Pallas kernels: 9.24 us -> 7.33 us  [local(): pl.pallas_call(main_kernel, out_shape=(jax.ShapeDtypeStruct((TOK, D), low...]
    reduce_sum x2 -> x1, other arithmetic: 1.25 us -> 0.02 us  [local(): final = jnp.sum(final.astype(wide), axis=0)]
    unnamed x26 -> x28, local copies, waits for them, and re-layouts: 2.34 us -> 2.33 us
  transfers between devices with their start and end apart: 9 -> 9, of which waited for: 6 -> 6; matrix products, arithmetic and copies ran while one was open for 2% -> 2% of each run, Pallas kernels for 12% -> 13%
where the time goes in v6:
time: 74.4 us; the launch traced here: 73.9 us
  starting transfers between devices  25.3 us (34%)
  waiting for transfers between devices  22.9 us (31%)
  Pallas kernels  17.9 us (24%)
  local copies, waits for them, and re-layouts  4.19 us (6%)
  other arithmetic  2.81 us (4%)
  between operations  0.82 us (1%)
    all_to_all x1, waiting for transfers between devices, local(): lax.all_to_all(pair, 'lon', 0, 0, axis_index_groups=groups, tiled=True)  9.68 us
    ppermute x4, starting transfers between devices, passed_along(): return lax.ppermute(value, axis, pairs)  8.66 us
    pallas_call x1, Pallas kernels, local(): pl.pallas_call(main_kernel, out_shape=(jax.ShapeDtypeStruct((TOK, D), low...  7.33 us
    all_to_all x1, starting transfers between devices, local(): lax.all_to_all(pair, 'lon', 0, 0, axis_index_groups=groups, tiled=True)  7.21 us
    all_to_all x1, starting transfers between devices, local(): final = lax.all_to_all(second, 'lat', 0, 0, tiled=True)  7.14 us
    ppermute x4, waiting for transfers between devices, passed_along(): return lax.ppermute(value, axis, pairs)  6.5 us
    all_to_all x1, waiting for transfers between devices, local(): final = lax.all_to_all(second, 'lat', 0, 0, tiled=True)  5.16 us
    pallas_call x1, Pallas kernels, local(): pl.pallas_call(pre_kernel, out_shape=(jax.ShapeDtypeStruct((HEADS, WIN_TO...  5.13 us
  transfers between devices with their start and end apart: 9, of which 6 were waited for; matrix products, arithmetic and copies ran while one was open for 2% of the time, Pallas kernels for 13%

profile of v6, /device:TPU:2, one launch (start us, length us, event | category | flops | bytes accessed | tf_op | source)
XLA Modules:
  0.0 73.9 jit_solution(16630868663798763816)
XLA Ops:
  0.6 0.7 broadcast_compare_fusion
  1.3 0.1 broadcast_in_dim.37
  1.4 0.1 eq.18
  1.5 1.1 %slice_bitcast_fusion.2 = (bf16[1,3,12,4,384]{4,3,2,1,0:T(4,128)(2,1)S(1)}, bf16[1,3,12,4,384]{4,3,2,1,0:T(4,128)(2,1)S(1)}) fusion(bf16[6,12,4,384]{3,2,1,0:T(4,128)(2,1)} %bitcast.26, bf16[6,12,4,384]{3,2,1,0:T(4,128)(2,1)} %bitcast.23, pred[4]{0:T(512)(128)(4,1)S(1)} %eq.18), kind=kLoop, calls=%fused_computation.7 | loop fusion | flops 55296 | bytes 442372 | tf_op jit(solution)/shard_map/stack | solution.py:427
  2.5 0.2 pad_maximum_fusion.1
  2.7 7.5 %collective-permute-start = (bf16[2,3,12,4,384]{4,3,2,1,0:T(4,128)(2,1)S(1)}, bf16[2,3,12,4,384]{4,3,2,1,0:T(4,128)(2,1)S(1)}, u32[]{:S(2)}, u32[]{:S(2)}) collective-permute-start(bf16[2,3,12,4,384]{4,3,2,1,0:T(4,128)(2,1)S(1)} %pad_maximum_fusion.1), channel_id=1, source_target_pairs={{0,240},{16,0},{32,16},{48,32},{64,48},{80,64},{96,80},{112,96},{1... | collective-permute-start | bytes 663560 | tf_op jit(solution)/shard_map/ppermute | solution.py:39
  10.2 0.1 pad_add_fusion.place_ref
  10.3 0.0 copy-start.3
  10.3 0.0 copy-start.6
  10.3 0.9 %copy-done.6 = s32[144,144]{1,0:T(8,128)S(1)} copy-done((s32[144,144]{1,0:T(8,128)S(1)}, s32[144,144]{1,0:T(8,128)}, u32[]{:S(2)}) %copy-start.6) | copy-done | bytes 82968
  11.2 0.0 copy-start.8
  11.2 0.8 %copy-done.8 = f32[1,12,759]{2,0,1:T(1,128)S(1)} copy-done((f32[1,12,759]{2,0,1:T(1,128)S(1)}, f32[1,12,759]{2,0,1:T(1,128)}, u32[]{:S(2)}) %copy-start.8) | copy-done | bytes 36456
  11.9 0.0 copy-start
  11.9 0.0 copy-start.1
  11.9 0.0 copy-start.12
  11.9 0.0 copy-start.13
  11.9 0.0 copy-start.4
  12.0 0.0 copy-start.5
  12.0 0.0 copy-start.9
  12.0 5.1 %shard_map.128 = (f32[12,144,256]{2,1,0:T(8,128)S(1)}, bf16[384,384]{1,0:T(8,128)(2,1)S(1)}) custom-call(s32[2]{0:T(128)S(1)} %pad_add_fusion.place_ref, f32[12,1,759]{2,1,0:T(1,128)S(1)} %bitcast.29, s32[144,144]{1,0:T(8,128)S(1)} %copy-done.6), custom_call_target="tpu_custom_call" | custom-call | flops 5000000000 | tf_op jit(solution)/shard_map/pallas_call | solution.py:429
  17.1 0.0 copy-done
  17.1 0.0 copy-done.1
  17.1 0.1 slice_bitcast_fusion.3
  17.2 0.0 collective-permute-done.lat_ref
  17.3 0.2 pad_maximum_fusion.2
  17.5 0.7 collective-permute-start.1
  18.1 0.0 copy-done.12
  18.1 0.0 copy-done.13
  18.2 3.4 %collective-permute-done.1.lon_ref = bf16[2,6,6,4,384]{4,3,2,1,0:T(4,128)(2,1)S(1)} collective-permute-done((bf16[2,6,6,4,384]{4,3,2,1,0:T(4,128)(2,1)S(1)}, bf16[2,6,6,4,384]{4,3,2,1,0:T(4,128)(2,1)S(1)}, u32[]{:S(2)}, u32[]{:S(2)}) %collective-permute-start.1) | collective-permute-done | bytes 221216 | tf_op jit(solution)/shard_map/ppermute | solution.py:39
  21.6 0.0 copy-done.3
  21.6 0.0 copy-done.4
  21.6 0.0 copy-done.5
  21.6 0.0 copy-done.9
  21.6 7.3 %shard_map.129 = (bf16[288,384]{1,0:T(8,128)(2,1)S(1)}, bf16[288,384]{1,0:T(8,128)(2,1)S(1)}, bf16[288,384]{1,0:T(8,128)(2,1)S(1)}, bf16[8,104,384]{2,1,0:T(8,12...) custom-call(s32[2]{0:T(128)S(1)} %pad_add_fusion.place_ref, ...), custom_call_target="tpu_custom_call" | custom-call | flops 10000000000 | tf_op jit(solution)/shard_map/pallas_call | solution.py:451
  28.9 0.0 copy-start.7
  29.0 0.5 shard_map.130
  29.4 2.2 %collective-permute-start.2 = (bf16[8,104,384]{2,1,0:T(8,128)(2,1)S(1)}, bf16[8,104,384]{2,1,0:T(8,128)(2,1)S(1)}, u32[]{:S(2)}, u32[]{:S(2)}) collective-permute-start(bf16[8,104,384]{2,1,0:T(8,128)(2,1)S(1)} %get-tuple-element.45), channel_id=1, source_target_pairs={{0,1},{1,0},{2,3},{3,2},{4,5},{5,4},{6,7},{7,6},{8,9},{9,8},{10,11... | collective-permute-start | bytes 1916936 | tf_op jit(solution)/shard_map/ppermute | solution.py:503
  31.7 0.1 collective-permute-start.3
  31.8 0.4 collective-permute-start.4
  32.2 1.6 %collective-permute-done.3.other_ref = bf16[6,176,128]{2,1,0:T(8,128)(2,1)S(1)} collective-permute-done((bf16[6,176,128]{2,1,0:T(8,128)(2,1)S(1)}, bf16[6,176,128]{2,1,0:T(8,128)(2,1)S(1)}, u32[]{:S(2)}, u32[]{:S(2)}) %collective-permute-start.3) | collective-permute-done | bytes 270368 | tf_op jit(solution)/shard_map/ppermute | solution.py:503
  33.8 0.0 copy-done.7
  33.8 1.7 %shard_map.131.table_ref = f32[48,128]{1,0:T(8,128)S(1)} custom-call(f32[6,176,128]{2,1,0:T(8,128)S(1)} %get-tuple-element.46.mine_ref, bf16[6,176,128]{2,1,0:T(8,128)(2,1)S(1)} %collective-permute-done.3.other_ref, s32[144,144]{1,0:T(8,128)S(1)} %copy-done.7), custom_call_target="tpu_custom_call" | custom-call | flops 1000000000 | bytes 1000000 | tf_op jit(solution)/shard_map/pallas_call | solution.py:521
  35.5 0.0 collective-permute-done.2.taken_ref
  35.5 1.0 %shard_map.132 = bf16[8,112,384]{2,1,0:T(8,128)(2,1)} custom-call(bf16[8,104,384]{2,1,0:T(8,128)(2,1)S(1)} %get-tuple-element.38.keep_ref, bf16[8,104,384]{2,1,0:T(8,128)(2,1)S(1)} %collective-permute-done.2.taken_ref, f32[48,128]{1,0:T(8,128)S(1)} %shard_map.131.table_ref), custom_call_target="tpu_custom_call" | custom-call | flops 1000000 | bytes 1000000 | tf_op jit(solution)/shard_map/pallas_call | solution.py:535
  36.5 0.6 collective-permute-done.4
  37.1 7.2 %all-to-all-start = ((bf16[8,112,384]{2,1,0:T(8,128)(2,1)}), bf16[8,112,384]{2,1,0:T(8,128)(2,1)S(1)}, u32[]{:S(2)}, u32[]{:S(2)}) async-start(bf16[8,112,384]{2,1,0:T(8,128)(2,1)} %shard_map.132), calls=%async_computation | async-start | bytes 1376256 | tf_op jit(solution)/shard_map/all_to_all | solution.py:545
  44.3 0.3 pad_maximum_fusion
  44.6 9.7 %all-to-all-done.got_ref = bf16[8,112,384]{2,1,0:T(8,128)(2,1)S(1)} async-done(((bf16[8,112,384]{2,1,0:T(8,128)(2,1)}), bf16[8,112,384]{2,1,0:T(8,128)(2,1)S(1)}, u32[]{:S(2)}, u32[]{:S(2)}) %all-to-all-start) | async-done | bytes 688160 | tf_op jit(solution)/shard_map/all_to_all | solution.py:545
  54.3 0.8 %shard_map.133 = (bf16[16,8,384]{2,1,0:T(8,128)(2,1)}, f32[48,128]{1,0:T(8,128)S(1)}) custom-call(bf16[8,112,384]{2,1,0:T(8,128)(2,1)S(1)} %all-to-all-done.got_ref), custom_call_target="tpu_custom_call" | custom-call | flops 1000000 | bytes 1000000 | tf_op jit(solution)/shard_map/pallas_call | solution.py:546
  55.1 0.2 fusion.2
  55.2 0.1 collective-permute-start.5
  55.3 7.1 %all-to-all-start.1 = ((bf16[16,8,384]{2,1,0:T(8,128)(2,1)}), bf16[16,8,384]{2,1,0:T(8,128)(2,1)S(1)}, u32[]{:S(2)}, u32[]{:S(2)}) async-start(bf16[16,8,384]{2,1,0:T(8,128)(2,1)} %get-tuple-element.53), calls=%async_computation.1 | async-start | bytes 196608 | tf_op jit(solution)/shard_map/all_to_all | solution.py:560
  62.5 2.5 %collective-permute-done.5 = bf16[2,3,12,4,384]{4,3,2,1,0:T(4,128)(2,1)S(1)} collective-permute-done((bf16[2,3,12,4,384]{4,3,2,1,0:T(4,128)(2,1)S(1)}, bf16[2,3,12,4,384]{4,3,2,1,0:T(4,128)(2,1)S(1)}, u32[]{:S(2)}, u32[]{:S(2)}) %collective-permute-start.5) | collective-permute-done | bytes 221216 | tf_op jit(solution)/shard_map/ppermute | solution.py:39
  64.9 0.0 collective-permute-start.6
  64.9 0.3 maximum_bitcast_fusion
  65.2 0.9 %slice_bitcast_fusion = (bf16[4,6,12,384]{3,0,2,1:T(4,128)(2,1)}, bf16[4,6,12,384]{3,0,2,1:T(4,128)(2,1)}) fusion(bf16[2,4,6,12,384]{4,1,3,2,0:T(4,128)(2,1)S(1)} %maximum_bitcast_fusion), kind=kLoop, calls=%fused_computation.2 | loop fusion | bytes 884736 | tf_op jit(solution)/shard_map/squeeze | solution.py:571
  66.1 0.0 collective-permute-done.6.other_ref
  66.1 0.0 copy-done.2
  66.1 0.6 copy-done.10
  66.7 1.4 %shard_map.134 = f32[12,1,759]{2,1,0:T(1,128)} custom-call(s32[2]{0:T(128)} %copy-done.3, f32[48,128]{1,0:T(8,128)} %copy-done.2, f32[48,128]{1,0:T(8,128)} %copy-done.10), custom_call_target="tpu_custom_call" | custom-call | flops 100000 | bytes 100000 | tf_op jit(solution)/shard_map/pallas_call | solution.py:563
  68.2 5.2 %all-to-all-done.1 = bf16[16,8,384]{2,1,0:T(8,128)(2,1)S(1)} async-done(((bf16[16,8,384]{2,1,0:T(8,128)(2,1)}), bf16[16,8,384]{2,1,0:T(8,128)(2,1)S(1)}, u32[]{:S(2)}, u32[]{:S(2)}) %all-to-all-start.1) | async-done | bytes 98336 | tf_op jit(solution)/shard_map/all_to_all | solution.py:560
  73.3 0.0 copy-start.11
  73.3 0.6 slice.51
  73.9 0.0 copy-done.11
  (6 shorter events, 0.1 us)
Async XLA Ops:
  2.7 14.6 %collective-permute-start = (bf16[2,3,12,4,384]{4,3,2,1,0:T(4,128)(2,1)S(1)}, bf16[2,3,12,4,384]{4,3,2,1,0:T(4,128)(2,1)S(1)}, u32[]{:S(2)}, u32[]{:S(2)}) collective-permute-start(bf16[2,3,12,4,384]{4,3,2,1,0:T(4,128)(2,1)S(1)} %pad_maximum_fusion.1), channel_id=1, source_target_pairs={{0,240},{16,0},{32,16},{48,32},{64,48},{80,64},{96,80},{112,96},{1... | collective-permute-start | bytes 663560 | tf_op jit(solution)/shard_map/ppermute | solution.py:39
  10.3 11.3 %copy-start.3 = (s32[2]{0:T(128)}, s32[2]{0:T(128)S(1)}, u32[]{:S(2)}) copy-start(s32[2]{0:T(128)S(1)} %pad_add_fusion.place_ref) | copy-start | bytes 28
  10.3 0.9 %copy-start.6 = (s32[144,144]{1,0:T(8,128)S(1)}, s32[144,144]{1,0:T(8,128)}, u32[]{:S(2)}) copy-start(s32[144,144]{1,0:T(8,128)} %ids_ref.1) | copy-start | bytes 248836
  11.2 0.8 %copy-start.8 = (f32[1,12,759]{2,0,1:T(1,128)S(1)}, f32[1,12,759]{2,0,1:T(1,128)}, u32[]{:S(2)}) copy-start(f32[1,12,759]{2,0,1:T(1,128)} %param.16) | copy-start | bytes 109300
  11.9 5.2 %copy-start = (bf16[4,6,12,384]{3,0,2,1:T(4,128)(2,1)S(1)}, bf16[4,6,12,384]{3,0,2,1:T(4,128)(2,1)}, u32[]{:S(2)}) copy-start(bf16[4,6,12,384]{3,0,2,1:T(4,128)(2,1)} %param.9) | copy-start | bytes 663556
  11.9 5.2 %copy-start.1 = (bf16[4,6,12,384]{3,0,2,1:T(4,128)(2,1)S(1)}, bf16[4,6,12,384]{3,0,2,1:T(4,128)(2,1)}, u32[]{:S(2)}) copy-start(bf16[4,6,12,384]{3,0,2,1:T(4,128)(2,1)} %param.10) | copy-start | bytes 663556
  11.9 6.2 %copy-start.12 = (bf16[384]{0:T(512)(128)(2,1)S(1)}, bf16[384]{0:T(512)(128)(2,1)}, u32[]{:S(2)}) copy-start(bf16[384]{0:T(512)(128)(2,1)} %param.12) | copy-start | bytes 2308
  11.9 6.2 %copy-start.13 = (bf16[384]{0:T(512)(128)(2,1)S(1)}, bf16[384]{0:T(512)(128)(2,1)}, u32[]{:S(2)}) copy-start(bf16[384]{0:T(512)(128)(2,1)} %param.13) | copy-start | bytes 2308
  11.9 9.6 %copy-start.4 = (bf16[1152,384]{1,0:T(8,128)(2,1)S(1)}, bf16[1152,384]{1,0:T(8,128)(2,1)}, u32[]{:S(2)}) copy-start(bf16[1152,384]{1,0:T(8,128)(2,1)} %wqkv_in_ref.1) | copy-start | bytes 2654212
  12.0 9.6 %copy-start.5 = (bf16[384,384]{1,0:T(8,128)(2,1)S(1)}, bf16[384,384]{1,0:T(8,128)(2,1)}, u32[]{:S(2)}) copy-start(bf16[384,384]{1,0:T(8,128)(2,1)} %wout_ref.3) | copy-start | bytes 884740
  12.0 9.6 %copy-start.9 = (s32[2,1,1]{0,2,1:T(1,128)S(1)}, s32[2,1,1]{0,2,1:T(1,128)}, u32[]{:S(2)}) copy-start(s32[2,1,1]{0,2,1:T(1,128)} %param.11) | copy-start | bytes 28
  17.5 4.1 %collective-permute-start.1 = (bf16[2,6,6,4,384]{4,3,2,1,0:T(4,128)(2,1)S(1)}, bf16[2,6,6,4,384]{4,3,2,1,0:T(4,128)(2,1)S(1)}, u32[]{:S(2)}, u32[]{:S(2)}) collective-permute-start(bf16[2,6,6,4,384]{4,3,2,1,0:T(4,128)(2,1)S(1)} %pad_maximum_fusion.2), channel_id=1, source_target_pairs={{0,15},{1,0},{2,1},{3,2},{4,3},{5,4},{6,5},{7,6},{8,7},{9,8},{10,9... | collective-permute-start | bytes 663560 | tf_op jit(solution)/shard_map/ppermute | solution.py:39
  28.9 4.8 %copy-start.7 = (s32[144,144]{1,0:T(8,128)S(1)}, s32[144,144]{1,0:T(8,128)}, u32[]{:S(2)}) copy-start(s32[144,144]{1,0:T(8,128)} %ids_ref.1) | copy-start | bytes 248836
  29.4 6.1 %collective-permute-start.2 = (bf16[8,104,384]{2,1,0:T(8,128)(2,1)S(1)}, bf16[8,104,384]{2,1,0:T(8,128)(2,1)S(1)}, u32[]{:S(2)}, u32[]{:S(2)}) collective-permute-start(bf16[8,104,384]{2,1,0:T(8,128)(2,1)S(1)} %get-tuple-element.45), channel_id=1, source_target_pairs={{0,1},{1,0},{2,3},{3,2},{4,5},{5,4},{6,7},{7,6},{8,9},{9,8},{10,11... | collective-permute-start | bytes 1916936 | tf_op jit(solution)/shard_map/ppermute | solution.py:503
  31.7 2.1 %collective-permute-start.3 = (bf16[6,176,128]{2,1,0:T(8,128)(2,1)S(1)}, bf16[6,176,128]{2,1,0:T(8,128)(2,1)S(1)}, u32[]{:S(2)}, u32[]{:S(2)}) collective-permute-start(bf16[6,176,128]{2,1,0:T(8,128)(2,1)S(1)} %get-tuple-element.47), channel_id=1, source_target_pairs={{0,1},{1,0},{2,3},{3,2},{4,5},{5,4},{6,7},{7,6},{8,9},{9,8},{10,11... | collective-permute-start | bytes 811016 | tf_op jit(solution)/shard_map/ppermute | solution.py:503
  31.8 5.4 %collective-permute-start.4 = (bf16[2,6,6,4,384]{4,3,2,1,0:T(4,128)(2,1)S(1)}, bf16[2,6,6,4,384]{4,3,2,1,0:T(4,128)(2,1)S(1)}, u32[]{:S(2)}, u32[]{:S(2)}) collective-permute-start(bf16[2,6,6,4,384]{4,3,2,1,0:T(4,128)(2,1)S(1)} %get-tuple-element.48), channel_id=1, source_target_pairs={{0,1},{1,2},{2,3},{3,4},{4,5},{5,6},{6,7},{7,8},{8,9},{9,10},{10,1... | collective-permute-start | bytes 663560 | tf_op jit(solution)/shard_map/ppermute | solution.py:39
  37.1 17.2 %all-to-all-start = ((bf16[8,112,384]{2,1,0:T(8,128)(2,1)}), bf16[8,112,384]{2,1,0:T(8,128)(2,1)S(1)}, u32[]{:S(2)}, u32[]{:S(2)}) async-start(bf16[8,112,384]{2,1,0:T(8,128)(2,1)} %shard_map.132), calls=%async_computation | async-start | bytes 1376256 | tf_op jit(solution)/shard_map/all_to_all | solution.py:545
  55.1 11.1 %copy-start.2 = (f32[48,128]{1,0:T(8,128)}, f32[48,128]{1,0:T(8,128)S(1)}, u32[]{:S(2)}) copy-start(f32[48,128]{1,0:T(8,128)S(1)} %get-tuple-element.56.mine_ref) | copy-start | bytes 73732
  55.2 9.7 %collective-permute-start.5 = (bf16[2,3,12,4,384]{4,3,2,1,0:T(4,128)(2,1)S(1)}, bf16[2,3,12,4,384]{4,3,2,1,0:T(4,128)(2,1)S(1)}, u32[]{:S(2)}, u32[]{:S(2)}) collective-permute-start(bf16[2,3,12,4,384]{4,3,2,1,0:T(4,128)(2,1)S(1)} %get-tuple-element.63), channel_id=1, source_target_pairs={{0,16},{16,32},{32,48},{48,64},{64,80},{80,96},{96,112},{112,128},... | collective-permute-start | bytes 663560 | tf_op jit(solution)/shard_map/ppermute | solution.py:39
  55.3 18.0 %all-to-all-start.1 = ((bf16[16,8,384]{2,1,0:T(8,128)(2,1)}), bf16[16,8,384]{2,1,0:T(8,128)(2,1)S(1)}, u32[]{:S(2)}, u32[]{:S(2)}) async-start(bf16[16,8,384]{2,1,0:T(8,128)(2,1)} %get-tuple-element.53), calls=%async_computation.1 | async-start | bytes 196608 | tf_op jit(solution)/shard_map/all_to_all | solution.py:560
  64.9 1.2 %collective-permute-start.6 = (f32[48,128]{1,0:T(8,128)S(1)}, f32[48,128]{1,0:T(8,128)S(1)}, u32[]{:S(2)}, u32[]{:S(2)}) collective-permute-start(f32[48,128]{1,0:T(8,128)S(1)} %get-tuple-element.56.mine_ref), channel_id=1, source_target_pairs={{0,1},{1,0},{2,3},{3,2},{4,5},{5,4},{6,7},{7,6},{8,9},{9,8},{10,11... | collective-permute-start | bytes 73736 | tf_op jit(solution)/shard_map/ppermute | solution.py:503
  66.1 0.6 copy-start.10
  73.3 0.6 copy-start.11

commit v7 on v6

--- a/solution.py
+++ b/solution.py
@@ -351,7 +351,7 @@
         return acc + mm(left, right, NT)
 
     start = jnp.zeros((HEADS * QSLOTS, LANES // 2), wide)
-    acc = lax.fori_loop(0, 18, one_step, start, unroll=6)
+    acc = lax.fori_loop(0, 18, one_step, start, unroll=18)
     for head in range(HEADS // 2):
         even = acc[2 * QSLOTS * head : 2 * QSLOTS * head + QSLOTS]
         odd = acc[2 * QSLOTS * head + QSLOTS : 2 * QSLOTS * (head + 1)]
@@ -515,9 +515,9 @@
         cost_estimate=pl.CostEstimate(flops=2 * 10**9, bytes_accessed=0, transcendentals=0),
     )(filled, mixed, igrad, out_weight)
     lon_out = passed_along(out_lon, "lon", 1)
-    give, pairs_give, out_own = lax.optimization_barrier((give, pairs_give, out_own))
     other_pairs = swapped(pairs_give, 1)
     taken = swapped(give, 1)
+    pairs, out_own = lax.optimization_barrier((pairs, out_own))
     table = pl.pallas_call(
         table_kernel,
         out_shape=jax.ShapeDtypeStruct((HEADS // 2 * QSLOTS, LANES), wide),

time: 74.4 us -> 73.5 us (0.988)
    ppermute x4, waiting for transfers between devices: 6.5 us -> 7.72 us  [passed_along(): return lax.ppermute(value, axis, pairs)]
    all_to_all x1, waiting for transfers between devices: 9.68 us -> 8.73 us  [local(): lax.all_to_all(pair, 'lon', 0, 0, axis_index_groups=groups, tiled=True)]
    ppermute x3, waiting for transfers between devices: 1.58 us -> 0.82 us  [swapped(): return lax.ppermute(value, 'lon', [(i, i ^ bit) for i in range(size)])]
where the time goes in v7:
time: 73.5 us; the launch traced here: 73.1 us
  starting transfers between devices  25.4 us (35%)
  waiting for transfers between devices  22.3 us (30%)
  Pallas kernels  17.5 us (24%)
  local copies, waits for them, and re-layouts  4.19 us (6%)
  other arithmetic  2.81 us (4%)
  between operations  0.81 us (1%)
    ppermute x4, starting transfers between devices, passed_along(): return lax.ppermute(value, axis, pairs)  8.92 us
    all_to_all x1, waiting for transfers between devices, local(): lax.all_to_all(pair, 'lon', 0, 0, axis_index_groups=groups, tiled=True)  8.73 us
    ppermute x4, waiting for transfers between devices, passed_along(): return lax.ppermute(value, axis, pairs)  7.72 us
    pallas_call x1, Pallas kernels, local(): pl.pallas_call(main_kernel, out_shape=(jax.ShapeDtypeStruct((TOK, D), low...  7.33 us
    all_to_all x1, starting transfers between devices, local(): final = lax.all_to_all(second, 'lat', 0, 0, tiled=True)  7.14 us
    all_to_all x1, starting transfers between devices, local(): lax.all_to_all(pair, 'lon', 0, 0, axis_index_groups=groups, tiled=True)  7.02 us
    pallas_call x1, Pallas kernels, local(): pl.pallas_call(pre_kernel, out_shape=(jax.ShapeDtypeStruct((HEADS, WIN_TO...  5.13 us
    all_to_all x1, waiting for transfers between devices, local(): final = lax.all_to_all(second, 'lat', 0, 0, tiled=True)  5.07 us
  transfers between devices with their start and end apart: 9, of which 6 were waited for; matrix products, arithmetic and copies ran while one was open for 2% of the time, Pallas kernels for 13%

profile of v7, /device:TPU:2, one launch (start us, length us, event | category | flops | bytes accessed | tf_op | source)
XLA Modules:
  0.0 73.1 jit_solution(15844655734753402150)
XLA Ops:
  0.6 0.7 broadcast_compare_fusion
  1.3 0.1 broadcast_in_dim.37
  1.4 0.1 eq.18
  1.5 1.1 %slice_bitcast_fusion.2 = (bf16[1,3,12,4,384]{4,3,2,1,0:T(4,128)(2,1)S(1)}, bf16[1,3,12,4,384]{4,3,2,1,0:T(4,128)(2,1)S(1)}) fusion(bf16[6,12,4,384]{3,2,1,0:T(4,128)(2,1)} %bitcast.26, bf16[6,12,4,384]{3,2,1,0:T(4,128)(2,1)} %bitcast.23, pred[4]{0:T(512)(128)(4,1)S(1)} %eq.18), kind=kLoop, calls=%fused_computation.7 | loop fusion | flops 55296 | bytes 442372 | tf_op jit(solution)/shard_map/stack | solution.py:427
  2.5 0.2 pad_maximum_fusion.1
  2.7 7.5 %collective-permute-start = (bf16[2,3,12,4,384]{4,3,2,1,0:T(4,128)(2,1)S(1)}, bf16[2,3,12,4,384]{4,3,2,1,0:T(4,128)(2,1)S(1)}, u32[]{:S(2)}, u32[]{:S(2)}) collective-permute-start(bf16[2,3,12,4,384]{4,3,2,1,0:T(4,128)(2,1)S(1)} %pad_maximum_fusion.1), channel_id=1, source_target_pairs={{0,240},{16,0},{32,16},{48,32},{64,48},{80,64},{96,80},{112,96},{1... | collective-permute-start | bytes 663560 | tf_op jit(solution)/shard_map/ppermute | solution.py:39
  10.2 0.1 pad_add_fusion.place_ref
  10.3 0.0 copy-start.3
  10.3 0.0 copy-start.6
  10.3 0.9 %copy-done.6 = s32[144,144]{1,0:T(8,128)S(1)} copy-done((s32[144,144]{1,0:T(8,128)S(1)}, s32[144,144]{1,0:T(8,128)}, u32[]{:S(2)}) %copy-start.6) | copy-done | bytes 82968
  11.2 0.0 copy-start.8
  11.2 0.8 %copy-done.8 = f32[1,12,759]{2,0,1:T(1,128)S(1)} copy-done((f32[1,12,759]{2,0,1:T(1,128)S(1)}, f32[1,12,759]{2,0,1:T(1,128)}, u32[]{:S(2)}) %copy-start.8) | copy-done | bytes 36456
  11.9 0.0 copy-start
  11.9 0.0 copy-start.1
  11.9 0.0 copy-start.12
  11.9 0.0 copy-start.13
  11.9 0.0 copy-start.4
  12.0 0.0 copy-start.5
  12.0 0.0 copy-start.9
  12.0 5.1 %shard_map.128 = (f32[12,144,256]{2,1,0:T(8,128)S(1)}, bf16[384,384]{1,0:T(8,128)(2,1)S(1)}) custom-call(s32[2]{0:T(128)S(1)} %pad_add_fusion.place_ref, f32[12,1,759]{2,1,0:T(1,128)S(1)} %bitcast.29, s32[144,144]{1,0:T(8,128)S(1)} %copy-done.6), custom_call_target="tpu_custom_call" | custom-call | flops 5000000000 | tf_op jit(solution)/shard_map/pallas_call | solution.py:429
  17.1 0.0 copy-done
  17.1 0.0 copy-done.1
  17.1 0.1 slice_bitcast_fusion.3
  17.2 0.0 collective-permute-done.lat_ref
  17.3 0.2 pad_maximum_fusion.2
  17.5 0.7 collective-permute-start.1
  18.1 0.0 copy-done.12
  18.1 0.0 copy-done.13
  18.2 3.4 %collective-permute-done.1.lon_ref = bf16[2,6,6,4,384]{4,3,2,1,0:T(4,128)(2,1)S(1)} collective-permute-done((bf16[2,6,6,4,384]{4,3,2,1,0:T(4,128)(2,1)S(1)}, bf16[2,6,6,4,384]{4,3,2,1,0:T(4,128)(2,1)S(1)}, u32[]{:S(2)}, u32[]{:S(2)}) %collective-permute-start.1) | collective-permute-done | bytes 221216 | tf_op jit(solution)/shard_map/ppermute | solution.py:39
  21.6 0.0 copy-done.3
  21.6 0.0 copy-done.4
  21.6 0.0 copy-done.5
  21.6 0.0 copy-done.9
  21.6 7.3 %shard_map.129 = (bf16[288,384]{1,0:T(8,128)(2,1)S(1)}, bf16[288,384]{1,0:T(8,128)(2,1)S(1)}, bf16[288,384]{1,0:T(8,128)(2,1)S(1)}, bf16[8,104,384]{2,1,0:T(8,12...) custom-call(s32[2]{0:T(128)S(1)} %pad_add_fusion.place_ref, ...), custom_call_target="tpu_custom_call" | custom-call | flops 10000000000 | tf_op jit(solution)/shard_map/pallas_call | solution.py:451
  28.9 2.2 %collective-permute-start.2 = (bf16[8,104,384]{2,1,0:T(8,128)(2,1)S(1)}, bf16[8,104,384]{2,1,0:T(8,128)(2,1)S(1)}, u32[]{:S(2)}, u32[]{:S(2)}) collective-permute-start(bf16[8,104,384]{2,1,0:T(8,128)(2,1)S(1)} %get-tuple-element.38), channel_id=1, source_target_pairs={{0,1},{1,0},{2,3},{3,2},{4,5},{5,4},{6,7},{7,6},{8,9},{9,8},{10,11... | collective-permute-start | bytes 1916936 | tf_op jit(solution)/shard_map/ppermute | solution.py:503
  31.2 0.1 collective-permute-start.3
  31.3 0.0 copy-start.7
  31.3 0.5 shard_map.130
  31.8 0.7 collective-permute-start.4
  32.4 0.8 %collective-permute-done.3.other_ref = bf16[6,176,128]{2,1,0:T(8,128)(2,1)S(1)} collective-permute-done((bf16[6,176,128]{2,1,0:T(8,128)(2,1)S(1)}, bf16[6,176,128]{2,1,0:T(8,128)(2,1)S(1)}, u32[]{:S(2)}, u32[]{:S(2)}) %collective-permute-start.3) | collective-permute-done | bytes 270368 | tf_op jit(solution)/shard_map/ppermute | solution.py:503
  33.3 0.0 copy-done.7
  33.3 1.4 %shard_map.131.table_ref = f32[48,128]{1,0:T(8,128)S(1)} custom-call(f32[6,176,128]{2,1,0:T(8,128)S(1)} %get-tuple-element.44.mine_ref, bf16[6,176,128]{2,1,0:T(8,128)(2,1)S(1)} %collective-permute-done.3.other_ref, s32[144,144]{1,0:T(8,128)S(1)} %copy-done.7), custom_call_target="tpu_custom_call" | custom-call | flops 1000000000 | bytes 1000000 | tf_op jit(solution)/shard_map/pallas_call | solution.py:521
  34.6 0.0 collective-permute-done.2.taken_ref
  34.6 1.0 %shard_map.132 = bf16[8,112,384]{2,1,0:T(8,128)(2,1)} custom-call(bf16[8,104,384]{2,1,0:T(8,128)(2,1)S(1)} %get-tuple-element.37.keep_ref, bf16[8,104,384]{2,1,0:T(8,128)(2,1)S(1)} %collective-permute-done.2.taken_ref, f32[48,128]{1,0:T(8,128)S(1)} %shard_map.131.table_ref), custom_call_target="tpu_custom_call" | custom-call | flops 1000000 | bytes 1000000 | tf_op jit(solution)/shard_map/pallas_call | solution.py:535
  35.6 1.8 %collective-permute-done.4 = bf16[2,6,6,4,384]{4,3,2,1,0:T(4,128)(2,1)S(1)} collective-permute-done((bf16[2,6,6,4,384]{4,3,2,1,0:T(4,128)(2,1)S(1)}, bf16[2,6,6,4,384]{4,3,2,1,0:T(4,128)(2,1)S(1)}, u32[]{:S(2)}, u32[]{:S(2)}) %collective-permute-start.4) | collective-permute-done | bytes 221216 | tf_op jit(solution)/shard_map/ppermute | solution.py:39
  37.4 7.0 %all-to-all-start = ((bf16[8,112,384]{2,1,0:T(8,128)(2,1)}), bf16[8,112,384]{2,1,0:T(8,128)(2,1)S(1)}, u32[]{:S(2)}, u32[]{:S(2)}) async-start(bf16[8,112,384]{2,1,0:T(8,128)(2,1)} %shard_map.132), calls=%async_computation | async-start | bytes 1376256 | tf_op jit(solution)/shard_map/all_to_all | solution.py:545
  44.4 0.3 pad_maximum_fusion
  44.7 8.7 %all-to-all-done.got_ref = bf16[8,112,384]{2,1,0:T(8,128)(2,1)S(1)} async-done(((bf16[8,112,384]{2,1,0:T(8,128)(2,1)}), bf16[8,112,384]{2,1,0:T(8,128)(2,1)S(1)}, u32[]{:S(2)}, u32[]{:S(2)}) %all-to-all-start) | async-done | bytes 688160 | tf_op jit(solution)/shard_map/all_to_all | solution.py:545
  53.4 0.8 %shard_map.133 = (bf16[16,8,384]{2,1,0:T(8,128)(2,1)}, f32[48,128]{1,0:T(8,128)S(1)}) custom-call(bf16[8,112,384]{2,1,0:T(8,128)(2,1)S(1)} %all-to-all-done.got_ref), custom_call_target="tpu_custom_call" | custom-call | flops 1000000 | bytes 1000000 | tf_op jit(solution)/shard_map/pallas_call | solution.py:546
  54.2 0.2 fusion.2
  54.4 0.1 collective-permute-start.5
  54.4 7.1 %all-to-all-start.1 = ((bf16[16,8,384]{2,1,0:T(8,128)(2,1)}), bf16[16,8,384]{2,1,0:T(8,128)(2,1)S(1)}, u32[]{:S(2)}, u32[]{:S(2)}) async-start(bf16[16,8,384]{2,1,0:T(8,128)(2,1)} %get-tuple-element.51), calls=%async_computation.1 | async-start | bytes 196608 | tf_op jit(solution)/shard_map/all_to_all | solution.py:560
  61.6 2.5 %collective-permute-done.5 = bf16[2,3,12,4,384]{4,3,2,1,0:T(4,128)(2,1)S(1)} collective-permute-done((bf16[2,3,12,4,384]{4,3,2,1,0:T(4,128)(2,1)S(1)}, bf16[2,3,12,4,384]{4,3,2,1,0:T(4,128)(2,1)S(1)}, u32[]{:S(2)}, u32[]{:S(2)}) %collective-permute-start.5) | collective-permute-done | bytes 221216 | tf_op jit(solution)/shard_map/ppermute | solution.py:39
  64.1 0.0 collective-permute-start.6
  64.1 0.3 maximum_bitcast_fusion
  64.4 0.9 %slice_bitcast_fusion = (bf16[4,6,12,384]{3,0,2,1:T(4,128)(2,1)}, bf16[4,6,12,384]{3,0,2,1:T(4,128)(2,1)}) fusion(bf16[2,4,6,12,384]{4,1,3,2,0:T(4,128)(2,1)S(1)} %maximum_bitcast_fusion), kind=kLoop, calls=%fused_computation.2 | loop fusion | bytes 884736 | tf_op jit(solution)/shard_map/squeeze | solution.py:571
  65.3 0.0 collective-permute-done.6.other_ref
  65.3 0.0 copy-done.2
  65.3 0.6 copy-done.10
  65.9 1.4 %shard_map.134 = f32[12,1,759]{2,1,0:T(1,128)} custom-call(s32[2]{0:T(128)} %copy-done.3, f32[48,128]{1,0:T(8,128)} %copy-done.2, f32[48,128]{1,0:T(8,128)} %copy-done.10), custom_call_target="tpu_custom_call" | custom-call | flops 100000 | bytes 100000 | tf_op jit(solution)/shard_map/pallas_call | solution.py:563
  67.4 5.1 %all-to-all-done.1 = bf16[16,8,384]{2,1,0:T(8,128)(2,1)S(1)} async-done(((bf16[16,8,384]{2,1,0:T(8,128)(2,1)}), bf16[16,8,384]{2,1,0:T(8,128)(2,1)S(1)}, u32[]{:S(2)}, u32[]{:S(2)}) %all-to-all-start.1) | async-done | bytes 98336 | tf_op jit(solution)/shard_map/all_to_all | solution.py:560
  72.5 0.0 copy-start.11
  72.5 0.6 slice.51
  73.0 0.0 copy-done.11
  (6 shorter events, 0.1 us)
Async XLA Ops:
  2.7 14.6 %collective-permute-start = (bf16[2,3,12,4,384]{4,3,2,1,0:T(4,128)(2,1)S(1)}, bf16[2,3,12,4,384]{4,3,2,1,0:T(4,128)(2,1)S(1)}, u32[]{:S(2)}, u32[]{:S(2)}) collective-permute-start(bf16[2,3,12,4,384]{4,3,2,1,0:T(4,128)(2,1)S(1)} %pad_maximum_fusion.1), channel_id=1, source_target_pairs={{0,240},{16,0},{32,16},{48,32},{64,48},{80,64},{96,80},{112,96},{1... | collective-permute-start | bytes 663560 | tf_op jit(solution)/shard_map/ppermute | solution.py:39
  10.3 11.3 %copy-start.3 = (s32[2]{0:T(128)}, s32[2]{0:T(128)S(1)}, u32[]{:S(2)}) copy-start(s32[2]{0:T(128)S(1)} %pad_add_fusion.place_ref) | copy-start | bytes 28
  10.3 0.9 %copy-start.6 = (s32[144,144]{1,0:T(8,128)S(1)}, s32[144,144]{1,0:T(8,128)}, u32[]{:S(2)}) copy-start(s32[144,144]{1,0:T(8,128)} %ids_ref.1) | copy-start | bytes 248836
  11.2 0.8 %copy-start.8 = (f32[1,12,759]{2,0,1:T(1,128)S(1)}, f32[1,12,759]{2,0,1:T(1,128)}, u32[]{:S(2)}) copy-start(f32[1,12,759]{2,0,1:T(1,128)} %param.16) | copy-start | bytes 109300
  11.9 5.2 %copy-start = (bf16[4,6,12,384]{3,0,2,1:T(4,128)(2,1)S(1)}, bf16[4,6,12,384]{3,0,2,1:T(4,128)(2,1)}, u32[]{:S(2)}) copy-start(bf16[4,6,12,384]{3,0,2,1:T(4,128)(2,1)} %param.9) | copy-start | bytes 663556
  11.9 5.2 %copy-start.1 = (bf16[4,6,12,384]{3,0,2,1:T(4,128)(2,1)S(1)}, bf16[4,6,12,384]{3,0,2,1:T(4,128)(2,1)}, u32[]{:S(2)}) copy-start(bf16[4,6,12,384]{3,0,2,1:T(4,128)(2,1)} %param.10) | copy-start | bytes 663556
  11.9 6.2 %copy-start.12 = (bf16[384]{0:T(512)(128)(2,1)S(1)}, bf16[384]{0:T(512)(128)(2,1)}, u32[]{:S(2)}) copy-start(bf16[384]{0:T(512)(128)(2,1)} %param.12) | copy-start | bytes 2308
  11.9 6.2 %copy-start.13 = (bf16[384]{0:T(512)(128)(2,1)S(1)}, bf16[384]{0:T(512)(128)(2,1)}, u32[]{:S(2)}) copy-start(bf16[384]{0:T(512)(128)(2,1)} %param.13) | copy-start | bytes 2308
  11.9 9.6 %copy-start.4 = (bf16[1152,384]{1,0:T(8,128)(2,1)S(1)}, bf16[1152,384]{1,0:T(8,128)(2,1)}, u32[]{:S(2)}) copy-start(bf16[1152,384]{1,0:T(8,128)(2,1)} %wqkv_in_ref.1) | copy-start | bytes 2654212
  12.0 9.6 %copy-start.5 = (bf16[384,384]{1,0:T(8,128)(2,1)S(1)}, bf16[384,384]{1,0:T(8,128)(2,1)}, u32[]{:S(2)}) copy-start(bf16[384,384]{1,0:T(8,128)(2,1)} %wout_ref.3) | copy-start | bytes 884740
  12.0 9.6 %copy-start.9 = (s32[2,1,1]{0,2,1:T(1,128)S(1)}, s32[2,1,1]{0,2,1:T(1,128)}, u32[]{:S(2)}) copy-start(s32[2,1,1]{0,2,1:T(1,128)} %param.11) | copy-start | bytes 28
  17.5 4.1 %collective-permute-start.1 = (bf16[2,6,6,4,384]{4,3,2,1,0:T(4,128)(2,1)S(1)}, bf16[2,6,6,4,384]{4,3,2,1,0:T(4,128)(2,1)S(1)}, u32[]{:S(2)}, u32[]{:S(2)}) collective-permute-start(bf16[2,6,6,4,384]{4,3,2,1,0:T(4,128)(2,1)S(1)} %pad_maximum_fusion.2), channel_id=1, source_target_pairs={{0,15},{1,0},{2,1},{3,2},{4,3},{5,4},{6,5},{7,6},{8,7},{9,8},{10,9... | collective-permute-start | bytes 663560 | tf_op jit(solution)/shard_map/ppermute | solution.py:39
  28.9 5.7 %collective-permute-start.2 = (bf16[8,104,384]{2,1,0:T(8,128)(2,1)S(1)}, bf16[8,104,384]{2,1,0:T(8,128)(2,1)S(1)}, u32[]{:S(2)}, u32[]{:S(2)}) collective-permute-start(bf16[8,104,384]{2,1,0:T(8,128)(2,1)S(1)} %get-tuple-element.38), channel_id=1, source_target_pairs={{0,1},{1,0},{2,3},{3,2},{4,5},{5,4},{6,7},{7,6},{8,9},{9,8},{10,11... | collective-permute-start | bytes 1916936 | tf_op jit(solution)/shard_map/ppermute | solution.py:503
  31.2 2.1 %collective-permute-start.3 = (bf16[6,176,128]{2,1,0:T(8,128)(2,1)S(1)}, bf16[6,176,128]{2,1,0:T(8,128)(2,1)S(1)}, u32[]{:S(2)}, u32[]{:S(2)}) collective-permute-start(bf16[6,176,128]{2,1,0:T(8,128)(2,1)S(1)} %get-tuple-element.45), channel_id=1, source_target_pairs={{0,1},{1,0},{2,3},{3,2},{4,5},{5,4},{6,7},{7,6},{8,9},{9,8},{10,11... | collective-permute-start | bytes 811016 | tf_op jit(solution)/shard_map/ppermute | solution.py:503
  31.3 2.0 %copy-start.7 = (s32[144,144]{1,0:T(8,128)S(1)}, s32[144,144]{1,0:T(8,128)}, u32[]{:S(2)}) copy-start(s32[144,144]{1,0:T(8,128)} %ids_ref.1) | copy-start | bytes 248836
  31.8 5.6 %collective-permute-start.4 = (bf16[2,6,6,4,384]{4,3,2,1,0:T(4,128)(2,1)S(1)}, bf16[2,6,6,4,384]{4,3,2,1,0:T(4,128)(2,1)S(1)}, u32[]{:S(2)}, u32[]{:S(2)}) collective-permute-start(bf16[2,6,6,4,384]{4,3,2,1,0:T(4,128)(2,1)S(1)} %get-tuple-element.46), channel_id=1, source_target_pairs={{0,1},{1,2},{2,3},{3,4},{4,5},{5,6},{6,7},{7,8},{8,9},{9,10},{10,1... | collective-permute-start | bytes 663560 | tf_op jit(solution)/shard_map/ppermute | solution.py:39
  37.4 16.0 %all-to-all-start = ((bf16[8,112,384]{2,1,0:T(8,128)(2,1)}), bf16[8,112,384]{2,1,0:T(8,128)(2,1)S(1)}, u32[]{:S(2)}, u32[]{:S(2)}) async-start(bf16[8,112,384]{2,1,0:T(8,128)(2,1)} %shard_map.132), calls=%async_computation | async-start | bytes 1376256 | tf_op jit(solution)/shard_map/all_to_all | solution.py:545
  54.2 11.2 %copy-start.2 = (f32[48,128]{1,0:T(8,128)}, f32[48,128]{1,0:T(8,128)S(1)}, u32[]{:S(2)}) copy-start(f32[48,128]{1,0:T(8,128)S(1)} %get-tuple-element.54.mine_ref) | copy-start | bytes 73732
  54.4 9.8 %collective-permute-start.5 = (bf16[2,3,12,4,384]{4,3,2,1,0:T(4,128)(2,1)S(1)}, bf16[2,3,12,4,384]{4,3,2,1,0:T(4,128)(2,1)S(1)}, u32[]{:S(2)}, u32[]{:S(2)}) collective-permute-start(bf16[2,3,12,4,384]{4,3,2,1,0:T(4,128)(2,1)S(1)} %get-tuple-element.61), channel_id=1, source_target_pairs={{0,16},{16,32},{32,48},{48,64},{64,80},{80,96},{96,112},{112,128},... | collective-permute-start | bytes 663560 | tf_op jit(solution)/shard_map/ppermute | solution.py:39
  54.4 18.0 %all-to-all-start.1 = ((bf16[16,8,384]{2,1,0:T(8,128)(2,1)}), bf16[16,8,384]{2,1,0:T(8,128)(2,1)S(1)}, u32[]{:S(2)}, u32[]{:S(2)}) async-start(bf16[16,8,384]{2,1,0:T(8,128)(2,1)} %get-tuple-element.51), calls=%async_computation.1 | async-start | bytes 196608 | tf_op jit(solution)/shard_map/all_to_all | solution.py:560
  64.1 1.2 %collective-permute-start.6 = (f32[48,128]{1,0:T(8,128)S(1)}, f32[48,128]{1,0:T(8,128)S(1)}, u32[]{:S(2)}, u32[]{:S(2)}) collective-permute-start(f32[48,128]{1,0:T(8,128)S(1)} %get-tuple-element.54.mine_ref), channel_id=1, source_target_pairs={{0,1},{1,0},{2,3},{3,2},{4,5},{5,4},{6,7},{7,6},{8,9},{9,8},{10,11... | collective-permute-start | bytes 73736 | tf_op jit(solution)/shard_map/ppermute | solution.py:503
  65.3 0.6 copy-start.10
  72.5 0.6 copy-start.11
